TPU v7x, 32 devices: a whole 2x2x4 slice. The times are simulated.
32 devices in a mesh: seq: 8 (over z, x), head: 4 (over y, core).
Axes of the slice: x: 2, y: 2, z: 4, core: 2. Of those that a mesh axis runs over, the one named last changes fastest.
Arguments:
- inputs: bfloat16 [4, 1024, 1024], P('head', 'seq'), may hold values from -6 to 6
- gain_attn: bfloat16 [1024], P(('seq', 'head')), may hold values from 0.099609375 to 1.8984375
- w_qkv: bfloat16 [1024, 3072], P(('seq', 'head')), may hold values from -0.1875 to 0.1875
- head_bias: float32 [16, 2], replicated, may hold values from -1 to 1
- w_out: bfloat16 [1024, 1024], P(('seq', 'head')), may hold values from -6 to 6
- gain_ffn: bfloat16 [1024], P(('seq', 'head')), may hold values from 0.099609375 to 1.8984375
- w_gate: bfloat16 [1024, 4096], P('seq', 'head'), may hold values from -0.1875 to 0.1875
- w_up: bfloat16 [1024, 4096], P('seq', 'head'), may hold values from -0.1875 to 0.1875
- w_down: bfloat16 [4096, 1024], P('head', 'seq'), may hold values from -0.09375 to 0.09375
- time_ids: int32 [4, 1024], replicated, may hold values from 0 to 511
- variate_ids: int32 [4, 1024], replicated, may hold values from 0 to 3
- seq_ids: int32 [4, 1024], replicated, may hold values from 0 to 11, as said below
- cotangent: bfloat16 [4, 1024, 1024], P('head', 'seq'), may hold values from -6 to 6
Outputs:
- output: bfloat16 [4, 1024, 1024], P('head', 'seq')
- grad_input: bfloat16 [4, 1024, 1024], P('head', 'seq')
- grad_gain_attn: float32 [1024], P(('seq', 'head'))
- grad_w_qkv: float32 [1024, 3072], P(('seq', 'head'))
- grad_head_bias: float32 [16, 2], replicated
- grad_w_out: float32 [1024, 1024], P(('seq', 'head'))
- grad_gain_ffn: float32 [1024], P(('seq', 'head'))
- grad_w_gate: float32 [1024, 4096], P('seq', 'head')
- grad_w_up: float32 [1024, 4096], P('seq', 'head')
- grad_w_down: float32 [4096, 1024], P('head', 'seq')
Inputs may be any that keep to these rules, and one draw needn't show every extreme that they name: `seq_ids`: ids never fall along a window's 1024 positions, and no two windows hold the same id.
All inputs are finite; a program needn't handle non-finite values.
Results may differ from a plain program's by a relative error of at most 0.024.
Values may be sent and summed in bfloat16 or wider, within the bound.
No kernel may reach another device: no remote copies, remote signals or barrier semaphores. Data moves between devices by JAX's collectives and lax.ppermute only.
A program may use at most 256 MiB of HBM per device.

v0:
```python
import math

import jax
import jax.numpy as jnp
from jax import lax
from jax.sharding import PartitionSpec as P

epsilon = 1e-05
masked_score = -1e30


def rope_tables(stamps, dimension):
    halfway = dimension // 2
    frequency = jnp.exp(-math.log(10000.0) * jnp.arange(halfway, dtype=jnp.float32) / halfway)
    angles = stamps.astype(jnp.float32)[:, None] * frequency[None, :]
    return (jnp.cos(angles), jnp.sin(angles))


def rotate(values, cosine, sine_table):
    halfway = values.shape[-1] // 2
    leading = values[..., :halfway]
    trailing = values[..., halfway:]
    cosine = cosine[:, None, :]
    sine_table = sine_table[:, None, :]
    return jnp.concatenate(
        [leading * cosine - trailing * sine_table, trailing * cosine + leading * sine_table],
        axis=-1,
    )


def unrotate(gradients, cosine, sine_table):
    halfway = gradients.shape[-1] // 2
    leading = gradients[..., :halfway]
    trailing = gradients[..., halfway:]
    cosine = cosine[:, None, :]
    sine_table = sine_table[:, None, :]
    return jnp.concatenate(
        [leading * cosine + trailing * sine_table, trailing * cosine - leading * sine_table],
        axis=-1,
    )


def normalize(values, scaling):
    inverse = lax.rsqrt(jnp.mean(values * values, axis=-1, keepdims=True) + epsilon)
    return (values * inverse * scaling, inverse)


def norm_backward(values, inverse, scaling, grad_normed):
    upstream = grad_normed * scaling
    grad_values = inverse * upstream - values * inverse**3 * jnp.mean(
        upstream * values, axis=-1, keepdims=True
    )
    grad_scaling = jnp.sum(grad_normed * values * inverse, axis=0)
    return (grad_values, grad_scaling)


def split_blocks(piece):
    row_count = piece.shape[0]
    block_rows = math.gcd(row_count, 512)
    block_count = row_count // block_rows
    return (piece.reshape((block_count, block_rows) + piece.shape[1:]), block_rows, block_count)


def score_block(
    query_rows,
    key_block,
    query_docs,
    query_kinds,
    seq_ids,
    variate_ids,
    offset,
    block_rows,
    local_bias,
):
    score_scale = query_rows.shape[-1] ** (-0.5)
    raw_scores = (
        jnp.einsum("tghd,rghd->ghtr", query_rows, key_block, preferred_element_type=jnp.float32)
        * score_scale
    )
    key_docs = lax.dynamic_slice_in_dim(seq_ids, offset, block_rows, 1)
    key_kinds = lax.dynamic_slice_in_dim(variate_ids, offset, block_rows, 1)
    same_var = (query_kinds[:, :, None] == key_kinds[:, None, :])[:, None]
    allowed = (query_docs[:, :, None] == key_docs[:, None, :])[:, None]
    bias_terms = jnp.where(
        same_var, local_bias[:, 0][None, :, None, None], local_bias[:, 1][None, :, None, None]
    )
    return (raw_scores + bias_terms, allowed, same_var)


def swiglu_forward(rows_low, gate_cols, up_cols, down_rows):
    gate_values = jnp.dot(rows_low, gate_cols, preferred_element_type=jnp.float32)
    up_values = jnp.dot(rows_low, up_cols, preferred_element_type=jnp.float32)
    sigmoid_gate = jax.nn.sigmoid(gate_values)
    activated = gate_values * sigmoid_gate
    hidden_low = (activated * up_values).astype(jnp.bfloat16)
    down_part = jnp.dot(hidden_low, down_rows, preferred_element_type=jnp.float32)
    return (gate_values, up_values, sigmoid_gate, activated, hidden_low, down_part)


def swiglu_backward(rows_low, grad_rows, gate_cols, up_cols, down_rows, saved):
    gate_values, up_values, sigmoid_gate, activated, hidden_low = saved
    grad_w_down = jnp.einsum("tf,td->fd", hidden_low, grad_rows, preferred_element_type=jnp.float32)
    grad_hidden = jnp.einsum("td,fd->tf", grad_rows, down_rows, preferred_element_type=jnp.float32)
    grad_gate = (
        grad_hidden * up_values * sigmoid_gate * (1.0 + gate_values * (1.0 - sigmoid_gate))
    ).astype(jnp.bfloat16)
    grad_up = (grad_hidden * activated).astype(jnp.bfloat16)
    grad_w_gate = jnp.einsum("td,tf->df", rows_low, grad_gate, preferred_element_type=jnp.float32)
    grad_w_up = jnp.einsum("td,tf->df", rows_low, grad_up, preferred_element_type=jnp.float32)
    two_part = jnp.einsum(
        "tf,df->td", grad_gate, gate_cols, preferred_element_type=jnp.float32
    ) + jnp.einsum("tf,df->td", grad_up, up_cols, preferred_element_type=jnp.float32)
    return (grad_w_gate, grad_w_up, grad_w_down, two_part)


def shards(
    inputs,
    gain_attn,
    w_qkv,
    head_bias,
    w_out,
    gain_ffn,
    w_gate,
    w_up,
    w_down,
    time_ids,
    variate_ids,
    seq_ids,
    cotangent,
):
    tokens = inputs[0].astype(jnp.float32)
    tok_rows = tokens.shape[0]
    model_width = tokens.shape[1]
    head_count = head_bias.shape[0]
    head_dim = model_width // head_count
    groups = lax.axis_size("head")
    local_heads = head_count // groups
    seq_index = lax.axis_index("seq")
    head_index = lax.axis_index("head")
    score_scale = head_dim ** (-0.5)
    gathered = (
        lax.all_gather(gain_attn, ("seq", "head"), axis=0, tiled=True),
        lax.all_gather(w_qkv, ("seq", "head"), axis=0, tiled=True),
        lax.all_gather(w_out, ("seq", "head"), axis=0, tiled=True),
        lax.all_gather(gain_ffn, ("seq", "head"), axis=0, tiled=True),
    )
    full_gain_attn, full_qkv, full_out, full_gain_ffn = gathered
    scaling_one = full_gain_attn.astype(jnp.float32)
    scaling_two = full_gain_ffn.astype(jnp.float32)
    my_stamps = lax.dynamic_slice(time_ids, (head_index, seq_index * tok_rows), (1, tok_rows))[0]
    cosine, sine_table = rope_tables(my_stamps, head_dim)
    normed, inverse_one = normalize(tokens, scaling_one)
    normed_low = normed.astype(jnp.bfloat16)
    packed = jnp.dot(normed_low, full_qkv, preferred_element_type=jnp.float32).reshape(
        tok_rows, head_count, 3, head_dim
    )
    qkv_low = jnp.concatenate(
        [
            rotate(packed[:, :, 0], cosine, sine_table),
            rotate(packed[:, :, 1], cosine, sine_table),
            packed[:, :, 2],
        ],
        axis=-1,
    ).astype(jnp.bfloat16)
    to_heads = lax.all_to_all(
        qkv_low.reshape(tok_rows, 1, head_count, 3 * head_dim),
        "head",
        split_axis=2,
        concat_axis=1,
        tiled=True,
    )
    query_rows = to_heads[..., :head_dim]
    key_values = to_heads[..., head_dim:]
    query_docs = lax.dynamic_slice_in_dim(seq_ids, seq_index * tok_rows, tok_rows, 1)
    query_kinds = lax.dynamic_slice_in_dim(variate_ids, seq_index * tok_rows, tok_rows, 1)
    local_bias = lax.dynamic_slice_in_dim(head_bias, head_index * local_heads, local_heads, 0)
    all_keys, gate_cols, up_cols, down_rows = (
        lax.all_gather(key_values, "seq", axis=0, tiled=True),
        lax.all_gather(w_gate, "seq", axis=0, tiled=True),
        lax.all_gather(w_up, "seq", axis=0, tiled=True),
        lax.all_gather(w_down, "seq", axis=1, tiled=True),
    )
    key_stack, block_rows, block_count = split_blocks(all_keys)
    offsets = block_rows * jnp.arange(block_count, dtype=jnp.int32)

    def step_block(running, element):
        maxima, totals, accumulated = running
        key_block, offset = element
        scores, allowed, same_var = score_block(
            query_rows,
            key_block[..., :head_dim],
            query_docs,
            query_kinds,
            seq_ids,
            variate_ids,
            offset,
            block_rows,
            local_bias,
        )
        scores = jnp.where(allowed, scores, masked_score)
        new_max = jnp.maximum(maxima, jnp.max(scores, axis=-1))
        factor = jnp.exp(maxima - new_max)
        block_weights = jnp.where(allowed, jnp.exp(scores - new_max[..., None]), 0.0)
        totals = totals * factor + jnp.sum(block_weights, axis=-1)
        update = jnp.einsum(
            "ghtr,rghd->tghd",
            block_weights.astype(jnp.bfloat16),
            key_block[..., head_dim:],
            preferred_element_type=jnp.float32,
        )
        accumulated = accumulated * jnp.transpose(factor, (2, 0, 1))[..., None] + update
        return ((new_max, totals, accumulated), None)

    start_state = (
        jnp.full((groups, local_heads, tok_rows), masked_score, jnp.float32),
        jnp.zeros((groups, local_heads, tok_rows), jnp.float32),
        jnp.zeros((tok_rows, groups, local_heads, head_dim), jnp.float32),
    )
    (maxima, totals, accumulated), unused = lax.scan(step_block, start_state, (key_stack, offsets))
    log_totals = maxima + jnp.log(totals)
    attended = (accumulated / jnp.transpose(totals, (2, 0, 1))[..., None]).astype(jnp.bfloat16)
    merged = lax.all_to_all(attended, "head", split_axis=1, concat_axis=2, tiled=True).reshape(
        tok_rows, model_width
    )
    middle = tokens + jnp.dot(merged, full_out, preferred_element_type=jnp.float32)
    normed_two, inverse_two = normalize(middle, scaling_two)
    normed_two_low = normed_two.astype(jnp.bfloat16)
    grad_out = cotangent[0]
    full_gate, full_up, full_down = (
        lax.all_gather(gate_cols, "head", axis=1, tiled=True),
        lax.all_gather(up_cols, "head", axis=1, tiled=True),
        lax.all_gather(down_rows, "head", axis=0, tiled=True),
    )
    forward_parts = swiglu_forward(normed_two_low, full_gate, full_up, full_down)
    grad_w_gate, grad_w_up, grad_w_down, grad_two = swiglu_backward(
        normed_two_low, grad_out, full_gate, full_up, full_down, forward_parts[:5]
    )
    down_sum = forward_parts[5]
    ffn_terms = (
        lax.psum_scatter(
            grad_w_gate.astype(jnp.bfloat16), "head", scatter_dimension=1, tiled=True
        ).astype(jnp.float32),
        lax.psum_scatter(
            grad_w_up.astype(jnp.bfloat16), "head", scatter_dimension=1, tiled=True
        ).astype(jnp.float32),
        lax.psum_scatter(
            grad_w_down.astype(jnp.bfloat16), "head", scatter_dimension=0, tiled=True
        ).astype(jnp.float32),
    )
    shard_gate, shard_up, shard_down = (
        lax.psum_scatter(
            ffn_terms[0].astype(jnp.bfloat16), "seq", scatter_dimension=0, tiled=True
        ).astype(jnp.float32),
        lax.psum_scatter(
            ffn_terms[1].astype(jnp.bfloat16), "seq", scatter_dimension=0, tiled=True
        ).astype(jnp.float32),
        lax.psum_scatter(
            ffn_terms[2].astype(jnp.bfloat16), "seq", scatter_dimension=1, tiled=True
        ).astype(jnp.float32),
    )
    output = middle + down_sum
    grad_from_norm, grad_gain_ffn = norm_backward(middle, inverse_two, scaling_two, grad_two)
    grad_middle = grad_out.astype(jnp.float32) + grad_from_norm
    grad_branch = grad_middle.astype(jnp.bfloat16)
    grad_w_out = jnp.einsum("te,td->ed", merged, grad_branch, preferred_element_type=jnp.float32)
    grad_merged = jnp.einsum(
        "td,ed->te", grad_branch, full_out, preferred_element_type=jnp.float32
    ).astype(jnp.bfloat16)
    grad_attended = lax.all_to_all(
        grad_merged.reshape(tok_rows, 1, head_count, head_dim),
        "head",
        split_axis=2,
        concat_axis=1,
        tiled=True,
    )
    row_dots = jnp.transpose(
        jnp.sum(grad_attended.astype(jnp.float32) * attended.astype(jnp.float32), axis=-1),
        (1, 2, 0),
    )

    def grad_block(running, element):
        grad_query, bias_grad = running
        key_block, offset = element
        scores, allowed, same_var = score_block(
            query_rows,
            key_block[..., :head_dim],
            query_docs,
            query_kinds,
            seq_ids,
            variate_ids,
            offset,
            block_rows,
            local_bias,
        )
        block_weights = jnp.where(allowed, jnp.exp(scores - log_totals[..., None]), 0.0)
        grad_weights = jnp.einsum(
            "tghd,rghd->ghtr",
            grad_attended,
            key_block[..., head_dim:],
            preferred_element_type=jnp.float32,
        )
        grad_scores = (block_weights * (grad_weights - row_dots[..., None])).astype(jnp.bfloat16)
        grad_query = grad_query + score_scale * jnp.einsum(
            "ghtr,rghd->tghd",
            grad_scores,
            key_block[..., :head_dim],
            preferred_element_type=jnp.float32,
        )
        grad_keys = score_scale * jnp.einsum(
            "ghtr,tghd->rghd", grad_scores, query_rows, preferred_element_type=jnp.float32
        )
        grad_values = jnp.einsum(
            "ghtr,tghd->rghd",
            block_weights.astype(jnp.bfloat16),
            grad_attended,
            preferred_element_type=jnp.float32,
        )
        score_wide = grad_scores.astype(jnp.float32)
        all_part = jnp.sum(score_wide, axis=(0, 2, 3))
        same_part = jnp.sum(jnp.where(same_var, score_wide, 0.0), axis=(0, 2, 3))
        bias_grad = bias_grad + jnp.stack([same_part, all_part - same_part], axis=-1)
        return ((grad_query, bias_grad), jnp.concatenate([grad_keys, grad_values], axis=-1))

    grad_start = (
        jnp.zeros((tok_rows, groups, local_heads, head_dim), jnp.float32),
        jnp.zeros((local_heads, 2), jnp.float32),
    )
    (grad_query, bias_grad), key_terms = lax.scan(grad_block, grad_start, (key_stack, offsets))
    key_terms = key_terms.reshape((block_count * block_rows,) + key_terms.shape[2:])
    key_grads = lax.psum_scatter(
        key_terms.astype(jnp.bfloat16), "seq", scatter_dimension=0, tiled=True
    ).astype(jnp.float32)
    grad_heads = jnp.concatenate([grad_query, key_grads], axis=-1).astype(jnp.bfloat16)
    returned = lax.all_to_all(grad_heads, "head", split_axis=1, concat_axis=2, tiled=True).reshape(
        tok_rows, head_count, 3 * head_dim
    )
    grad_rot_query = unrotate(returned[..., :head_dim].astype(jnp.float32), cosine, sine_table)
    grad_rot_key = unrotate(
        returned[..., head_dim : 2 * head_dim].astype(jnp.float32), cosine, sine_table
    )
    grad_packed = (
        jnp.concatenate(
            [grad_rot_query, grad_rot_key, returned[..., 2 * head_dim :].astype(jnp.float32)],
            axis=-1,
        )
        .astype(jnp.bfloat16)
        .reshape(tok_rows, 3 * model_width)
    )
    grad_w_qkv = jnp.einsum(
        "td,tc->dc", normed_low, grad_packed, preferred_element_type=jnp.float32
    )
    grad_one = jnp.einsum("tc,dc->td", grad_packed, full_qkv, preferred_element_type=jnp.float32)
    grad_from_first, grad_gain_attn = norm_backward(tokens, inverse_one, scaling_one, grad_one)
    grad_input = (
        (grad_middle + grad_from_first).astype(jnp.bfloat16).reshape(1, tok_rows, model_width)
    )
    full_bias = lax.dynamic_update_slice_in_dim(
        jnp.zeros((head_count, 2), jnp.float32), bias_grad, head_index * local_heads, 0
    )
    bias_total = lax.psum(full_bias, ("seq", "head"))
    shard_gain_attn, shard_qkv, shard_out, shard_gain_ffn = (
        lax.psum_scatter(grad_gain_attn, ("seq", "head"), scatter_dimension=0, tiled=True),
        lax.psum_scatter(grad_w_qkv, ("seq", "head"), scatter_dimension=0, tiled=True),
        lax.psum_scatter(grad_w_out, ("seq", "head"), scatter_dimension=0, tiled=True),
        lax.psum_scatter(grad_gain_ffn, ("seq", "head"), scatter_dimension=0, tiled=True),
    )
    output_low = output.astype(jnp.bfloat16).reshape(1, tok_rows, model_width)
    return (
        output_low,
        grad_input,
        shard_gain_attn,
        shard_qkv,
        bias_total,
        shard_out,
        shard_gain_ffn,
        shard_gate,
        shard_up,
        shard_down,
    )


def solution(mesh):
    placed = (
        P("head", "seq", None),
        P(("seq", "head")),
        P(("seq", "head"), None),
        P(),
        P(("seq", "head"), None),
        P(("seq", "head")),
        P("seq", "head"),
        P("seq", "head"),
        P("head", "seq"),
        P(),
        P(),
        P(),
        P("head", "seq", None),
    )
    return jax.shard_map(
        shards,
        mesh=mesh,
        in_specs=placed,
        out_specs=(
            P("head", "seq", None),
            P("head", "seq", None),
            P(("seq", "head")),
            P(("seq", "head"), None),
            P(),
            P(("seq", "head"), None),
            P(("seq", "head")),
            P("seq", "head"),
            P("seq", "head"),
            P("head", "seq"),
        ),
        check_vma=False,
    )
```

profile of v0, /device:TPU:0, one launch (start us, length us, event | category | flops | bytes accessed | tf_op | source)
XLA Modules:
  0.0 1394.8 jit_solution(11786009448599790015)
XLA Ops:
  11.7 42.5 %all-reduce.5 = (bf16[1024]{0:T(1024)(128)(2,1)S(1)}, bf16[1024]{0:T(1024)(128)(2,1)S(1)}) all-reduce(bf16[1024]{0:T(1024)(128)(2,1)S(1)} %dynamic-update-slice, bf16[1024]{0:T(1024)(128)(2,1)S(1)} %dynamic-update-slice.1), channel_id=1, replica_groups=mesh['seq'=8,'head'=4] {'seq','head'}, use_global_device_ids=true, to_apply=%add | all-reduce | flops 2048 | bytes 8192
  56.8 26.5 %all-gather.10.cloned.1.call-done = bf16[1024,3072]{1,0:T(8,128)(2,1)} async-done(((bf16[32,3072]{1,0:T(8,128)(2,1)}), bf16[1024,3072]{1,0:T(8,128)(2,1)}) %all-gather.10.cloned.1.call-update) | async-done | bytes 6291472 | tf_op jit(solution)/shard_map/all_gather | solution.py:143
  83.3 8.7 copy.67
  97.2 14.2 %all_to_all.42 = bf16[128,1,16,192]{0,3,1,2:T(8,128)(2,1)S(1)} all-to-all(bf16[128,1,16,192]{0,3,1,2:T(8,128)(2,1)S(1)} %bitcast.265), channel_id=1, replica_groups=mesh['seq'=8,'head'=4] {'head'}, dimensions={2} | all-to-all | bytes 1572864 | tf_op jit(solution)/shard_map/all_to_all | solution.py:165
  113.7 19.6 %all-gather.16.cloned.1.call-done = bf16[1024,1024]{1,0:T(8,128)(2,1)} async-done(((bf16[128,1024]{1,0:T(8,128)(2,1)}), bf16[1024,1024]{1,0:T(8,128)(2,1)}) %all-gather.16.cloned.1.call-update) | async-done | bytes 2097168 | tf_op jit(solution)/shard_map/all_gather | solution.py:179
  133.3 49.9 %all-gather.20.cloned.1.call-done = bf16[1024,1024]{1,0:T(8,128)(2,1)} async-done(((bf16[128,1024]{1,0:T(8,128)(2,1)}), bf16[1024,1024]{1,0:T(8,128)(2,1)}) %all-gather.20.cloned.1.call-update) | async-done | bytes 2097168 | tf_op jit(solution)/shard_map/all_gather | solution.py:180
  183.3 51.4 %all-gather.24.cloned.1.call-done = bf16[1024,1024]{1,0:T(8,128)(2,1)} async-done(((bf16[1024,128]{1,0:T(8,128)(2,1)}), bf16[1024,1024]{1,0:T(8,128)(2,1)}) %all-gather.24.cloned.1.call-update) | async-done | bytes 2097168 | tf_op jit(solution)/shard_map/all_gather | solution.py:181
  235.2 73.7 %all-gather.12.cloned.1.call-done = bf16[1024,4,4,128]{3,0,2,1:T(8,128)(2,1)} async-done(((bf16[128,4,4,128]{3,0,2,1:T(8,128)(2,1)}), bf16[1024,4,4,128]{3,0,2,1:T(8,128)(2,1)}) %all-gather.12.cloned.1.call-update) | async-done | bytes 4194320 | tf_op jit(solution)/shard_map/all_gather | solution.py:178
  316.2 28.7 %while.30 = (s32[]{:T(128)}, f32[4,4,128]{2,1,0:T(4,128)S(1)}, f32[4,4,128]{2,1,0:T(4,128)S(1)}, f32[128,4,4,64]{0,3,2,1:T(8,128)S(1)}, s32[4,128]{1,0:T(4,128)S...) while((s32[]{:T(128)}, f32[4,4,128]{2,1,0:T(4,128)S(1)}, ...), condition=%wide.region_4.5_spmd.clone, body=%wide.region_1.4_spmd.clone.sunk | while | flops 289288192 | bytes 39246156 | solution.py:219
  349.5 17.3 %all-gather.14.cloned.1.call-done = bf16[1024,1024]{1,0:T(8,128)(2,1)} async-done(((bf16[32,1024]{1,0:T(8,128)(2,1)}), bf16[1024,1024]{1,0:T(8,128)(2,1)}) %all-gather.14.cloned.1.call-update) | async-done | bytes 2097168 | tf_op jit(solution)/shard_map/all_gather | solution.py:144
  369.1 56.0 %all-gather.18.cloned.1.call-done = bf16[1024,4096]{1,0:T(8,128)(2,1)} async-done(((bf16[1024,1024]{1,0:T(8,128)(2,1)}), bf16[1024,4096]{1,0:T(8,128)(2,1)}) %all-gather.18.cloned.1.call-update) | async-done | bytes 8388624 | tf_op jit(solution)/shard_map/all_gather | solution.py:230
  431.1 53.9 %all-gather.22.cloned.1.call-done = bf16[1024,4096]{1,0:T(8,128)(2,1)} async-done(((bf16[1024,1024]{1,0:T(8,128)(2,1)}), bf16[1024,4096]{1,0:T(8,128)(2,1)}) %all-gather.22.cloned.1.call-update) | async-done | bytes 8388624 | tf_op jit(solution)/shard_map/all_gather | solution.py:231
  491.0 53.9 %all-gather.26.cloned.1.call-done = bf16[4096,1024]{1,0:T(8,128)(2,1)} async-done(((bf16[1024,1024]{1,0:T(8,128)(2,1)}), bf16[4096,1024]{1,0:T(8,128)(2,1)}) %all-gather.26.cloned.1.call-update) | async-done | bytes 8388624 | tf_op jit(solution)/shard_map/all_gather | solution.py:232
  594.1 9.0 all-to-all-done.2
  604.1 52.8 %while.31 = (s32[]{:T(128)}, f32[128,4,4,64]{0,3,2,1:T(8,128)S(1)}, f32[4,2]{0,1:T(2,128)S(1)}, bf16[2,512,4,4,128]{4,1,0,3,2:T(8,128)(2,1)}, bf16[2,512,4,4,128...) while((s32[]{:T(128)}, f32[128,4,4,64]{0,3,2,1:T(8,128)S(1)}, ...), condition=%wide.region_11.12_spmd.clone, body=%wide.region_8.11_spmd.clone.sunk | while | flops 696123392 | bytes 53032980 | solution.py:328
  661.1 47.6 %reduce-scatter.18.cloned.1.call-done = bf16[1024,1024]{1,0:T(8,128)(2,1)} async-done(((bf16[1024,4096]{1,0:T(8,128)(2,1)}), bf16[1024,1024]{1,0:T(8,128)(2,1)}) %reduce-scatter.18.cloned.1.call-update) | async-done | bytes 2097168 | tf_op jit(solution)/shard_map/reduce_scatter | solution.py:240
  708.8 74.1 %reduce-scatter.22.cloned.1.call-done = bf16[1024,1024]{1,0:T(8,128)(2,1)} async-done(((bf16[1024,4096]{1,0:T(8,128)(2,1)}), bf16[1024,1024]{1,0:T(8,128)(2,1)}) %reduce-scatter.22.cloned.1.call-update) | async-done | bytes 2097168 | tf_op jit(solution)/shard_map/reduce_scatter | solution.py:243
  786.1 89.1 %reduce-scatter.12.cloned.1.call-done = bf16[128,4,4,128]{3,0,2,1:T(8,128)(2,1)} async-done(((bf16[1024,4,4,128]{3,0,2,1:T(8,128)(2,1)}), bf16[128,4,4,128]{3,0,2,1:T(8,128)(2,1)}) %reduce-scatter.12.cloned.1.call-update) | async-done | bytes 524304 | tf_op jit(solution)/shard_map/reduce_scatter | solution.py:330
  877.5 14.4 %all_to_all.43 = bf16[128,4,4,192]{0,3,2,1:T(8,128)(2,1)S(1)} all-to-all(bf16[128,4,4,192]{0,3,2,1:T(8,128)(2,1)S(1)} %copy.80), channel_id=1, replica_groups=mesh['seq'=8,'head'=4] {'head'}, dimensions={1} | all-to-all | bytes 1572864 | tf_op jit(solution)/shard_map/all_to_all | solution.py:334
  911.8 39.8 %all-reduce.4 = (f32[1024]{0:T(1024)S(1)}, f32[16,2]{0,1:T(2,128)}, f32[1024]{0:T(1024)S(1)}) all-reduce(f32[1024]{0:T(1024)S(1)} %get-tuple-element.331, f32[16,2]{0,1:T(2,128)S(1)} %dynamic_update_slice.7, f32[1024]{0:T(1024)S(1)} %get-tuple-element.329), channel_id=3, replica_groups=mesh['seq'=8,'head'=4] {'seq','head'}, use_global_device_ids=true, to_apply=%region_15.16.clone | all-reduce | flops 2080 | bytes 16640
  955.6 60.9 %reduce-scatter.20.cloned.1.call-done = bf16[128,1024]{1,0:T(8,128)(2,1)} async-done(((bf16[1024,1024]{1,0:T(8,128)(2,1)}), bf16[128,1024]{1,0:T(8,128)(2,1)}) %reduce-scatter.20.cloned.1.call-update) | async-done | bytes 262160 | tf_op jit(solution)/shard_map/reduce_scatter | solution.py:251
  1018.4 68.2 %reduce-scatter.24.cloned.1.call-done = bf16[128,1024]{1,0:T(8,128)(2,1)} async-done(((bf16[1024,1024]{1,0:T(8,128)(2,1)}), bf16[128,1024]{1,0:T(8,128)(2,1)}) %reduce-scatter.24.cloned.1.call-update) | async-done | bytes 262160 | tf_op jit(solution)/shard_map/reduce_scatter | solution.py:254
  1088.4 141.2 %reduce-scatter.16.cloned.1.call-done = f32[32,1024]{1,0:T(8,128)} async-done(((f32[1024,1024]{1,0:T(8,128)}), f32[32,1024]{1,0:T(8,128)}) %reduce-scatter.16.cloned.1.call-update) | async-done | bytes 131088 | tf_op jit(solution)/shard_map/reduce_scatter | solution.py:364
  1229.6 158.2 %reduce-scatter.14.cloned.1.call-done = f32[32,3072]{1,0:T(8,128)} async-done(((f32[1024,3072]{1,0:T(8,128)}), f32[32,3072]{1,0:T(8,128)}) %reduce-scatter.14.cloned.1.call-update) | async-done | bytes 393232 | tf_op jit(solution)/shard_map/reduce_scatter | solution.py:363
  (236 shorter events, 201.5 us)
Async XLA Ops:
  7.2 227.6 %copy-start = (f32[16,2]{0,1:T(2,128)S(1)}, f32[16,2]{0,1:T(2,128)}, u32[]{:S(2)}) copy-start(f32[16,2]{0,1:T(2,128)} %param.20) | copy-start | bytes 388
  7.2 76.1 %all-gather.10.cloned.1.call-start = ((), (), s32[]{:S(2)}) async-start(), calls=%async_computation.13 | async-start | bytes 6488064 | tf_op jit(solution)/shard_map/all_gather | solution.py:143
  7.9 125.3 %all-gather.16.cloned.1.call-start = ((), (), s32[]{:S(2)}) async-start(), calls=%async_computation.16 | async-start | bytes 2359296 | tf_op jit(solution)/shard_map/all_gather | solution.py:179
  8.7 174.6 %all-gather.20.cloned.1.call-start = ((), (), s32[]{:S(2)}) async-start(), calls=%async_computation.18 | async-start | bytes 2359296 | tf_op jit(solution)/shard_map/all_gather | solution.py:180
  9.4 225.3 %all-gather.24.cloned.1.call-start = ((), (), s32[]{:S(2)}) async-start(), calls=%async_computation.20 | async-start | bytes 2359296 | tf_op jit(solution)/shard_map/all_gather | solution.py:181
  10.0 298.9 %all-gather.12.cloned.1.call-start = ((), (), s32[]{:S(2)}) async-start(), calls=%async_computation.14 | async-start | bytes 4718592 | tf_op jit(solution)/shard_map/all_gather | solution.py:178
  112.0 122.9 %copy-start.23 = (s32[4,1024]{1,0:T(4,128)S(1)}, s32[4,1024]{1,0:T(4,128)}, u32[]{:S(2)}) copy-start(s32[4,1024]{1,0:T(4,128)} %param.27) | copy-start | bytes 49156
  112.0 122.9 %copy-start.24 = (s32[4,1024]{1,0:T(4,128)S(1)}, s32[4,1024]{1,0:T(4,128)}, u32[]{:S(2)}) copy-start(s32[4,1024]{1,0:T(4,128)} %param.28) | copy-start | bytes 49156
  113.1 253.7 %all-gather.14.cloned.1.call-start = ((), (), s32[]{:S(2)}) async-start(), calls=%async_computation.15 | async-start | bytes 2162688 | tf_op jit(solution)/shard_map/all_gather | solution.py:144
  113.6 311.4 %all-gather.18.cloned.1.call-start = ((), (), s32[]{:S(2)}) async-start(), calls=%async_computation.17 | async-start | bytes 10485760 | tf_op jit(solution)/shard_map/all_gather | solution.py:230
  133.3 351.7 %all-gather.22.cloned.1.call-start = ((), (), s32[]{:S(2)}) async-start(), calls=%async_computation.19 | async-start | bytes 10485760 | tf_op jit(solution)/shard_map/all_gather | solution.py:231
  183.3 361.6 %all-gather.26.cloned.1.call-start = ((), (), s32[]{:S(2)}) async-start(), calls=%async_computation.21 | async-start | bytes 10485760 | tf_op jit(solution)/shard_map/all_gather | solution.py:232
  345.8 20.9 %all-to-all-start.1 = ((bf16[128,4,4,64]{0,3,2,1:T(8,128)(2,1)}), bf16[128,4,4,64]{0,3,2,1:T(8,128)(2,1)S(1)}, u32[]{:S(2)}, u32[]{:S(2)}) async-start(bf16[128,4,4,64]{0,3,2,1:T(8,128)(2,1)} %divide_convert_fusion), calls=%async_computation.1 | async-start | bytes 524288 | tf_op jit(solution)/shard_map/all_to_all | solution.py:222
  349.2 307.9 %reduce-scatter.26.cloned.1.call-start = ((), (), s32[]{:S(2)}) async-start(), calls=%async_computation.29 | async-start | bytes 10485760 | tf_op jit(solution)/shard_map/reduce_scatter | solution.py:246
  559.5 149.2 %reduce-scatter.18.cloned.1.call-start = ((), (), s32[]{:S(2)}) async-start(), calls=%async_computation.25 | async-start | bytes 10485760 | tf_op jit(solution)/shard_map/reduce_scatter | solution.py:240
  565.4 217.5 %reduce-scatter.22.cloned.1.call-start = ((), (), s32[]{:S(2)}) async-start(), calls=%async_computation.27 | async-start | bytes 10485760 | tf_op jit(solution)/shard_map/reduce_scatter | solution.py:243
  589.8 13.3 all-to-all-start.2
  593.8 281.4 %reduce-scatter.12.cloned.1.call-start = ((), (), s32[]{:S(2)}) async-start(), calls=%async_computation.22 | async-start | bytes 4718592 | tf_op jit(solution)/shard_map/reduce_scatter | solution.py:330
  657.0 296.7 %reduce-scatter.28.cloned.1.call-start = ((), (), s32[]{:S(2)}) async-start(), calls=%async_computation.30 | async-start | bytes 2359296
  661.0 355.5 %reduce-scatter.20.cloned.1.call-start = ((), (), s32[]{:S(2)}) async-start(), calls=%async_computation.26 | async-start | bytes 2359296 | tf_op jit(solution)/shard_map/reduce_scatter | solution.py:251
  708.7 377.9 %reduce-scatter.24.cloned.1.call-start = ((), (), s32[]{:S(2)}) async-start(), calls=%async_computation.28 | async-start | bytes 2359296 | tf_op jit(solution)/shard_map/reduce_scatter | solution.py:254
  782.9 446.6 %reduce-scatter.16.cloned.1.call-start = ((), (), s32[]{:S(2)}) async-start(), calls=%async_computation.24 | async-start | bytes 4325376 | tf_op jit(solution)/shard_map/reduce_scatter | solution.py:364
  785.7 602.0 %reduce-scatter.14.cloned.1.call-start = ((), (), s32[]{:S(2)}) async-start(), calls=%async_computation.23 | async-start | bytes 12976128 | tf_op jit(solution)/shard_map/reduce_scatter | solution.py:363
  906.6 481.2 %copy-start.1 = (f32[16,2]{0,1:T(2,128)S(1)}, f32[16,2]{0,1:T(2,128)}, u32[]{:S(2)}) copy-start(f32[16,2]{0,1:T(2,128)} %param.20) | copy-start | bytes 388
  (28 other events, 903.7 us)
Sparse Core Ops, SparseCore 0:
  10.9 72.3 all-gather.9
  85.5 47.7 all-gather.15
  135.4 47.7 all-gather.19
  185.1 49.5 all-gather.23
  237.3 71.5 all-gather.11
  311.6 55.0 all-gather.13
  368.3 56.7 all-gather.17
  426.6 58.2 all-gather.21
  486.5 58.2 all-gather.25
  559.6 74.5 reduce-scatter.25
  636.9 71.7 reduce-scatter.17
  711.1 71.7 reduce-scatter.21
  787.0 88.2 reduce-scatter.11
  878.7 67.7 reduce-scatter.27
  949.8 66.7 reduce-scatter.19
  1020.0 66.5 reduce-scatter.23
  1089.3 140.2 reduce-scatter.15
  1236.0 151.6 reduce-scatter.13
where the time goes:
time: 1400 us; the launch traced here: 1390 us
  waiting for transfers between devices  1050 us (75%)
  matrix products  117 us (8%)
  blocking collectives  111 us (8%)
  local copies, waits for them, and re-layouts  60.1 us (4%)
  other arithmetic  21.2 us (2%)
  between operations  15.1 us (1%)
    reduce_scatter x1, waiting for transfers between devices, shards(): lax.psum_scatter(grad_w_qkv, ('seq', 'head'), scatter_dimension=0, tiled=...  158 us
    reduce_scatter x1, waiting for transfers between devices, shards(): lax.psum_scatter(grad_w_out, ('seq', 'head'), scatter_dimension=0, tiled=...  141 us
    reduce_scatter x1, waiting for transfers between devices, shards(): lax.psum_scatter(key_terms.astype(jnp.bfloat16), 'seq', scatter_dimension...  89.1 us
    unnamed x2, blocking collectives  82.4 us
    reduce_scatter x1, waiting for transfers between devices, shards(): lax.psum_scatter(grad_w_up.astype(jnp.bfloat16), 'head', scatter_dimensio...  74.1 us
    all_gather x1, waiting for transfers between devices, shards(): lax.all_gather(key_values, 'seq', axis=0, tiled=True)  73.7 us
    reduce_scatter x1, waiting for transfers between devices, shards(): lax.psum_scatter(ffn_terms[1].astype(jnp.bfloat16), 'seq', scatter_dimens...  68.2 us
    reduce_scatter x1, waiting for transfers between devices, shards(): lax.psum_scatter(ffn_terms[0].astype(jnp.bfloat16), 'seq', scatter_dimens...  60.9 us
  transfers between devices with their start and end apart: 20, of which 17 were waited for; matrix products, arithmetic and copies ran while one was open for 13% of the time, Pallas kernels for 0%

commit v1 on v0

v1 whole, which is shorter than its diff:
```python
import functools
import math

import jax
import jax.numpy as jnp
from jax import lax
from jax.experimental import pallas as pl
from jax.experimental.pallas import tpu as pltpu
from jax.sharding import PartitionSpec as P


epsilon = 1e-05
masked_score = -1e30
low = jnp.bfloat16
wide = jnp.float32
lanes = 128
half_lanes = 64


def dot(a, b):
    return jnp.dot(a, b, preferred_element_type=wide)


def dot_t(a, b):
    return lax.dot_general(a, b, (((1,), (1,)), ((), ())), preferred_element_type=wide)


def t_dot(a, b):
    return lax.dot_general(a, b, (((0,), (0,)), ((), ())), preferred_element_type=wide)


class Place:
    def __init__(self):
        self.seq_size = lax.axis_size("seq")
        self.head_size = lax.axis_size("head")
        self.z_size = self.seq_size // 2
        self.y_size = self.head_size // 2
        self.seq = lax.axis_index("seq")
        self.head = lax.axis_index("head")
        self.z, self.x = self.seq // 2, self.seq % 2
        self.y, self.c = self.head // 2, self.head % 2

    def along_z(self, value, step):
        return lax.ppermute(value, "seq", [(i, i ^ (2 * step)) for i in range(self.seq_size)])

    def along_x(self, value):
        return lax.ppermute(value, "seq", [(i, i ^ 1) for i in range(self.seq_size)])

    def along_c(self, value):
        return lax.ppermute(value, "head", [(i, i ^ 1) for i in range(self.head_size)])

    def along_xy(self, value, dx, dy):
        if dy == 0:
            return self.along_x(value)
        if dx == 0:
            return lax.ppermute(
                value, "head", [(i, i ^ (2 * dy)) for i in range(self.head_size)]
            )
        return lax.ppermute(
            value,
            ("seq", "head"),
            [
                (s * self.head_size + h, (s ^ dx) * self.head_size + (h ^ (2 * dy)))
                for s in range(self.seq_size)
                for h in range(self.head_size)
            ],
        )

    def turn(self, value):
        return lax.ppermute(
            value,
            ("seq", "head"),
            [
                (s * self.head_size + h, ((s & ~1) | (h & 1)) * self.head_size + ((h & ~1) | (s & 1)))
                for s in range(self.seq_size)
                for h in range(self.head_size)
            ],
        )

    def pairs(self):
        return [(dx, dy) for dy in range(self.y_size) for dx in range(2)]

    def gather_xy(self, value):
        return [value if d == (0, 0) else self.along_xy(value, *d) for d in self.pairs()]

    def scatter_xy(self, blocks):
        return [
            block if d == (0, 0) else self.along_xy(block, *d)
            for d, block in zip(self.pairs(), blocks)
        ]

    def gather_z(self, value):
        return [value if d == 0 else self.along_z(value, d) for d in range(self.z_size)]

    def scatter_z(self, blocks):
        return [block if d == 0 else self.along_z(block, d) for d, block in enumerate(blocks)]


def pick(bit, zero, one):
    return jnp.where(bit == 0, zero, one)


def xor_list(blocks, me):
    step = 1
    while step < len(blocks):
        on = (me // step) % 2
        blocks = [pick(on, blocks[i], blocks[i ^ step]) for i in range(len(blocks))]
        step *= 2
    return blocks


def reorder_kernel(me_ref, in_ref, out_ref):
    count = in_ref.shape[0]
    me = me_ref[0]

    @pl.loop(0, count)
    def _(i):
        out_ref[i] = in_ref[jnp.bitwise_xor(i, me)]


def reorder(blocks, me):
    return pl.pallas_call(
        reorder_kernel,
        out_shape=jax.ShapeDtypeStruct(blocks.shape, blocks.dtype),
        in_specs=[pl.BlockSpec(memory_space=pltpu.SMEM), pl.BlockSpec(memory_space=pltpu.VMEM)],
        out_specs=pl.BlockSpec(memory_space=pltpu.VMEM),
        compiler_params=pltpu.CompilerParams(vmem_limit_bytes=32 * 2**20),
        cost_estimate=pl.CostEstimate(flops=0, bytes_accessed=2 * blocks.size * 2, transcendentals=0),
    )(me.reshape(1).astype(jnp.int32), blocks)


def lane_ids(rows):
    return lax.broadcasted_iota(jnp.int32, (rows, lanes), 1)


def swap_halves(value):
    first = lane_ids(value.shape[0]) % half_lanes < half_lanes // 2
    return jnp.where(first, pltpu.roll(value, lanes - 32, 1), pltpu.roll(value, 32, 1))


def three_pieces(value):
    one = value.astype(low).astype(wide)
    rest = value - one
    two = rest.astype(low).astype(wide)
    return one, two, (rest - two).astype(low).astype(wide)


def attend_kernel(
    heads,
    bias_ref,
    near_ref,
    far_ref,
    w_ref,
    cosine_ref,
    sine_ref,
    kinds_ref,
    docs_col_ref,
    docs_row_ref,
    query_ref,
    key_ref,
    value_ref,
    out_ref,
):
    rows = near_ref.shape[0]
    length = 2 * rows
    step = min(rows, 256)
    padded = w_ref.shape[1] // 3
    for part, source in enumerate((near_ref, far_ref)):
        for start in range(0, rows, step):
            at = pl.ds(part * rows + start, step)
            packed = dot(source[start : start + step, :], w_ref[...])
            cosine, sine = cosine_ref[at, :], sine_ref[at, :]
            lane = lane_ids(step)
            kind = kinds_ref[at, :]
            own = (lane == 64 + kind).astype(wide)
            own_two = (lane == 68 + kind).astype(wide)
            extra_query = ((lane == 72 + kind) | (lane == 76)).astype(wide)
            extra_key = own + own_two + ((lane >= 77) & (lane < 80)).astype(wide)
            extra_value = ((lane >= 64) & (lane < 67)).astype(wide)
            for head in range(heads):
                base = head // 2 * lanes
                query = packed[:, base : base + lanes]
                key = packed[:, padded + base : padded + base + lanes]
                value = packed[:, 2 * padded + base : 2 * padded + base + lanes]
                query = (query * cosine + swap_halves(query) * sine).astype(low).astype(wide) * 0.125
                key = key * cosine + swap_halves(key) * sine
                if head % 2:
                    query, key, value = (pltpu.roll(v, half_lanes, 1) for v in (query, key, value))
                body = lane < half_lanes
                extra = extra_query + own * bias_ref[0, head] + own_two * bias_ref[1, head]
                query_ref[head, at, :] = jnp.where(body, query, extra).astype(low)
                key_ref[head, at, :] = jnp.where(body, key, extra_key).astype(low)
                value_ref[head, at, :] = jnp.where(body, value, extra_value).astype(low)
    block = min(length, 256)
    lane = lane_ids(block)

    @pl.loop(0, length // block)
    def _(i):
        at = pl.ds(pl.multiple_of(i * block, block), block)
        allowed = docs_col_ref[at, :] == docs_row_ref[...]
        done = []
        for head in range(heads):
            query = query_ref[head, at, :]
            scores = jnp.where(allowed, dot_t(query, key_ref[head]), masked_score)
            top = jnp.max(scores, axis=1, keepdims=True)
            weights = jnp.exp(scores - top).astype(low)
            summed = dot(weights, value_ref[head])
            total = summed[:, half_lanes : half_lanes + 1]
            one, two, three = three_pieces(-(top + jnp.log(total)))
            extra = jnp.where(lane == 77, one, jnp.where(lane == 78, two, jnp.where(lane == 79, three, 0.0)))
            query_ref[head, at, :] = jnp.where(lane < 77, query.astype(wide), extra).astype(low)
            done.append(summed / total)
        for base in range(0, heads, 2):
            both = done[base]
            if base + 1 < heads:
                both = jnp.where(lane < half_lanes, both, pltpu.roll(done[base + 1], half_lanes, 1))
            out_ref[at, base // 2 * lanes : (base // 2 + 1) * lanes] = both.astype(low)


def attend(bias, near, far, w, cosine, sine, kinds, docs, heads):
    length = 2 * near.shape[0]
    padded = w.shape[1] // 3
    vmem = pl.BlockSpec(memory_space=pltpu.VMEM)
    whole = jax.ShapeDtypeStruct((heads, length, lanes), low)
    flops = 2 * length * near.shape[1] * w.shape[1] + 4 * heads * length * length * lanes
    return pl.pallas_call(
        functools.partial(attend_kernel, heads),
        out_shape=(whole, whole, whole, jax.ShapeDtypeStruct((length, padded), low)),
        in_specs=[pl.BlockSpec(memory_space=pltpu.SMEM)] + [vmem] * 8,
        out_specs=(vmem, vmem, vmem, vmem),
        compiler_params=pltpu.CompilerParams(vmem_limit_bytes=48 * 2**20),
        cost_estimate=pl.CostEstimate(
            flops=flops, bytes_accessed=8 * 2**20, transcendentals=heads * length * length
        ),
    )(bias, near, far, w, cosine, sine, kinds, docs.reshape(length, 1), docs.reshape(1, length))


def attend_grad_kernel(
    heads,
    query_ref,
    key_ref,
    value_ref,
    out_ref,
    grad_out_ref,
    cosine_ref,
    sine_ref,
    kinds_ref,
    docs_col_ref,
    docs_row_ref,
    packed_ref,
    bias_ref,
    grad_query_ref,
    grad_key_ref,
    grad_value_ref,
):
    length = query_ref.shape[1]
    padded = packed_ref.shape[1] // 3
    block = min(length, 256)
    lane = lane_ids(block)
    grad_key_ref[...] = jnp.zeros_like(grad_key_ref)
    grad_value_ref[...] = jnp.zeros_like(grad_value_ref)

    @pl.loop(0, length // block)
    def _(i):
        at = pl.ds(pl.multiple_of(i * block, block), block)
        allowed = docs_col_ref[...] == docs_row_ref[:, at]
        for head in range(heads):
            columns = slice(head // 2 * lanes, (head // 2 + 1) * lanes)
            grad_out = grad_out_ref[at, columns].astype(wide)
            product = grad_out * out_ref[at, columns].astype(wide)
            mine = (lane >= half_lanes) if head % 2 else (lane < half_lanes)
            row_dot = jnp.sum(jnp.where(mine, product, 0.0), axis=1, keepdims=True)
            one, two, three = three_pieces(-row_dot)
            if head % 2:
                grad_out = pltpu.roll(grad_out, half_lanes, 1)
            extra = jnp.where(lane == 64, one, jnp.where(lane == 65, two, jnp.where(lane == 66, three, 0.0)))
            grad_out = jnp.where(lane < half_lanes, grad_out, extra).astype(low)
            query, key = query_ref[head, at, :], key_ref[head]
            weights = jnp.exp(jnp.where(allowed, dot_t(key, query), masked_score))
            grad_scores = (weights * dot_t(value_ref[head], grad_out)).astype(low)
            grad_value_ref[head] += dot(weights.astype(low), grad_out)
            grad_key_ref[head] += dot(grad_scores, query)
            grad_query_ref[head, at, :] = t_dot(grad_scores, key)

    for start in range(0, length, block):
        at = slice(start, start + block)
        cosine, sine = cosine_ref[at, :], sine_ref[at, :]
        for base in range(0, heads, 2):

            def joined(ref):
                both = ref[base, at, :]
                if base + 1 < heads:
                    both = jnp.where(lane < half_lanes, both, pltpu.roll(ref[base + 1, at, :], half_lanes, 1))
                else:
                    both = jnp.where(lane < half_lanes, both, 0.0)
                return both

            columns = base // 2 * lanes
            query = joined(grad_query_ref) * 0.125
            key = joined(grad_key_ref)
            value = joined(grad_value_ref)
            query = query * cosine - swap_halves(query) * sine
            key = key * cosine - swap_halves(key) * sine
            for part, result in enumerate((query, key, value)):
                packed_ref[at, part * padded + columns : part * padded + columns + lanes] = result.astype(low)
    every = lane_ids(length)
    kinds = kinds_ref[...]
    for head in range(heads):
        grads = grad_key_ref[head]
        same = jnp.sum(jnp.where(every == 72 + kinds, grads, 0.0))
        total = jnp.sum(jnp.where(every == 76, grads, 0.0))
        bias_ref[head, 0] = same
        bias_ref[head, 1] = total - same


def attend_grad(query, key, value, out, grad_out, cosine, sine, kinds, docs, padded):
    heads, length, _ = query.shape
    vmem = pl.BlockSpec(memory_space=pltpu.VMEM)
    scratch = pltpu.VMEM((heads, length, lanes), wide)
    return pl.pallas_call(
        functools.partial(attend_grad_kernel, heads),
        out_shape=(
            jax.ShapeDtypeStruct((length, 3 * padded), low),
            jax.ShapeDtypeStruct((heads, 2), wide),
        ),
        in_specs=[vmem] * 10,
        out_specs=(vmem, pl.BlockSpec(memory_space=pltpu.SMEM)),
        scratch_shapes=[scratch] * 3,
        compiler_params=pltpu.CompilerParams(vmem_limit_bytes=48 * 2**20),
        cost_estimate=pl.CostEstimate(
            flops=10 * heads * length * length * lanes,
            bytes_accessed=8 * 2**20,
            transcendentals=heads * length * length,
        ),
    )(query, key, value, out, grad_out, cosine, sine, kinds, docs.reshape(length, 1), docs.reshape(1, length))


def rope_tables(stamps, dimension):
    halfway = dimension // 2
    frequency = jnp.exp(-math.log(10000.0) * jnp.arange(halfway, dtype=wide) / halfway)
    repeated = jnp.tile(frequency, lanes // halfway)
    angles = stamps.astype(wide)[:, None] * repeated[None, :]
    sign = jnp.where(jnp.arange(lanes) % dimension < halfway, -1.0, 1.0)
    return (jnp.cos(angles), jnp.sin(angles) * sign[None, :])


def shards(
    inputs,
    gain_attn,
    w_qkv,
    head_bias,
    w_out,
    gain_ffn,
    w_gate,
    w_up,
    w_down,
    time_ids,
    variate_ids,
    seq_ids,
    cotangent,
):
    at = Place()
    z_size, y_size = at.z_size, at.y_size
    tokens = inputs[0].astype(wide)
    rows, width = tokens.shape
    head_count = head_bias.shape[0]
    head_dim = width // head_count
    groups = at.seq_size
    heads = head_count // groups
    padded = (heads + 1) // 2 * lanes
    share = width // (at.seq_size * at.head_size)
    group = 2 * at.z + at.c
    window = 2 * at.y + at.x

    inverse_one = lax.rsqrt(jnp.mean(tokens * tokens, axis=-1, keepdims=True) + epsilon)
    unit = tokens * inverse_one
    near = jnp.concatenate(at.gather_z(at.turn(unit.astype(low))), axis=0)
    far = at.along_c(near)

    gain_one = gain_attn.astype(wide)[:, None]
    scaled = (w_qkv.astype(wide) * gain_one).astype(low)

    def to_parts(columns):
        parts = columns.reshape(-1, groups, heads, 3, head_dim).transpose(0, 1, 3, 2, 4)
        parts = parts.reshape(-1, groups, 3, heads * head_dim)
        parts = jnp.pad(parts, ((0, 0), (0, 0), (0, 0), (0, padded - heads * head_dim)))
        return parts.reshape(-1, groups, 3 * padded)

    parts = to_parts(scaled).reshape(share, z_size, 2, 3 * padded)
    core_own = pick(at.c, parts[:, :, 0], parts[:, :, 1])
    core_other = at.along_c(pick(at.c, parts[:, :, 1], parts[:, :, 0]))
    both = jnp.stack([core_own, core_other])
    sent = [
        lax.dynamic_index_in_dim(both, jnp.bitwise_xor(at.z, d), axis=2, keepdims=False)
        for d in range(z_size)
    ]
    by_z = jnp.stack(at.scatter_z(sent))
    by_xy = jnp.stack(at.gather_xy(by_z.reshape(2 * z_size * share, 3 * padded)))
    blocks = by_xy.reshape(y_size, 2, z_size, 2, share, 3 * padded).transpose(2, 1, 0, 3, 4, 5)
    device_id = at.seq * at.head_size + at.head
    w_heads = reorder(blocks.reshape(-1, share, 3 * padded), device_id).reshape(width, 3 * padded)

    def of_window(ids):
        row = lax.dynamic_index_in_dim(ids, window, axis=0, keepdims=False).reshape(z_size, 2, rows)
        order = [
            lax.dynamic_slice(
                row, (jnp.bitwise_xor(at.z, d), jnp.bitwise_xor(at.c, e), 0), (1, 1, rows)
            ).reshape(rows)
            for e in range(2)
            for d in range(z_size)
        ]
        return jnp.concatenate(order)

    docs = of_window(seq_ids)
    kinds = of_window(variate_ids)[:, None]
    cosine, sine = rope_tables(of_window(time_ids), head_dim)
    local_bias = lax.dynamic_slice_in_dim(head_bias, group * heads, heads, 0)
    difference = local_bias[:, 0] - local_bias[:, 1]
    difference_high = difference.astype(low).astype(wide)
    bias = jnp.stack([difference_high, difference - difference_high])

    depth, units = w_gate.shape[0], w_gate.shape[1] // 2
    stacked = jnp.concatenate([w_gate, w_up, w_down.T], axis=1).reshape(depth, 3, 2, units)
    mine = pick(at.x, stacked[:, :, 0], stacked[:, :, 1]).reshape(depth, 3 * units)
    other = at.along_x(pick(at.x, stacked[:, :, 1], stacked[:, :, 0]).reshape(depth, 3 * units))
    z_block = jnp.concatenate([pick(at.x, mine, other), pick(at.x, other, mine)], axis=0)
    w_ffn = jnp.concatenate(at.gather_z(z_block), axis=0)
    w_gate_up, w_down_t = w_ffn[:, : 2 * units], w_ffn[:, 2 * units :]

    z_columns = width // z_size

    def turn_columns(value):
        pieces = [value[:, i * z_columns : (i + 1) * z_columns] for i in range(z_size)]
        return jnp.concatenate(xor_list(pieces, at.z), axis=1)

    def gather_tokens(value):
        near_rows = jnp.concatenate(at.gather_xy(value), axis=0)
        return jnp.concatenate([near_rows, at.along_c(near_rows)], axis=0)

    grad_out = cotangent[0]
    grad_out_all = gather_tokens(turn_columns(grad_out))

    out_and_gain = jnp.concatenate(
        [w_out, jnp.pad(gain_ffn[:, None], ((0, 0), (0, lanes - 1)))], axis=1
    )
    gathered = lax.all_gather(out_and_gain, ("seq", "head"), axis=0, tiled=True)
    gain_two = gathered[:, width].astype(wide)
    out_rows = reorder(gathered[:, :width].reshape(groups, -1, width), at.seq)
    out_rows = out_rows.reshape(z_size, 2, -1, width).transpose(1, 0, 2, 3).reshape(width, width)

    query, key, value, attended = attend(bias, near, far, w_heads, cosine, sine, kinds, docs, heads)

    group_width = heads * head_dim
    sent = attended[:, :group_width].reshape(2, z_size, rows, group_width)
    received = at.scatter_z([sent[:, d] for d in range(z_size)])
    kept = jnp.concatenate([block[0] for block in received], axis=1)
    passed = at.along_c(jnp.concatenate([block[1] for block in received], axis=1))
    merged = at.turn(jnp.concatenate([kept, passed], axis=1))

    middle = tokens + dot(merged, out_rows)
    inverse_two = lax.rsqrt(jnp.mean(middle * middle, axis=-1, keepdims=True) + epsilon)
    normed_two = (middle * inverse_two * gain_two).astype(low)
    normed_two_all = gather_tokens(turn_columns(normed_two))

    gate_up = dot(normed_two_all, w_gate_up)
    gate_values, up_values = gate_up[:, :units], gate_up[:, units:]
    sigmoid_gate = jax.nn.sigmoid(gate_values)
    activated = gate_values * sigmoid_gate
    hidden = (activated * up_values).astype(low)
    grad_hidden = dot(grad_out_all, w_down_t)
    grad_gate = (
        grad_hidden * up_values * sigmoid_gate * (1.0 + gate_values * (1.0 - sigmoid_gate))
    ).astype(low)
    grad_up = (grad_hidden * activated).astype(low)
    grad_gate_up = jnp.concatenate([grad_gate, grad_up], axis=1)

    def scatter_tokens(part):
        cut = part.shape[0] // 2
        kept = part[:cut] + at.along_c(part[cut:].astype(low)).astype(wide)
        received = at.scatter_xy([kept[:rows]] + [
            kept[i * rows : (i + 1) * rows].astype(low) for i in range(1, 2 * y_size)
        ])
        return turn_columns(functools.reduce(jnp.add, [block.astype(wide) for block in received]))

    upstream = scatter_tokens(dot_t(grad_gate_up, w_gate_up)) * gain_two
    grad_middle = (
        grad_out.astype(wide)
        + inverse_two * upstream
        - middle * inverse_two**3 * jnp.mean(upstream * middle, axis=-1, keepdims=True)
    )
    grad_branch = grad_middle.astype(low)
    grad_merged = dot_t(grad_branch, out_rows).astype(low)

    turned = at.turn(grad_merged)
    cut = width // 2
    kept, passed = turned[:, :cut], at.along_c(turned[:, cut:])
    sent = [
        jnp.stack([part[:, d * group_width : (d + 1) * group_width] for part in (kept, passed)])
        for d in range(z_size)
    ]
    received = jnp.stack(at.scatter_z(sent), axis=1)
    grad_attended = received.reshape(2 * z_size * rows, group_width)
    if padded > group_width:
        grad_attended = jnp.pad(grad_attended, ((0, 0), (0, padded - group_width)))
    grad_packed, bias_grad = attend_grad(
        query, key, value, attended, grad_attended, cosine, sine, kinds, docs, padded
    )

    half = near.shape[0]
    upstream_far = dot_t(grad_packed[half:], w_heads).astype(low)
    upstream_near = dot_t(grad_packed[:half], w_heads) + at.along_c(upstream_far).astype(wide)
    received = at.scatter_z([upstream_near[:rows]] + [
        upstream_near[i * rows : (i + 1) * rows].astype(low) for i in range(1, z_size)
    ])
    upstream_one = functools.reduce(jnp.add, [block.astype(wide) for block in received])
    upstream_one = at.turn(upstream_one.astype(low)).astype(wide)
    grad_input = grad_middle + inverse_one * (
        upstream_one - unit * jnp.mean(upstream_one * unit, axis=-1, keepdims=True)
    )

    grad_heads = t_dot(near, grad_packed[:half]) + t_dot(far, grad_packed[half:])
    grad_heads = grad_heads.astype(low).reshape(z_size, 2, y_size, 2, share, 3 * padded)

    def rows_of(dx, dy):
        picked = lax.dynamic_slice(
            grad_heads,
            (0, jnp.bitwise_xor(at.x, dx), jnp.bitwise_xor(at.y, dy), 0, 0, 0),
            (z_size, 1, 1, 2, share, 3 * padded),
        )
        return picked.reshape(z_size, 2, share, 3 * padded)

    received = at.scatter_xy([rows_of(*d) for d in at.pairs()])
    summed = functools.reduce(jnp.add, [block.astype(wide) for block in received]).astype(low)
    sent = [
        lax.dynamic_index_in_dim(summed, jnp.bitwise_xor(at.z, d), axis=0, keepdims=False)
        for d in range(z_size)
    ]
    received = jnp.stack(at.scatter_z(sent))
    core_own = pick(at.c, received[:, 0], received[:, 1])
    core_other = at.along_c(pick(at.c, received[:, 1], received[:, 0]))
    by_group = jnp.stack([core_own, core_other], axis=1).reshape(groups, share, 3 * padded)
    by_group = reorder(by_group, group).astype(wide).reshape(groups, share, 3, padded)
    by_group = by_group[..., :group_width].reshape(groups, share, 3, heads, head_dim)
    raw = by_group.transpose(1, 0, 3, 2, 4).reshape(share, 3 * width)
    grad_w_qkv = raw * gain_one
    grad_gain_attn = jnp.sum(raw * w_qkv.astype(wide), axis=1)

    full_bias = lax.dynamic_update_slice_in_dim(
        jnp.zeros((head_count, 2), wide), bias_grad, group * heads, 0
    )
    full_bias = full_bias + at.along_c(full_bias)
    for d in range(int(math.log2(z_size))):
        full_bias = full_bias + at.along_z(full_bias, 1 << d)
    full_bias = full_bias + at.along_x(full_bias)
    for d in range(int(math.log2(y_size))):
        full_bias = full_bias + at.along_xy(full_bias, 0, 1 << d)

    grad_out_rows = t_dot(merged, grad_branch).astype(low)
    grad_out_rows = grad_out_rows.reshape(2, z_size, -1, width).transpose(1, 0, 2, 3)
    grad_out_rows = reorder(grad_out_rows.reshape(groups, -1, width), at.seq).reshape(width, width)
    grad_w_out = lax.psum_scatter(
        grad_out_rows, ("seq", "head"), scatter_dimension=0, tiled=True
    ).astype(wide)

    sent = []
    for d in range(z_size):
        columns = slice(d * z_columns, (d + 1) * z_columns)
        sent.append(
            jnp.concatenate(
                [
                    t_dot(normed_two_all[:, columns], grad_gate_up),
                    t_dot(grad_out_all[:, columns], hidden),
                ],
                axis=1,
            )
        )
    received = at.scatter_z(sent[:1] + [block.astype(low) for block in sent[1:]])
    summed = functools.reduce(jnp.add, [block.astype(wide) for block in received])
    mine = pick(at.x, summed[:depth], summed[depth:])
    other = at.along_x(pick(at.x, summed[depth:], summed[:depth]).astype(low)).astype(wide)
    first, second = pick(at.x, mine, other), pick(at.x, other, mine)
    grad_w_gate, grad_w_up, grad_w_down_t = (
        jnp.concatenate([first[:, i * units : (i + 1) * units], second[:, i * units : (i + 1) * units]], axis=1)
        for i in range(3)
    )
    gain_part = jnp.sum(grad_w_gate * w_gate.astype(wide) + grad_w_up * w_up.astype(wide), axis=1)
    gain_part = gain_part + at.along_c(gain_part)
    for d in range(int(math.log2(y_size))):
        gain_part = gain_part + at.along_xy(gain_part, 0, 1 << d)
    grad_gain_ffn = lax.dynamic_slice_in_dim(gain_part, at.head * share, share, 0) / gain_ffn.astype(wide)

    output = middle + scatter_tokens(dot_t(hidden, w_down_t))

    return (
        output.astype(low).reshape(1, rows, width),
        grad_input.astype(low).reshape(1, rows, width),
        grad_gain_attn,
        grad_w_qkv,
        full_bias,
        grad_w_out,
        grad_gain_ffn,
        grad_w_gate,
        grad_w_up,
        grad_w_down_t.T,
    )


def solution(mesh):
    placed = (
        P("head", "seq", None),
        P(("seq", "head")),
        P(("seq", "head"), None),
        P(),
        P(("seq", "head"), None),
        P(("seq", "head")),
        P("seq", "head"),
        P("seq", "head"),
        P("head", "seq"),
        P(),
        P(),
        P(),
        P("head", "seq", None),
    )
    return jax.shard_map(
        shards,
        mesh=mesh,
        in_specs=placed,
        out_specs=(
            P("head", "seq", None),
            P("head", "seq", None),
            P(("seq", "head")),
            P(("seq", "head"), None),
            P(),
            P(("seq", "head"), None),
            P(("seq", "head")),
            P("seq", "head"),
            P("seq", "head"),
            P("head", "seq"),
        ),
        check_vma=False,
    )
```

time: 1400 us -> 461 us (0.33)
  waiting for transfers between devices: 1050 us -> 222 us
  blocking collectives: 111 us -> 0 us
  starting transfers between devices: 8.96 us -> 114 us
  matrix products: 117 us -> 23.8 us
  local copies, waits for them, and re-layouts: 60.1 us -> 27.2 us
  Pallas kernels: 0 us -> 19.6 us
    reduce_scatter x8 -> x1, waiting for transfers between devices: 639 us -> 56 us  [shards(): lax.psum_scatter(grad_out_rows, ('seq', 'head'), scatter_dimension=0, til...]
    all_gather x9 -> x1, waiting for transfers between devices: 402 us -> 0.01 us  [shards(): gathered = lax.all_gather(out_and_gain, ('seq', 'head'), axis=0, tiled=True)]
    ppermute x0 -> x65, waiting for transfers between devices: none -> 166 us  [the longest x26 134 us: along_z(): lax.ppermute(value, 'seq', [(i, i ^ 2 * step) for i in range(self.seq_siz...]
    ppermute x0 -> x65, starting transfers between devices: none -> 114 us  [the longest x26 72.2 us: along_z(): lax.ppermute(value, 'seq', [(i, i ^ 2 * step) for i in range(self.seq_siz...]
    dot_general x29 -> x19, matrix products: 117 us -> 23.8 us  [the longest x11 9.41 us: t_dot(): lax.dot_general(a, b, (((0,), (0,)), ((), ())), preferred_element_type=wide)]
    unnamed x2 -> x0, blocking collectives: 82.4 us -> none
    all_to_all x2 -> x0, blocking collectives: 28.6 us -> none  [the longest x1 14.4 us: shards(): lax.all_to_all(grad_heads, 'head', split_axis=1, concat_axis=2, tiled=True)]
    pallas_call x0 -> x6, Pallas kernels: none -> 19.6 us  [the longest x1 8.83 us: attend_grad(): pl.pallas_call(functools.partial(attend_grad_kernel, heads), out_shape=(j...]
  transfers between devices with their start and end apart: 20 -> 67, of which waited for: 17 -> 27; matrix products, arithmetic and copies ran while one was open for 13% -> 13% of each run, Pallas kernels for 0% -> 4%
where the time goes in v1:
time: 461 us; the launch traced here: 452 us
  waiting for transfers between devices  222 us (48%)
  starting transfers between devices  114 us (25%)
  other arithmetic  29.2 us (6%)
  local copies, waits for them, and re-layouts  27.2 us (6%)
  matrix products  23.8 us (5%)
  Pallas kernels  19.6 us (4%)
  between operations  16.1 us (3%)
    ppermute x26, waiting for transfers between devices, along_z(): lax.ppermute(value, 'seq', [(i, i ^ 2 * step) for i in range(self.seq_siz...  134 us
    ppermute x26, starting transfers between devices, along_z(): lax.ppermute(value, 'seq', [(i, i ^ 2 * step) for i in range(self.seq_siz...  72.2 us
    reduce_scatter x1, waiting for transfers between devices, shards(): lax.psum_scatter(grad_out_rows, ('seq', 'head'), scatter_dimension=0, til...  56 us
    ppermute x8, waiting for transfers between devices, along_xy(): lax.ppermute(value, 'head', [(i, i ^ 2 * dy) for i in range(self.head_siz...  20.9 us
    unnamed x122, local copies, waits for them, and re-layouts  14.2 us
    ppermute x9, starting transfers between devices, along_x(): lax.ppermute(value, 'seq', [(i, i ^ 1) for i in range(self.seq_size)])  11.8 us
    ppermute x8, starting transfers between devices, along_xy(): lax.ppermute(value, 'head', [(i, i ^ 2 * dy) for i in range(self.head_siz...  11.8 us
    dot_general x11, matrix products, t_dot(): lax.dot_general(a, b, (((0,), (0,)), ((), ())), preferred_element_type=wide)  9.41 us
  transfers between devices with their start and end apart: 67, of which 27 were waited for; matrix products, arithmetic and copies ran while one was open for 13% of the time, Pallas kernels for 4%

profile of v1, /device:TPU:0, one launch (start us, length us, event | category | flops | bytes accessed | tf_op | source)
XLA Modules:
  0.0 451.5 jit_solution(16508015665888069869)
XLA Ops:
  14.6 3.7 collective-permute-start.21
  28.6 7.7 %collective-permute-done.1 = bf16[128,1024]{1,0:T(8,128)(2,1)S(1)} collective-permute-done((bf16[128,1024]{1,0:T(8,128)(2,1)S(1)}, bf16[128,1024]{1,0:T(8,128)(2,1)S(1)}, u32[]{:S(2)}, u32[]{:S(2)}) %collective-permute-start.1) | collective-permute-done | bytes 262176 | tf_op jit(solution)/shard_map/ppermute | solution.py:44
  38.2 10.5 %collective-permute-done.2 = bf16[128,1024]{1,0:T(8,128)(2,1)S(1)} collective-permute-done((bf16[128,1024]{1,0:T(8,128)(2,1)S(1)}, bf16[128,1024]{1,0:T(8,128)(2,1)S(1)}, u32[]{:S(2)}, u32[]{:S(2)}) %collective-permute-start.2) | collective-permute-done | bytes 262176 | tf_op jit(solution)/shard_map/ppermute | solution.py:44
  53.6 3.1 collective-permute-done.7
  65.9 5.1 %collective-permute-done.10 = bf16[256,384]{1,0:T(8,128)(2,1)S(1)} collective-permute-done((bf16[256,384]{1,0:T(8,128)(2,1)S(1)}, bf16[256,384]{1,0:T(8,128)(2,1)S(1)}, u32[]{:S(2)}, u32[]{:S(2)}) %collective-permute-start.10) | collective-permute-done | bytes 196640 | tf_op jit(solution)/shard_map/ppermute | solution.py:56
  75.9 8.5 %shard_map.205 = (bf16[2,1024,128]{2,1,0:T(8,128)(2,1)S(1)}, bf16[2,1024,128]{2,1,0:T(8,128)(2,1)S(1)}, bf16[2,1024,128]{2,1,0:T(8,128)(2,1)S(1)}, bf16[1024,128]{1,0:T(8,128)(2,1)S(1)}) custom-call(f32[2,2]{1,0:T(2,128)S(1)} %pad_maximum_fusion.21.bias_ref, bf16[512,1024]{1,0:T(8,128)(2,1)S(1)} %constant_dynamic-update-slice_fusion.near_ref, ...), custom_call_target="tpu_custom_call" | custom-call | flops 1879048192 | bytes 8388608 | tf_op jit(solution)/shard_map/pallas_call | solution.py:226
  92.0 2.9 collective-permute-done.12
  97.5 3.6 collective-permute-start.16
  118.1 3.4 collective-permute-done.17
  122.4 3.4 collective-permute-done.18
  129.2 9.3 %collective-permute-done.22 = bf16[256,1536]{1,0:T(8,128)(2,1)} collective-permute-done((bf16[256,1536]{1,0:T(8,128)(2,1)}, bf16[256,1536]{1,0:T(8,128)(2,1)}, u32[]{:S(2)}, u32[]{:S(2)}) %collective-permute-start.22) | collective-permute-done | bytes 786464 | tf_op jit(solution)/shard_map/ppermute | solution.py:44
  139.7 23.0 %collective-permute-done.23 = bf16[256,1536]{1,0:T(8,128)(2,1)S(1)} collective-permute-done((bf16[256,1536]{1,0:T(8,128)(2,1)}, bf16[256,1536]{1,0:T(8,128)(2,1)S(1)}, u32[]{:S(2)}, u32[]{:S(2)}) %collective-permute-start.23) | collective-permute-done | bytes 786464 | tf_op jit(solution)/shard_map/ppermute | solution.py:44
  174.1 17.2 %collective-permute-start.59 = (bf16[256,1536]{1,0:T(8,128)(2,1)S(1)}, bf16[256,1536]{1,0:T(8,128)(2,1)S(1)}, u32[]{:S(2)}, u32[]{:S(2)}) collective-permute-start(bf16[256,1536]{1,0:T(8,128)(2,1)S(1)} %pad_maximum_fusion.6), channel_id=1, source_target_pairs={{0,8},{4,12},{8,0},{12,4},{16,24},{20,28},{24,16},{28,20},{1,9},{5... | collective-permute-start | bytes 2359304 | tf_op jit(solution)/shard_map/ppermute | solution.py:44
  197.4 26.8 %collective-permute-done.59 = bf16[256,1536]{1,0:T(8,128)(2,1)S(1)} collective-permute-done((bf16[256,1536]{1,0:T(8,128)(2,1)S(1)}, bf16[256,1536]{1,0:T(8,128)(2,1)S(1)}, u32[]{:S(2)}, u32[]{:S(2)}) %collective-permute-start.59) | collective-permute-done | bytes 786464 | tf_op jit(solution)/shard_map/ppermute | solution.py:44
  224.2 22.2 %collective-permute-done.60 = bf16[256,1536]{1,0:T(8,128)(2,1)S(1)} collective-permute-done((bf16[256,1536]{1,0:T(8,128)(2,1)S(1)}, bf16[256,1536]{1,0:T(8,128)(2,1)S(1)}, u32[]{:S(2)}, u32[]{:S(2)}) %collective-permute-start.60) | collective-permute-done | bytes 786464 | tf_op jit(solution)/shard_map/ppermute | solution.py:44
  255.9 3.0 collective-permute-done.62
  271.6 10.1 %collective-permute-done.35 = bf16[128,1024]{1,0:T(8,128)(2,1)S(1)} collective-permute-done((bf16[128,1024]{1,0:T(8,128)(2,1)}, bf16[128,1024]{1,0:T(8,128)(2,1)S(1)}, u32[]{:S(2)}, u32[]{:S(2)}) %collective-permute-start.35) | collective-permute-done | bytes 262176 | tf_op jit(solution)/shard_map/ppermute | solution.py:56
  293.5 16.7 %collective-permute-start.39 = (bf16[2,128,128]{2,1,0:T(8,128)(2,1)S(1)}, bf16[2,128,128]{2,1,0:T(8,128)(2,1)S(1)}, u32[]{:S(2)}, u32[]{:S(2)}) collective-permute-start(bf16[2,128,128]{2,1,0:T(8,128)(2,1)S(1)} %pad_maximum_fusion.18), channel_id=1, source_target_pairs={{0,8},{4,12},{8,0},{12,4},{16,24},{20,28},{24,16},{28,20},{1,9},{5... | collective-permute-start | bytes 196616 | tf_op jit(solution)/shard_map/ppermute | solution.py:44
  312.7 5.8 %collective-permute-done.40 = bf16[2,128,128]{2,1,0:T(8,128)(2,1)S(1)} collective-permute-done((bf16[2,128,128]{2,1,0:T(8,128)(2,1)S(1)}, bf16[2,128,128]{2,1,0:T(8,128)(2,1)S(1)}, u32[]{:S(2)}, u32[]{:S(2)}) %collective-permute-start.40) | collective-permute-done | bytes 65568 | tf_op jit(solution)/shard_map/ppermute | solution.py:44
  320.8 8.8 %shard_map.207 = (bf16[1024,384]{1,0:T(8,128)(2,1)S(1)}, f32[2,2]{1,0:T(2,128)S(1)}) custom-call(bf16[2,1024,128]{2,1,0:T(8,128)(2,1)S(1)} %copy-done.9, bf16[2,1024,128]{2,1,0:T(8,128)(2,1)S(1)} %copy-done.11, bf16[2,1024,128]{2,1,0:T(8,128)(2,1)S(1)} %copy-done.13, bf16[1024,128]{1,0:T(8,128)(2,1)S(1)} %get-tuple-element.16.out_ref, ...), custom_call_target="tpu_custom_call" | custom-call | flops 2684354560 | bytes 8388608 | tf_op jit(solution)/shard_map/pallas_call | solution.py:320
  341.8 2.9 collective-permute-done.56
  364.4 8.2 %collective-permute-done.43 = bf16[128,1024]{1,0:T(8,128)(2,1)S(1)} collective-permute-done((bf16[128,1024]{1,0:T(8,128)(2,1)S(1)}, bf16[128,1024]{1,0:T(8,128)(2,1)S(1)}, u32[]{:S(2)}, u32[]{:S(2)}) %collective-permute-start.43) | collective-permute-done | bytes 262176 | tf_op jit(solution)/shard_map/ppermute | solution.py:44
  372.6 9.0 %collective-permute-done.44 = bf16[128,1024]{1,0:T(8,128)(2,1)S(1)} collective-permute-done((bf16[128,1024]{1,0:T(8,128)(2,1)S(1)}, bf16[128,1024]{1,0:T(8,128)(2,1)S(1)}, u32[]{:S(2)}, u32[]{:S(2)}) %collective-permute-start.44) | collective-permute-done | bytes 262176 | tf_op jit(solution)/shard_map/ppermute | solution.py:44
  386.7 56.0 %reduce-scatter.2.cloned.1.call-done = bf16[32,1024]{1,0:T(8,128)(2,1)} async-done(((bf16[1024,1024]{1,0:T(8,128)(2,1)}), bf16[32,1024]{1,0:T(8,128)(2,1)}) %reduce-scatter.2.cloned.1.call-update) | async-done | bytes 65552 | tf_op jit(solution)/shard_map/reduce_scatter | solution.py:561
  (385 shorter events, 164.4 us)
Async XLA Ops:
  7.2 97.9 %all-gather.2.cloned.1.call-start = ((), (), s32[]{:S(2)}) async-start(), calls=%async_computation.1 | async-start | bytes 2433024 | tf_op jit(solution)/shard_map/all_gather | solution.py:446
  13.1 429.6 %reduce-scatter.2.cloned.1.call-start = ((), (), s32[]{:S(2)}) async-start(), calls=%async_computation.2 | async-start | bytes 2162688 | tf_op jit(solution)/shard_map/reduce_scatter | solution.py:561
  14.6 59.8 %collective-permute-start.21 = (bf16[128,1536]{1,0:T(8,128)(2,1)}, bf16[128,1536]{1,0:T(8,128)(2,1)}, u32[]{:S(2)}, u32[]{:S(2)}) collective-permute-start(bf16[128,1536]{1,0:T(8,128)(2,1)} %copy.89), channel_id=1, source_target_pairs={{0,4},{4,0},{8,12},{12,8},{16,20},{20,16},{24,28},{28,24},{1,5},{5... | collective-permute-start | bytes 1179656 | tf_op jit(solution)/shard_map/ppermute | solution.py:47
  24.1 24.6 %collective-permute-start.2 = (bf16[128,1024]{1,0:T(8,128)(2,1)S(1)}, bf16[128,1024]{1,0:T(8,128)(2,1)S(1)}, u32[]{:S(2)}, u32[]{:S(2)}) collective-permute-start(bf16[128,1024]{1,0:T(8,128)(2,1)S(1)} %collective-permute-done), channel_id=1, source_target_pairs={{0,16},{4,20},{8,24},{12,28},{16,0},{20,4},{24,8},{28,12},{1,17},{... | collective-permute-start | bytes 786440 | tf_op jit(solution)/shard_map/ppermute | solution.py:44
  26.8 26.8 %collective-permute-start.6 = (bf16[2,32,384]{2,1,0:T(8,128)(2,1)S(1)}, bf16[2,32,384]{2,1,0:T(8,128)(2,1)S(1)}, u32[]{:S(2)}, u32[]{:S(2)}) collective-permute-start(bf16[2,32,384]{2,1,0:T(8,128)(2,1)S(1)} %get-tuple-element.127), channel_id=1, source_target_pairs={{0,8},{4,12},{8,0},{12,4},{16,24},{20,28},{24,16},{28,20},{1,9},{5... | collective-permute-start | bytes 147464 | tf_op jit(solution)/shard_map/ppermute | solution.py:44
  27.3 23.8 %collective-permute-start.3 = (bf16[128,1024]{1,0:T(8,128)(2,1)S(1)}, bf16[128,1024]{1,0:T(8,128)(2,1)S(1)}, u32[]{:S(2)}, u32[]{:S(2)}) collective-permute-start(bf16[128,1024]{1,0:T(8,128)(2,1)S(1)} %collective-permute-done), channel_id=1, source_target_pairs={{0,24},{4,28},{8,16},{12,20},{16,8},{20,12},{24,0},{28,4},{1,25},{... | collective-permute-start | bytes 786440 | tf_op jit(solution)/shard_map/ppermute | solution.py:44
  36.4 20.3 %collective-permute-start.7 = (bf16[2,32,384]{2,1,0:T(8,128)(2,1)S(1)}, bf16[2,32,384]{2,1,0:T(8,128)(2,1)S(1)}, u32[]{:S(2)}, u32[]{:S(2)}) collective-permute-start(bf16[2,32,384]{2,1,0:T(8,128)(2,1)S(1)} %get-tuple-element.128), channel_id=1, source_target_pairs={{0,16},{4,20},{8,24},{12,28},{16,0},{20,4},{24,8},{28,12},{1,17},{... | collective-permute-start | bytes 147464 | tf_op jit(solution)/shard_map/ppermute | solution.py:44
  51.1 24.7 %collective-permute-start.4 = (bf16[512,1024]{1,0:T(8,128)(2,1)S(1)}, bf16[512,1024]{1,0:T(8,128)(2,1)}, u32[]{:S(2)}, u32[]{:S(2)}) collective-permute-start(bf16[512,1024]{1,0:T(8,128)(2,1)S(1)} %constant_dynamic-update-slice_fusion.near_ref), channel_id=1, source_target_pairs={{0,1},{1,0},{2,3},{3,2},{4,5},{5,4},{6,7},{7,6},{8,9},{9,8},{10,11... | collective-permute-start | bytes 3145736 | tf_op jit(solution)/shard_map/ppermute | solution.py:50
  64.7 47.6 %collective-permute-start.29 = (bf16[128,1024]{1,0:T(8,128)(2,1)}, bf16[128,1024]{1,0:T(8,128)(2,1)}, u32[]{:S(2)}, u32[]{:S(2)}) collective-permute-start(bf16[128,1024]{1,0:T(8,128)(2,1)} %get-tuple-element.105), channel_id=1, source_target_pairs={{0,4},{4,0},{8,12},{12,8},{16,20},{20,16},{24,28},{28,24},{1,5},{5... | collective-permute-start | bytes 786440 | tf_op jit(solution)/shard_map/ppermute | solution.py:47
  71.0 41.4 %collective-permute-start.30 = (bf16[128,1024]{1,0:T(8,128)(2,1)}, bf16[128,1024]{1,0:T(8,128)(2,1)}, u32[]{:S(2)}, u32[]{:S(2)}) collective-permute-start(bf16[128,1024]{1,0:T(8,128)(2,1)} %get-tuple-element.105), channel_id=1, source_target_pairs={{0,2},{1,3},{2,0},{3,1},{4,6},{5,7},{6,4},{7,5},{8,10},{9,11},{10,... | collective-permute-start | bytes 786440 | tf_op jit(solution)/shard_map/ppermute | solution.py:56
  73.5 40.4 %collective-permute-start.31 = (bf16[128,1024]{1,0:T(8,128)(2,1)}, bf16[128,1024]{1,0:T(8,128)(2,1)}, u32[]{:S(2)}, u32[]{:S(2)}) collective-permute-start(bf16[128,1024]{1,0:T(8,128)(2,1)} %get-tuple-element.105), channel_id=1, source_target_pairs={{0,6},{1,7},{2,4},{3,5},{4,2},{5,3},{6,0},{7,1},{8,14},{9,15},{10,... | collective-permute-start | bytes 786440 | tf_op jit(solution)/shard_map/ppermute | solution.py:59
  104.0 34.6 %collective-permute-start.22 = (bf16[256,1536]{1,0:T(8,128)(2,1)}, bf16[256,1536]{1,0:T(8,128)(2,1)}, u32[]{:S(2)}, u32[]{:S(2)}) collective-permute-start(bf16[256,1536]{1,0:T(8,128)(2,1)} %pad_maximum_fusion.5), channel_id=1, source_target_pairs={{0,8},{4,12},{8,0},{12,4},{16,24},{20,28},{24,16},{28,20},{1,9},{5... | collective-permute-start | bytes 2359304 | tf_op jit(solution)/shard_map/ppermute | solution.py:44
  107.5 55.3 %collective-permute-start.23 = (bf16[256,1536]{1,0:T(8,128)(2,1)}, bf16[256,1536]{1,0:T(8,128)(2,1)S(1)}, u32[]{:S(2)}, u32[]{:S(2)}) collective-permute-start(bf16[256,1536]{1,0:T(8,128)(2,1)} %pad_maximum_fusion.5), channel_id=1, source_target_pairs={{0,16},{4,20},{8,24},{12,28},{16,0},{20,4},{24,8},{28,12},{1,17},{... | collective-permute-start | bytes 2359304 | tf_op jit(solution)/shard_map/ppermute | solution.py:44
  121.4 41.4 %collective-permute-start.32 = (bf16[512,1024]{1,0:T(8,128)(2,1)S(1)}, bf16[512,1024]{1,0:T(8,128)(2,1)S(1)}, u32[]{:S(2)}, u32[]{:S(2)}) collective-permute-start(bf16[512,1024]{1,0:T(8,128)(2,1)S(1)} %pad_maximum_fusion.2), channel_id=1, source_target_pairs={{0,1},{1,0},{2,3},{3,2},{4,5},{5,4},{6,7},{7,6},{8,9},{9,8},{10,11... | collective-permute-start | bytes 3145736 | tf_op jit(solution)/shard_map/ppermute | solution.py:50
  125.8 37.0 %collective-permute-start.24 = (bf16[256,1536]{1,0:T(8,128)(2,1)}, bf16[256,1536]{1,0:T(8,128)(2,1)S(1)}, u32[]{:S(2)}, u32[]{:S(2)}) collective-permute-start(bf16[256,1536]{1,0:T(8,128)(2,1)} %pad_maximum_fusion.5), channel_id=1, source_target_pairs={{0,24},{4,28},{8,16},{12,20},{16,8},{20,12},{24,0},{28,4},{1,25},{... | collective-permute-start | bytes 2359304 | tf_op jit(solution)/shard_map/ppermute | solution.py:44
  129.1 33.9 %collective-permute-start.20 = (bf16[512,1024]{1,0:T(8,128)(2,1)S(1)}, bf16[512,1024]{1,0:T(8,128)(2,1)S(1)}, u32[]{:S(2)}, u32[]{:S(2)}) collective-permute-start(bf16[512,1024]{1,0:T(8,128)(2,1)S(1)} %pad_maximum_fusion.1), channel_id=1, source_target_pairs={{0,1},{1,0},{2,3},{3,2},{4,5},{5,4},{6,7},{7,6},{8,9},{9,8},{10,11... | collective-permute-start | bytes 3145736 | tf_op jit(solution)/shard_map/ppermute | solution.py:50
  174.1 50.1 %collective-permute-start.59 = (bf16[256,1536]{1,0:T(8,128)(2,1)S(1)}, bf16[256,1536]{1,0:T(8,128)(2,1)S(1)}, u32[]{:S(2)}, u32[]{:S(2)}) collective-permute-start(bf16[256,1536]{1,0:T(8,128)(2,1)S(1)} %pad_maximum_fusion.6), channel_id=1, source_target_pairs={{0,8},{4,12},{8,0},{12,4},{16,24},{20,28},{24,16},{28,20},{1,9},{5... | collective-permute-start | bytes 2359304 | tf_op jit(solution)/shard_map/ppermute | solution.py:44
  191.3 55.2 %collective-permute-start.60 = (bf16[256,1536]{1,0:T(8,128)(2,1)S(1)}, bf16[256,1536]{1,0:T(8,128)(2,1)S(1)}, u32[]{:S(2)}, u32[]{:S(2)}) collective-permute-start(bf16[256,1536]{1,0:T(8,128)(2,1)S(1)} %pad_maximum_fusion.7), channel_id=1, source_target_pairs={{0,16},{4,20},{8,24},{12,28},{16,0},{20,4},{24,8},{28,12},{1,17},{... | collective-permute-start | bytes 2359304 | tf_op jit(solution)/shard_map/ppermute | solution.py:44
  192.0 54.5 %collective-permute-start.61 = (bf16[256,1536]{1,0:T(8,128)(2,1)S(1)}, bf16[256,1536]{1,0:T(8,128)(2,1)S(1)}, u32[]{:S(2)}, u32[]{:S(2)}) collective-permute-start(bf16[256,1536]{1,0:T(8,128)(2,1)S(1)} %pad_maximum_fusion.8), channel_id=1, source_target_pairs={{0,24},{4,28},{8,16},{12,20},{16,8},{20,12},{24,0},{28,4},{1,25},{... | collective-permute-start | bytes 2359304 | tf_op jit(solution)/shard_map/ppermute | solution.py:44
  195.4 52.6 %collective-permute-start.25 = (bf16[512,1024]{1,0:T(8,128)(2,1)S(1)}, bf16[512,1024]{1,0:T(8,128)(2,1)S(1)}, u32[]{:S(2)}, u32[]{:S(2)}) collective-permute-start(bf16[512,1024]{1,0:T(8,128)(2,1)S(1)} %slice.733), channel_id=1, source_target_pairs={{0,1},{1,0},{2,3},{3,2},{4,5},{5,4},{6,7},{7,6},{8,9},{9,8},{10,11... | collective-permute-start | bytes 3145736 | tf_op jit(solution)/shard_map/ppermute | solution.py:50
  195.6 58.6 %collective-permute-start.33 = (bf16[512,1024]{1,0:T(8,128)(2,1)S(1)}, bf16[512,1024]{1,0:T(8,128)(2,1)S(1)}, u32[]{:S(2)}, u32[]{:S(2)}) collective-permute-start(bf16[512,1024]{1,0:T(8,128)(2,1)S(1)} %slice.732), channel_id=1, source_target_pairs={{0,1},{1,0},{2,3},{3,2},{4,5},{5,4},{6,7},{7,6},{8,9},{9,8},{10,11... | collective-permute-start | bytes 3145736 | tf_op jit(solution)/shard_map/ppermute | solution.py:50
  331.4 26.4 %collective-permute-start.42 = (bf16[512,1024]{1,0:T(8,128)(2,1)}, bf16[512,1024]{1,0:T(8,128)(2,1)}, u32[]{:S(2)}, u32[]{:S(2)}) collective-permute-start(bf16[512,1024]{1,0:T(8,128)(2,1)} %convolution_convert_fusion.1), channel_id=1, source_target_pairs={{0,1},{1,0},{2,3},{3,2},{4,5},{5,4},{6,7},{7,6},{8,9},{9,8},{10,11... | collective-permute-start | bytes 3145736 | tf_op jit(solution)/shard_map/ppermute | solution.py:50
  360.3 21.3 %collective-permute-start.44 = (bf16[128,1024]{1,0:T(8,128)(2,1)S(1)}, bf16[128,1024]{1,0:T(8,128)(2,1)S(1)}, u32[]{:S(2)}, u32[]{:S(2)}) collective-permute-start(bf16[128,1024]{1,0:T(8,128)(2,1)S(1)} %get-tuple-element.70), channel_id=1, source_target_pairs={{0,16},{4,20},{8,24},{12,28},{16,0},{20,4},{24,8},{28,12},{1,17},{... | collective-permute-start | bytes 786440 | tf_op jit(solution)/shard_map/ppermute | solution.py:44
  361.7 19.9 %collective-permute-start.45 = (bf16[128,1024]{1,0:T(8,128)(2,1)S(1)}, bf16[128,1024]{1,0:T(8,128)(2,1)S(1)}, u32[]{:S(2)}, u32[]{:S(2)}) collective-permute-start(bf16[128,1024]{1,0:T(8,128)(2,1)S(1)} %get-tuple-element.69), channel_id=1, source_target_pairs={{0,24},{4,28},{8,16},{12,20},{16,8},{20,12},{24,0},{28,4},{1,25},{... | collective-permute-start | bytes 786440 | tf_op jit(solution)/shard_map/ppermute | solution.py:44
  (84 other events, 939.6 us)
Sparse Core Ops, SparseCore 0:
  13.2 71.7 all-gather.1
  289.8 152.8 reduce-scatter.1

commit v2 on v1

v2 whole, which is shorter than its diff:
```python
import functools
import math

import jax
import jax.numpy as jnp
from jax import lax
from jax.experimental import pallas as pl
from jax.experimental.layout import Layout, with_layout_constraint
from jax.experimental.pallas import tpu as pltpu
from jax.sharding import PartitionSpec as P


epsilon = 1e-05
masked_score = -1e30
low = jnp.bfloat16
wide = jnp.float32
lanes = 128
half_lanes = 64


def dot(a, b):
    return jnp.dot(a, b, preferred_element_type=wide)


def dot_t(a, b):
    return lax.dot_general(a, b, (((1,), (1,)), ((), ())), preferred_element_type=wide)


def t_dot(a, b):
    return lax.dot_general(a, b, (((0,), (0,)), ((), ())), preferred_element_type=wide)


class Place:
    def __init__(self):
        self.seq_size = lax.axis_size("seq")
        self.head_size = lax.axis_size("head")
        self.z_size = self.seq_size // 2
        self.y_size = self.head_size // 2
        self.seq = lax.axis_index("seq")
        self.head = lax.axis_index("head")
        self.z, self.x = self.seq // 2, self.seq % 2
        self.y, self.c = self.head // 2, self.head % 2

    def along_z(self, value, step):
        return lax.ppermute(value, "seq", [(i, i ^ (2 * step)) for i in range(self.seq_size)])

    def along_x(self, value):
        return lax.ppermute(value, "seq", [(i, i ^ 1) for i in range(self.seq_size)])

    def along_c(self, value):
        return lax.ppermute(value, "head", [(i, i ^ 1) for i in range(self.head_size)])

    def along_xy(self, value, dx, dy):
        if dy == 0:
            return self.along_x(value)
        if dx == 0:
            return lax.ppermute(
                value, "head", [(i, i ^ (2 * dy)) for i in range(self.head_size)]
            )
        return lax.ppermute(
            value,
            ("seq", "head"),
            [
                (s * self.head_size + h, (s ^ dx) * self.head_size + (h ^ (2 * dy)))
                for s in range(self.seq_size)
                for h in range(self.head_size)
            ],
        )

    def turn(self, value):
        return lax.ppermute(
            value,
            ("seq", "head"),
            [
                (s * self.head_size + h, ((s & ~1) | (h & 1)) * self.head_size + ((h & ~1) | (s & 1)))
                for s in range(self.seq_size)
                for h in range(self.head_size)
            ],
        )

    def pairs(self):
        return [(dx, dy) for dy in range(self.y_size) for dx in range(2)]

    def gather_xy(self, value):
        return [value if d == (0, 0) else self.along_xy(value, *d) for d in self.pairs()]

    def scatter_xy(self, blocks):
        return [
            block if d == (0, 0) else self.along_xy(block, *d)
            for d, block in zip(self.pairs(), blocks)
        ]

    def columns_z(self):
        return [[x + 2 * z for z in range(self.z_size)] for x in range(2)]

    def gather_z(self, value):
        return [value if d == 0 else self.along_z(value, d) for d in range(self.z_size)]

    def scatter_z(self, blocks):
        return [block if d == 0 else self.along_z(block, d) for d, block in enumerate(blocks)]

    def gather_steps(self, value, moves):
        held = value[None]
        for move in moves:
            held = jnp.concatenate([held, move(held)], axis=0)
        return held

    def scatter_steps(self, held, moves):
        for move in reversed(moves):
            cut = held.shape[0] // 2
            held = held[:cut].astype(wide) + move(held[cut:].astype(low)).astype(wide)
        return held[0]

    def xy_moves(self):
        steps = [1 << i for i in range(self.y_size.bit_length() - 1)]
        return [self.along_x] + [functools.partial(self.along_xy, dx=0, dy=step) for step in steps]

    def z_moves(self):
        steps = [1 << i for i in reversed(range(self.z_size.bit_length() - 1))]
        return [functools.partial(self.along_z, step=step) for step in steps]

    def z_order(self):
        order = [0]
        for step in [1 << i for i in reversed(range(self.z_size.bit_length() - 1))]:
            order = order + [step ^ d for d in order]
        return order


def called(name, move, *operands):
    with jax.named_scope(name):
        return move(*operands)


def tied(*values):
    return lax.optimization_barrier(values)


def pick(bit, zero, one):
    return jnp.where(bit == 0, zero, one)


def xor_list(blocks, me):
    step = 1
    while step < len(blocks):
        on = (me // step) % 2
        blocks = [pick(on, blocks[i], blocks[i ^ step]) for i in range(len(blocks))]
        step *= 2
    return blocks


def place_kernel(masks, me_ref, in_ref, out_ref):
    for i, mask in enumerate(masks):
        out_ref[jnp.bitwise_xor(me_ref[0], mask)] = in_ref[i]


def fetch_kernel(masks, me_ref, in_ref, out_ref):
    for i, mask in enumerate(masks):
        out_ref[i] = in_ref[jnp.bitwise_xor(me_ref[0], mask)]


def move_blocks(kernel, blocks, me, masks):
    return pl.pallas_call(
        functools.partial(kernel, masks),
        out_shape=jax.ShapeDtypeStruct(blocks.shape, blocks.dtype),
        in_specs=[pl.BlockSpec(memory_space=pltpu.SMEM), pl.BlockSpec(memory_space=pltpu.VMEM)],
        out_specs=pl.BlockSpec(memory_space=pltpu.VMEM),
        compiler_params=pltpu.CompilerParams(vmem_limit_bytes=32 * 2**20),
        cost_estimate=pl.CostEstimate(flops=0, bytes_accessed=4 * blocks.size, transcendentals=0),
    )(me.reshape(1).astype(jnp.int32), blocks)


def place(blocks, me, masks):
    return move_blocks(place_kernel, blocks, me, masks)


def fetch(blocks, me, masks):
    return move_blocks(fetch_kernel, blocks, me, masks)


def lane_ids(rows):
    return lax.broadcasted_iota(jnp.int32, (rows, lanes), 1)


def swap_halves(value):
    first = lane_ids(value.shape[0]) % half_lanes < half_lanes // 2
    return jnp.where(first, pltpu.roll(value, lanes - 32, 1), pltpu.roll(value, 32, 1))


def three_pieces(value):
    one = value.astype(low).astype(wide)
    rest = value - one
    two = rest.astype(low).astype(wide)
    return one, two, (rest - two).astype(low).astype(wide)


def attend_kernel(
    heads,
    bias_ref,
    near_ref,
    far_ref,
    w_ref,
    cosine_ref,
    sine_ref,
    kinds_ref,
    docs_col_ref,
    docs_row_ref,
    query_ref,
    key_ref,
    value_ref,
    out_ref,
):
    rows = near_ref.shape[0]
    length = 2 * rows
    step = min(rows, 256)
    padded = w_ref.shape[1] // 3
    for part, source in enumerate((near_ref, far_ref)):
        for start in range(0, rows, step):
            at = pl.ds(part * rows + start, step)
            packed = dot(source[start : start + step, :], w_ref[...])
            cosine, sine = cosine_ref[at, :], sine_ref[at, :]
            lane = lane_ids(step)
            kind = kinds_ref[at, :1]
            own = (lane == 64 + kind).astype(wide)
            own_two = (lane == 68 + kind).astype(wide)
            extra_query = ((lane == 72 + kind) | (lane == 76)).astype(wide)
            extra_key = own + own_two + ((lane >= 77) & (lane < 80)).astype(wide)
            extra_value = ((lane >= 64) & (lane < 67)).astype(wide)
            for head in range(heads):
                base = head // 2 * lanes
                query = packed[:, base : base + lanes]
                key = packed[:, padded + base : padded + base + lanes]
                value = packed[:, 2 * padded + base : 2 * padded + base + lanes]
                query = (query * cosine + swap_halves(query) * sine).astype(low).astype(wide) * 0.125
                key = key * cosine + swap_halves(key) * sine
                if head % 2:
                    query, key, value = (pltpu.roll(v, half_lanes, 1) for v in (query, key, value))
                body = lane < half_lanes
                extra = extra_query + own * bias_ref[0, head] + own_two * bias_ref[1, head]
                query_ref[head, at, :] = jnp.where(body, query, extra).astype(low)
                key_ref[head, at, :] = jnp.where(body, key, extra_key).astype(low)
                value_ref[head, at, :] = jnp.where(body, value, extra_value).astype(low)
    block = min(length, 256)
    lane = lane_ids(block)

    @pl.loop(0, length // block)
    def _(i):
        at = pl.ds(pl.multiple_of(i * block, block), block)
        allowed = docs_col_ref[at, :1] == docs_row_ref[...]
        done = []
        for head in range(heads):
            query = query_ref[head, at, :]
            scores = jnp.where(allowed, dot_t(query, key_ref[head]), masked_score)
            top = jnp.max(scores, axis=1, keepdims=True)
            weights = jnp.exp(scores - top).astype(low)
            summed = dot(weights, value_ref[head])
            total = summed[:, half_lanes : half_lanes + 1]
            one, two, three = three_pieces(-(top + jnp.log(total)))
            extra = jnp.where(lane == 77, one, jnp.where(lane == 78, two, jnp.where(lane == 79, three, 0.0)))
            query_ref[head, at, :] = jnp.where(lane < 77, query.astype(wide), extra).astype(low)
            done.append(summed / total)
        for base in range(0, heads, 2):
            both = done[base]
            if base + 1 < heads:
                both = jnp.where(lane < half_lanes, both, pltpu.roll(done[base + 1], half_lanes, 1))
            out_ref[at, base // 2 * lanes : (base // 2 + 1) * lanes] = both.astype(low)


def attend(bias, near, far, w, cosine, sine, ids, heads):
    length = 2 * near.shape[0]
    padded = w.shape[1] // 3
    vmem = pl.BlockSpec(memory_space=pltpu.VMEM)
    whole = jax.ShapeDtypeStruct((heads, length, lanes), low)
    return pl.pallas_call(
        functools.partial(attend_kernel, heads),
        out_shape=(whole, whole, whole, jax.ShapeDtypeStruct((length, padded), low)),
        in_specs=[pl.BlockSpec(memory_space=pltpu.SMEM)] + [vmem] * 8,
        out_specs=(vmem, vmem, vmem, vmem),
        compiler_params=pltpu.CompilerParams(vmem_limit_bytes=48 * 2**20),
        cost_estimate=pl.CostEstimate(
            flops=2**20, bytes_accessed=2**10, transcendentals=0
        ),
    )(bias, near, far, w, cosine, sine, *ids)


def attend_grad_kernel(
    heads,
    query_ref,
    key_ref,
    value_ref,
    out_ref,
    grad_out_ref,
    cosine_ref,
    sine_ref,
    kinds_ref,
    docs_col_ref,
    docs_row_ref,
    near_ref,
    far_ref,
    w_ref,
    near_up_ref,
    far_up_ref,
    grad_w_ref,
    bias_ref,
    grad_query_ref,
    grad_key_ref,
    grad_value_ref,
    packed_ref,
):
    length = query_ref.shape[1]
    padded = packed_ref.shape[1] // 3
    half = length // 2
    block = min(length, 256)
    lane = lane_ids(block)
    grad_key_ref[...] = jnp.zeros_like(grad_key_ref)
    grad_value_ref[...] = jnp.zeros_like(grad_value_ref)

    @pl.loop(0, length // block)
    def _(i):
        at = pl.ds(pl.multiple_of(i * block, block), block)
        allowed = docs_col_ref[:, :1] == docs_row_ref[:, at]
        for head in range(heads):
            columns = slice(head // 2 * lanes, (head // 2 + 1) * lanes)
            grad_out = grad_out_ref[at, columns].astype(wide)
            product = grad_out * out_ref[at, columns].astype(wide)
            mine = (lane >= half_lanes) if head % 2 else (lane < half_lanes)
            row_dot = jnp.sum(jnp.where(mine, product, 0.0), axis=1, keepdims=True)
            one, two, three = three_pieces(-row_dot)
            if head % 2:
                grad_out = pltpu.roll(grad_out, half_lanes, 1)
            extra = jnp.where(lane == 64, one, jnp.where(lane == 65, two, jnp.where(lane == 66, three, 0.0)))
            grad_out = jnp.where(lane < half_lanes, grad_out, extra).astype(low)
            query, key = query_ref[head, at, :], key_ref[head]
            weights = jnp.exp(jnp.where(allowed, dot_t(key, query), masked_score))
            grad_scores = (weights * dot_t(value_ref[head], grad_out)).astype(low)
            grad_value_ref[head] += dot(weights.astype(low), grad_out)
            grad_key_ref[head] += dot(grad_scores, query)
            grad_query_ref[head, at, :] = t_dot(grad_scores, key)

    for start in range(0, length, block):
        at = slice(start, start + block)
        cosine, sine = cosine_ref[at, :], sine_ref[at, :]
        for base in range(0, heads, 2):

            def joined(ref):
                both = ref[base, at, :]
                if base + 1 < heads:
                    both = jnp.where(lane < half_lanes, both, pltpu.roll(ref[base + 1, at, :], half_lanes, 1))
                else:
                    both = jnp.where(lane < half_lanes, both, 0.0)
                return both

            columns = base // 2 * lanes
            query = joined(grad_query_ref) * 0.125
            key = joined(grad_key_ref)
            value = joined(grad_value_ref)
            query = query * cosine - swap_halves(query) * sine
            key = key * cosine - swap_halves(key) * sine
            for part, result in enumerate((query, key, value)):
                packed_ref[at, part * padded + columns : part * padded + columns + lanes] = result.astype(low)
    for start in range(0, half, block):
        here = slice(start, start + block)
        far_up_ref[here, :] = dot_t(packed_ref[half + start : half + start + block, :], w_ref[...]).astype(low)
        near_up_ref[here, :] = dot_t(packed_ref[here, :], w_ref[...]).astype(low)
    width = near_ref.shape[1]
    for start in range(0, width, 256):
        here = slice(start, start + 256)
        grads = t_dot(near_ref[:, here], packed_ref[:half, :]) + t_dot(far_ref[:, here], packed_ref[half:, :])
        grad_w_ref[here, :] = grads.astype(low)
    every = lane_ids(length)
    kinds = kinds_ref[:, :1]
    for head in range(heads):
        grads = grad_key_ref[head]
        same = jnp.sum(jnp.where(every == 72 + kinds, grads, 0.0))
        total = jnp.sum(jnp.where(every == 76, grads, 0.0))
        bias_ref[head, 0] = same
        bias_ref[head, 1] = total - same


def attend_grad(query, key, value, out, grad_out, cosine, sine, ids, near, far, w):
    heads, length, _ = query.shape
    half, width = near.shape
    vmem = pl.BlockSpec(memory_space=pltpu.VMEM)
    scratch = pltpu.VMEM((heads, length, lanes), wide)
    return pl.pallas_call(
        functools.partial(attend_grad_kernel, heads),
        out_shape=(
            jax.ShapeDtypeStruct((half, width), low),
            jax.ShapeDtypeStruct((half, width), low),
            jax.ShapeDtypeStruct(w.shape, low),
            jax.ShapeDtypeStruct((heads, 2), wide),
        ),
        in_specs=[vmem] * 13,
        out_specs=(vmem, vmem, vmem, pl.BlockSpec(memory_space=pltpu.SMEM)),
        scratch_shapes=[scratch] * 3 + [pltpu.VMEM((length, w.shape[1]), low)],
        compiler_params=pltpu.CompilerParams(vmem_limit_bytes=48 * 2**20),
        cost_estimate=pl.CostEstimate(flops=2**20, bytes_accessed=2**10, transcendentals=0),
    )(
        query, key, value, out, grad_out, cosine, sine, *ids, near, far, w
    )


def feed_kernel(units, tokens_ref, grads_ref, w_ref, hidden_ref, grad_units_ref, up_ref, down_ref):
    gate_up = dot(tokens_ref[...], w_ref[:, : 2 * units])
    count = grads_ref.shape[0] * grads_ref.shape[1]
    grad_hidden = dot(grads_ref[...].reshape(count, -1), w_ref[:, 2 * units :])
    gate_values, up_values = gate_up[:, :units], gate_up[:, units:]
    sigmoid_gate = jax.nn.sigmoid(gate_values)
    activated = gate_values * sigmoid_gate
    hidden_ref[...] = (activated * up_values).astype(low)
    slope = sigmoid_gate + activated * (1.0 - sigmoid_gate)
    grad_units_ref[:, :units] = (grad_hidden * up_values * slope).astype(low)
    grad_units_ref[:, units:] = (grad_hidden * activated).astype(low)
    up_ref[...] = dot_t(grad_units_ref[...], w_ref[:, : 2 * units]).astype(low)
    down_ref[...] = dot_t(hidden_ref[...], w_ref[:, 2 * units :]).astype(low)


def feed(tokens, grads, w):
    count, width = tokens.shape
    rows = count // grads.shape[0]
    units = w.shape[1] // 3
    step = min(count, 256)
    return pl.pallas_call(
        functools.partial(feed_kernel, units),
        grid=(count // step,),
        out_shape=(
            jax.ShapeDtypeStruct((count, units), low),
            jax.ShapeDtypeStruct((count, 2 * units), low),
            jax.ShapeDtypeStruct((count, width), low),
            jax.ShapeDtypeStruct((count, width), low),
        ),
        in_specs=[
            pl.BlockSpec((step, width), lambda i: (i, 0)),
            pl.BlockSpec((step // rows, rows, width), lambda i: (i, 0, 0)),
            pl.BlockSpec(memory_space=pltpu.VMEM),
        ],
        out_specs=(
            pl.BlockSpec((step, units), lambda i: (i, 0)),
            pl.BlockSpec((step, 2 * units), lambda i: (i, 0)),
            pl.BlockSpec((step, width), lambda i: (i, 0)),
            pl.BlockSpec((step, width), lambda i: (i, 0)),
        ),
        compiler_params=pltpu.CompilerParams(vmem_limit_bytes=32 * 2**20),
        cost_estimate=pl.CostEstimate(
            flops=10 * count * width * units, bytes_accessed=8 * 2**20, transcendentals=count * units
        ),
    )(tokens, grads, w)


def feed_grad_kernel(units, *refs):
    *parts, out_ref = refs
    results = [0.0, 0.0]
    for tokens_ref, grads_ref, hidden_ref, grad_units_ref in (parts[:4], parts[4:]):
        grads = grads_ref[...]
        grads = grads.reshape(grads.shape[0] * grads.shape[1], -1)
        results[0] += t_dot(tokens_ref[...], grad_units_ref[...])
        results[1] += t_dot(grads, hidden_ref[...])
    out_ref[:, : 2 * units] = results[0].astype(low)
    out_ref[:, 2 * units :] = results[1].astype(low)


def feed_grad(near, far):
    tokens, grads, hidden, _ = near
    count, width = tokens.shape
    rows = count // grads.shape[0]
    units = hidden.shape[1]
    step = min(width, 256)
    whole = pl.BlockSpec(memory_space=pltpu.VMEM)
    part = [
        pl.BlockSpec((count, step), lambda i: (0, i)),
        pl.BlockSpec((grads.shape[0], rows, step), lambda i: (0, 0, i)),
        whole,
        whole,
    ]
    return pl.pallas_call(
        functools.partial(feed_grad_kernel, units),
        grid=(width // step,),
        out_shape=jax.ShapeDtypeStruct((width, 3 * units), low),
        in_specs=part + part,
        out_specs=pl.BlockSpec((step, 3 * units), lambda i: (i, 0)),
        compiler_params=pltpu.CompilerParams(vmem_limit_bytes=32 * 2**20),
        cost_estimate=pl.CostEstimate(
            flops=12 * count * width * units, bytes_accessed=12 * 2**20, transcendentals=0
        ),
    )(*near, *far)


def rope_tables(stamps, dimension):
    halfway = dimension // 2
    frequency = jnp.exp(-math.log(10000.0) * jnp.arange(halfway, dtype=wide) / halfway)
    repeated = jnp.tile(frequency, lanes // halfway)
    angles = stamps.astype(wide)[:, None] * repeated[None, :]
    sign = jnp.where(jnp.arange(lanes) % dimension < halfway, -1.0, 1.0)
    return (jnp.cos(angles), jnp.sin(angles) * sign[None, :])


def shards(
    inputs,
    gain_attn,
    w_qkv,
    head_bias,
    w_out,
    gain_ffn,
    w_gate,
    w_up,
    w_down,
    time_ids,
    variate_ids,
    seq_ids,
    cotangent,
):
    at = Place()
    z_size, y_size = at.z_size, at.y_size
    tokens = inputs[0].astype(wide)
    rows, width = tokens.shape
    head_count = head_bias.shape[0]
    head_dim = width // head_count
    groups = at.seq_size
    heads = head_count // groups
    group_width = heads * head_dim
    padded = (heads + 1) // 2 * lanes
    share = width // (at.seq_size * at.head_size)
    group = 2 * at.z + at.c
    window = 2 * at.y + at.x
    device_id = at.seq * at.head_size + at.head

    inverse_one = lax.rsqrt(jnp.mean(tokens * tokens, axis=-1, keepdims=True) + epsilon)
    unit = tokens * inverse_one
    turned = called("tokens_turn", at.turn, unit.astype(low))

    depth, units = w_gate.shape[0], w_gate.shape[1] // 2
    turned, late_gate, late_up, late_down = tied(turned, w_gate, w_up, w_down)
    down_t = with_layout_constraint(late_down.T, Layout(major_to_minor=(0, 1)))
    firsts = jnp.concatenate([v[:, :units] for v in (late_gate, late_up, down_t)], axis=1)
    seconds = jnp.concatenate([v[:, units:] for v in (late_gate, late_up, down_t)], axis=1)
    mine = pick(at.x, firsts, seconds)
    other = called("ffn_x", at.along_x, pick(at.x, seconds, firsts))
    z_block = jnp.concatenate([pick(at.x, mine, other), pick(at.x, other, mine)], axis=0)

    gain_one = gain_attn.astype(wide)[:, None]
    scaled = (w_qkv.astype(wide) * gain_one).astype(low)

    def to_parts(columns):
        parts = columns.reshape(-1, groups, heads, 3, head_dim).transpose(0, 1, 3, 2, 4)
        parts = parts.reshape(-1, groups, 3, group_width)
        parts = jnp.pad(parts, ((0, 0), (0, 0), (0, 0), (0, padded - group_width)))
        return parts.reshape(-1, groups, 3 * padded)

    parts = to_parts(scaled).reshape(share, z_size, 2, 3 * padded)
    core_own = pick(at.c, parts[:, :, 0], parts[:, :, 1])
    core_sent = pick(at.c, parts[:, :, 1], parts[:, :, 0]).reshape(-1, 3 * padded)

    def with_extra(block, *values):
        extra = jnp.stack([jnp.pad(v.astype(low), (0, 3 * padded - v.shape[0])) for v in values])
        return jnp.concatenate([block, jnp.pad(extra, ((0, 16 - len(values)), (0, 0)))], axis=0)

    core_got = called("qkv_core", at.along_c, with_extra(core_sent, gain_ffn))
    both = jnp.stack([core_own, core_got[:-16].reshape(core_own.shape)])
    both, turned, w_out_early = tied(both, turned, w_out)
    gains = jnp.concatenate([gain_ffn, core_got[-16, :share]])
    sent = []
    for d in range(z_size):
        block = lax.dynamic_index_in_dim(both, jnp.bitwise_xor(at.z, d), axis=2, keepdims=False)
        sent.append(with_extra(block.reshape(-1, 3 * padded), gains))
    by_z = jnp.stack(called("qkv_z", at.scatter_z, sent))
    gains = by_z[:, -16, : 2 * share].reshape(-1)
    by_z = by_z[:, :-16].reshape(-1, 3 * padded)
    out_z = called("out_z", at.gather_steps, w_out_early, at.z_moves()).reshape(-1, width)
    near = called("tokens_z", at.gather_steps, turned, at.z_moves()).reshape(-1, width)
    near, z_block = tied(near, z_block)
    w_ffn = lax.all_gather(z_block, "seq", axis=0, tiled=True, axis_index_groups=at.columns_z())
    by_xy = called("qkv_xy", at.gather_steps, with_extra(by_z, gains), at.xy_moves())
    gains = by_xy[:, -16, : gains.shape[0]].reshape(y_size, 2, z_size, 2, share)
    gains = gains.transpose(2, 1, 0, 3, 4).reshape(-1, share)
    by_xy = by_xy[:, :-16]
    devices = jnp.arange(at.seq_size * at.head_size)
    from_device = (devices[None, :] == jnp.bitwise_xor(devices[:, None], device_id)).astype(low)
    gain_two = dot(from_device, gains).reshape(1, width)
    masks = [
        (2 * d + dx) * at.head_size + 2 * dy + e
        for dx, dy in at.pairs()
        for d in range(z_size)
        for e in range(2)
    ]
    w_heads = place(by_xy.reshape(-1, share, 3 * padded), device_id, masks).reshape(width, 3 * padded)

    time_ids, variate_ids, seq_ids, by_z = tied(time_ids, variate_ids, seq_ids, by_z)

    def of_window(ids):
        row = lax.dynamic_index_in_dim(ids, window, axis=0, keepdims=False).reshape(z_size, 2, rows)
        order = [
            lax.dynamic_slice(
                row, (jnp.bitwise_xor(at.z, d), jnp.bitwise_xor(at.c, e), 0), (1, 1, rows)
            ).reshape(rows)
            for e in range(2)
            for d in at.z_order()
        ]
        return jnp.concatenate(order)

    docs = of_window(seq_ids)
    docs_columns = jnp.broadcast_to(docs[:, None], (docs.shape[0], lanes))
    kinds = jnp.broadcast_to(of_window(variate_ids)[:, None], docs_columns.shape)
    cosine, sine = rope_tables(of_window(time_ids), head_dim)
    local_bias = lax.dynamic_slice_in_dim(head_bias, group * heads, heads, 0)
    difference = local_bias[:, 0] - local_bias[:, 1]
    difference_high = difference.astype(low).astype(wide)
    bias = jnp.stack([difference_high, difference - difference_high])

    grad_out = cotangent[0]
    xy_rows = jnp.concatenate([grad_out, out_z], axis=0)
    xy_rows = called("cotangent_x", at.gather_steps, xy_rows, at.xy_moves()[:1])

    near, w_heads, cosine, sine, kinds, docs, docs_columns = tied(
        near, w_heads, cosine, sine, kinds, docs, docs_columns
    )
    ids = (kinds, docs_columns, docs.reshape(1, -1))
    xy_rows = called("cotangent_y", at.gather_steps, xy_rows, at.xy_moves()[1:])
    xy_rows = xy_rows.reshape(2 * y_size, -1, width)
    far = called("tokens_core", at.along_c, near)
    query, key, value, attended = attend(bias, near, far, w_heads, cosine, sine, ids, heads)

    xy_rows, query = tied(xy_rows, query)
    xy_rows_far = called("cotangent_core", at.along_c, xy_rows)
    out_blocks = jnp.stack([xy_rows[:, rows:], xy_rows_far[:, rows:]]).reshape(-1, share, width)
    out_masks = [
        (dx * z_size + d) * at.head_size + 2 * dy + e
        for e in range(2)
        for dx, dy in at.pairs()
        for d in range(z_size)
    ]
    out_rows = place(out_blocks, at.head, out_masks).reshape(width, width)

    sent = attended[:, :group_width].reshape(2, z_size, rows, group_width)
    places = {d: i for i, d in enumerate(at.z_order())}
    received = called("attended_z", at.scatter_z, [sent[:, places[d]] for d in range(z_size)])
    received = [received[d] for d in at.z_order()]
    kept = jnp.concatenate([block[0] for block in received], axis=1)
    passed = jnp.concatenate([block[1] for block in received], axis=1)
    passed = called("attended_core", at.along_c, passed)
    passed, w_ffn = tied(passed, w_ffn)
    merged = called("attended_turn", at.turn, jnp.concatenate([kept, passed], axis=1))

    middle = tokens + dot(merged, out_rows)
    inverse_two = lax.rsqrt(jnp.mean(middle * middle, axis=-1, keepdims=True) + epsilon)
    unit_two = middle * inverse_two
    normed_two = (unit_two * gain_two).astype(low)
    normed_near = jnp.concatenate(called("normed_xy", at.gather_xy, normed_two), axis=0)
    normed_far = called("normed_core", at.along_c, normed_near)

    hidden_near, units_near, up_near, down_near = feed(normed_near, xy_rows, w_ffn)
    hidden_far, units_far, up_far, down_far = feed(normed_far, xy_rows_far, w_ffn)

    units_far, up_far = tied(units_far, up_far)
    grad_w_ffn = feed_grad(
        (normed_near, xy_rows, hidden_near, units_near),
        (normed_far, xy_rows_far, hidden_far, units_far),
    )
    up_far = called("up_core", at.along_c, up_far)
    up_far, grad_w_ffn = tied(up_far, grad_w_ffn)
    kept = [
        up_near[i * rows : (i + 1) * rows].astype(wide) + up_far[i * rows : (i + 1) * rows].astype(wide)
        for i in range(2 * y_size)
    ]
    received = called("up_xy", at.scatter_xy, kept[:1] + [block.astype(low) for block in kept[1:]])
    grad_two = functools.reduce(jnp.add, [block.astype(wide) for block in received])
    gain_part = jnp.sum(grad_two * unit_two, axis=0)
    upstream = grad_two * gain_two
    grad_w_ffn = lax.psum_scatter(
        grad_w_ffn, "seq", scatter_dimension=0, tiled=True, axis_index_groups=at.columns_z()
    )

    grad_middle = (
        grad_out.astype(wide)
        + inverse_two * upstream
        - unit_two * inverse_two * jnp.mean(upstream * unit_two, axis=-1, keepdims=True)
    )
    grad_branch = grad_middle.astype(low)
    grad_merged = dot_t(grad_branch, out_rows).astype(low)

    turned_back = called("merged_turn", at.turn, grad_merged)
    cut = width // 2
    kept, passed = turned_back[:, :cut], called("merged_core", at.along_c, turned_back[:, cut:])
    sent = []
    for d in range(z_size):
        columns = slice(places[d] * group_width, (places[d] + 1) * group_width)
        sent.append(jnp.stack([part[:, columns] for part in (kept, passed)]))
    received = called("merged_z", at.scatter_z, sent)
    received = jnp.stack([received[d] for d in at.z_order()], axis=1)
    grad_attended = received.reshape(2 * z_size * rows, group_width)
    if padded > group_width:
        grad_attended = jnp.pad(grad_attended, ((0, 0), (0, padded - group_width)))

    down_far, grad_branch = tied(down_far, grad_branch)
    down = down_near.astype(wide) + called("down_core", at.along_c, down_far).astype(wide)
    down = down.reshape(y_size, 2, rows, width)
    down = called("down_y", at.scatter_steps, down, at.xy_moves()[1:])

    merged, grad_branch, turned_back = tied(merged, grad_branch, turned_back)
    grad_out_rows = t_dot(merged, grad_branch).astype(low)
    grad_out_rows = fetch(grad_out_rows.reshape(-1, share, width), at.head, out_masks)
    grad_out_rows = grad_out_rows.reshape(2, 2 * y_size, z_size * share, width)
    grad_out_far = called("w_out_core", at.along_c, grad_out_rows[1])
    grad_out_rows = (grad_out_rows[0].astype(wide) + grad_out_far.astype(wide)).astype(low)

    grad_attended, down, grad_out_rows = tied(grad_attended, down, grad_out_rows)
    output = middle + called("down_x", at.scatter_steps, down, at.xy_moves()[:1])
    upstream_near, upstream_far, grad_heads, bias_grad = attend_grad(
        query, key, value, attended, grad_attended, cosine, sine, ids, near, far, w_heads
    )

    upstream_far, grad_w_ffn = tied(upstream_far, grad_w_ffn)
    upstream_far = called("input_core", at.along_c, upstream_far)
    upstream_near = upstream_near.astype(wide) + upstream_far.astype(wide)
    z_moves = at.z_moves()
    upstream_z = upstream_near.reshape(z_size, rows, width)
    cut = z_size // 2
    upstream_z = upstream_z[:cut] + called("input_z", z_moves[-1], upstream_z[cut:].astype(low)).astype(wide)

    grad_heads = grad_heads.reshape(z_size, 2, y_size, 2, share, 3 * padded)

    def halves(values):
        high = values.astype(low)
        return high, (values - high.astype(wide)).astype(low)

    def joined(block, row, count):
        return block[row, :count].astype(wide) + block[row + 1, :count].astype(wide)

    gain_part = gain_part.reshape(z_size, 2, y_size, 2, share)
    bias_count, gain_count = 2 * heads, 2 * z_size * share

    grad_out_rows = grad_out_rows.reshape(2 * y_size, z_size, share, 2, width // 2)
    grad_out_rows = grad_out_rows.transpose(0, 1, 3, 2, 4).reshape(2 * y_size, -1, width // 2)

    def rows_of(index, dx, dy):
        x, y = jnp.bitwise_xor(at.x, dx), jnp.bitwise_xor(at.y, dy)
        picked = lax.dynamic_slice(
            grad_heads, (0, x, y, 0, 0, 0), (z_size, 1, 1, 2, share, 3 * padded)
        )
        gain = lax.dynamic_slice(gain_part, (0, x, y, 0, 0), (z_size, 1, 1, 2, share)).reshape(-1)
        block = with_extra(picked.reshape(-1, 3 * padded), *halves(bias_grad.reshape(-1)), *halves(gain))
        return jnp.concatenate([block, jnp.pad(grad_out_rows[index], ((0, 16), (0, 0)))], axis=1)

    received = called("grad_qkv_xy", at.scatter_xy, [rows_of(i, *d) for i, d in enumerate(at.pairs())])
    summed = functools.reduce(jnp.add, [block.astype(wide) for block in received])
    summed, upstream_z = tied(summed, upstream_z)
    upstream_one = called("input_z", at.scatter_steps, upstream_z, z_moves[:-1])
    bias_sum = joined(summed[-16:], 0, bias_count)
    gain_sum = joined(summed[-16:], 2, gain_count).reshape(z_size, 2 * share)
    out_sum = summed[:-16, 3 * padded :].astype(low).reshape(z_size, 2 * share, width // 2)
    summed = summed[:-16, : 3 * padded].astype(low).reshape(z_size, 2 * share, 3 * padded)
    sent = []
    for d in range(z_size):
        block, gain = (
            lax.dynamic_index_in_dim(v, jnp.bitwise_xor(at.z, d), axis=0, keepdims=False)
            for v in (summed, gain_sum)
        )
        block = with_extra(block, *halves(bias_sum), *halves(gain))
        out_block = jnp.pad(out_sum[places[d]], ((0, 16), (0, 0)))
        sent.append(jnp.concatenate([block, out_block], axis=1))
    received = called("grad_qkv_z", at.scatter_z, sent)
    grad_w_out = functools.reduce(
        jnp.add, [block[:-16, 3 * padded :].astype(wide) for block in received]
    )
    grad_w_out = grad_w_out.reshape(2, share, width // 2).transpose(1, 0, 2).reshape(share, width)
    received = [block[:, : 3 * padded] for block in received]
    bias_z = jnp.concatenate([joined(block[-16:], 0, bias_count) for block in received])
    gain_sum = functools.reduce(jnp.add, [joined(block[-16:], 2, 2 * share) for block in received])
    received = jnp.stack([block[:-16] for block in received]).reshape(z_size, 2, share, 3 * padded)
    core_own = pick(at.c, received[:, 0], received[:, 1])
    core_sent = pick(at.c, received[:, 1], received[:, 0]).reshape(-1, 3 * padded)
    gain_own = pick(at.c, gain_sum[:share], gain_sum[share:])
    gain_sent = pick(at.c, gain_sum[share:], gain_sum[:share])
    core_sent, upstream_one = tied(core_sent, upstream_one)
    mine = pick(at.x, grad_w_ffn[:depth], grad_w_ffn[depth:]).astype(wide)
    other = pick(at.x, grad_w_ffn[depth:], grad_w_ffn[:depth])
    other = called("grad_ffn_x", at.along_x, other).astype(wide)
    upstream_one, other = tied(upstream_one.astype(low), other)
    upstream_one = called("input_turn", at.turn, upstream_one).astype(wide)
    grad_input = grad_middle + inverse_one * (
        upstream_one - unit * jnp.mean(upstream_one * unit, axis=-1, keepdims=True)
    )
    core_got = called(
        "grad_qkv_core", at.along_c, with_extra(core_sent, *halves(bias_z), *halves(gain_sent))
    )
    core_other = core_got[:-16].reshape(z_size, share, 3 * padded)
    grad_gain_ffn = gain_own + joined(core_got[-16:], 2, share)
    biases = jnp.stack([bias_z, joined(core_got[-16:], 0, z_size * bias_count)])
    biases = list(biases.reshape(2, z_size, heads, 2).transpose(1, 0, 2, 3).reshape(groups, heads, 2))
    full_bias = jnp.concatenate(xor_list(biases, group), axis=0)
    by_group = jnp.stack([core_own, core_other], axis=1).reshape(groups, share, 3 * padded)
    by_group = place(by_group, group, list(range(groups))).astype(wide).reshape(groups, share, 3, padded)
    by_group = by_group[..., :group_width].reshape(groups, share, 3, heads, head_dim)
    raw = by_group.transpose(1, 0, 3, 2, 4).reshape(share, 3 * width)
    grad_w_qkv = raw * gain_one
    grad_gain_attn = jnp.sum(raw * w_qkv.astype(wide), axis=1)
    first, second = pick(at.x, mine, other), pick(at.x, other, mine)
    grad_w_gate, grad_w_up, grad_w_down_t = (
        jnp.concatenate([first[:, i * units : (i + 1) * units], second[:, i * units : (i + 1) * units]], axis=1)
        for i in range(3)
    )
    return (
        output.astype(low).reshape(1, rows, width),
        grad_input.astype(low).reshape(1, rows, width),
        grad_gain_attn,
        grad_w_qkv,
        full_bias,
        grad_w_out,
        grad_gain_ffn,
        grad_w_gate,
        grad_w_up,
        grad_w_down_t.T,
    )


def solution(mesh):
    placed = (
        P("head", "seq", None),
        P(("seq", "head")),
        P(("seq", "head"), None),
        P(),
        P(("seq", "head"), None),
        P(("seq", "head")),
        P("seq", "head"),
        P("seq", "head"),
        P("head", "seq"),
        P(),
        P(),
        P(),
        P("head", "seq", None),
    )
    return jax.shard_map(
        shards,
        mesh=mesh,
        in_specs=placed,
        out_specs=(
            P("head", "seq", None),
            P("head", "seq", None),
            P(("seq", "head")),
            P(("seq", "head"), None),
            P(),
            P(("seq", "head"), None),
            P(("seq", "head")),
            P("seq", "head"),
            P("seq", "head"),
            P("head", "seq"),
        ),
        check_vma=False,
    )
```

time: 461 us -> 334 us (0.72); the launches traced: 452 us -> 332 us
  waiting for transfers between devices: 222 us -> 136 us
  starting transfers between devices: 114 us -> 69.7 us
  matrix products: 23.8 us -> 4.04 us
  Pallas kernels: 19.6 us -> 35.9 us
  other arithmetic: 29.2 us -> 38.5 us
    ppermute x26 -> x18, waiting for transfers between devices: 134 us -> 51 us  [along_z(): lax.ppermute(value, 'seq', [(i, i ^ 2 * step) for i in range(self.seq_siz...]
    reduce_scatter x1, waiting for transfers between devices: 56 us -> 0.01 us  [shards(): lax.psum_scatter(grad_w_ffn, 'seq', scatter_dimension=0, tiled=True, axis...]
    ppermute x26 -> x18, starting transfers between devices: 72.2 us -> 24.5 us  [along_z(): lax.ppermute(value, 'seq', [(i, i ^ 2 * step) for i in range(self.seq_siz...]
    ppermute x9 -> x8, waiting for transfers between devices: 9.15 us -> 31.3 us  [along_x(): lax.ppermute(value, 'seq', [(i, i ^ 1) for i in range(self.seq_size)])]
    ppermute x8 -> x6, waiting for transfers between devices: 20.9 us -> 41.8 us  [along_xy(): lax.ppermute(value, 'head', [(i, i ^ 2 * dy) for i in range(self.head_siz...]
    pallas_call x4 -> x7, Pallas kernels: 2.27 us -> 15.4 us  [the longest x2 9.63 us: feed(): pl.pallas_call(functools.partial(feed_kernel, units), grid=(count // step...]
    ppermute x9 -> x8, starting transfers between devices: 11.8 us -> 20.4 us  [along_x(): lax.ppermute(value, 'seq', [(i, i ^ 1) for i in range(self.seq_size)])]
    dot_general x11 -> x1, matrix products: 9.41 us -> 1.77 us  [t_dot(): lax.dot_general(a, b, (((0,), (0,)), ((), ())), preferred_element_type=wide)]
  transfers between devices with their start and end apart: 67 -> 52, of which waited for: 27 -> 24; matrix products, arithmetic and copies ran while one was open for 13% -> 18% of each run, Pallas kernels for 4% -> 9%
where the time goes in v2:
time: 334 us; the launch traced here: 332 us
  waiting for transfers between devices  136 us (41%)
  starting transfers between devices  69.7 us (21%)
  other arithmetic  38.5 us (12%)
  Pallas kernels  35.9 us (11%)
  local copies, waits for them, and re-layouts  31.2 us (9%)
  between operations  16.2 us (5%)
  matrix products  4.04 us (1%)
    ppermute x18, waiting for transfers between devices, along_z(): lax.ppermute(value, 'seq', [(i, i ^ 2 * step) for i in range(self.seq_siz...  51 us
    ppermute x6, waiting for transfers between devices, along_xy(): lax.ppermute(value, 'head', [(i, i ^ 2 * dy) for i in range(self.head_siz...  41.8 us
    ppermute x8, waiting for transfers between devices, along_x(): lax.ppermute(value, 'seq', [(i, i ^ 1) for i in range(self.seq_size)])  31.3 us
    ppermute x18, starting transfers between devices, along_z(): lax.ppermute(value, 'seq', [(i, i ^ 2 * step) for i in range(self.seq_siz...  24.5 us
    ppermute x8, starting transfers between devices, along_x(): lax.ppermute(value, 'seq', [(i, i ^ 1) for i in range(self.seq_size)])  20.4 us
    pallas_call x1, Pallas kernels, attend_grad(): pl.pallas_call(functools.partial(attend_grad_kernel, heads), out_shape=(j...  11.6 us
    unnamed x164, local copies, waits for them, and re-layouts  9.75 us
    pallas_call x2, Pallas kernels, feed(): pl.pallas_call(functools.partial(feed_kernel, units), grid=(count // step...  9.63 us
  transfers between devices with their start and end apart: 52, of which 24 were waited for; matrix products, arithmetic and copies ran while one was open for 18% of the time, Pallas kernels for 9%

profile of v2, /device:TPU:0, one launch (start us, length us, event | category | flops | bytes accessed | tf_op | source)
XLA Modules:
  0.0 331.5 jit_solution(8000598109847513870)
XLA Ops:
  22.2 7.9 %collective-permute-start.4 = (bf16[128,1536]{1,0:T(8,128)(2,1)}, bf16[128,1536]{1,0:T(8,128)(2,1)}, u32[]{:S(2)}, u32[]{:S(2)}) collective-permute-start(bf16[128,1536]{1,0:T(8,128)(2,1)} %broadcast_select_fusion.4), channel_id=1, source_target_pairs={{0,4},{4,0},{8,12},{12,8},{16,20},{20,16},{24,28},{28,24},{1,5},{5... | collective-permute-start | bytes 1179656 | tf_op jit(solution)/shard_map/ffn_x/ppermute | solution.py:48
  37.2 5.7 %collective-permute-done.2 = bf16[1,128,1024]{2,1,0:T(8,128)(2,1)S(1)} collective-permute-done((bf16[1,128,1024]{2,1,0:T(8,128)(2,1)S(1)}, bf16[1,128,1024]{2,1,0:T(8,128)(2,1)S(1)}, u32[]{:S(2)}, u32[]{:S(2)}) %collective-permute-start.2) | collective-permute-done | bytes 262176 | tf_op jit(solution)/shard_map/tokens_z/ppermute | solution.py:45
  45.2 11.7 %collective-permute-done.3 = bf16[2,128,1024]{2,1,0:T(8,128)(2,1)S(1)} collective-permute-done((bf16[2,128,1024]{2,1,0:T(8,128)(2,1)S(1)}, bf16[2,128,1024]{2,1,0:T(8,128)(2,1)S(1)}, u32[]{:S(2)}, u32[]{:S(2)}) %collective-permute-start.3) | collective-permute-done | bytes 524320 | tf_op jit(solution)/shard_map/tokens_z/ppermute | solution.py:45
  60.2 5.0 %collective-permute-done.8 = bf16[1,272,384]{2,1,0:T(8,128)(2,1)S(1)} collective-permute-done((bf16[1,272,384]{2,1,0:T(8,128)(2,1)S(1)}, bf16[1,272,384]{2,1,0:T(8,128)(2,1)S(1)}, u32[]{:S(2)}, u32[]{:S(2)}) %collective-permute-start.8) | collective-permute-done | bytes 208928 | tf_op jit(solution)/shard_map/qkv_xy/ppermute | solution.py:48
  66.9 7.6 %collective-permute-done.18 = bf16[1,256,1024]{2,1,0:T(8,128)(2,1)S(1)} collective-permute-done((bf16[1,256,1024]{2,1,0:T(8,128)(2,1)S(1)}, bf16[1,256,1024]{2,1,0:T(8,128)(2,1)S(1)}, u32[]{:S(2)}, u32[]{:S(2)}) %collective-permute-start.18) | collective-permute-done | bytes 524320 | tf_op jit(solution)/shard_map/cotangent_x/ppermute | solution.py:48
  79.0 19.1 %collective-permute-done.19 = bf16[1,2,256,1024]{3,2,1,0:T(8,128)(2,1)} collective-permute-done((bf16[1,2,256,1024]{3,2,1,0:T(8,128)(2,1)S(1)}, bf16[1,2,256,1024]{3,2,1,0:T(8,128)(2,1)}, u32[]{:S(2)}, u32[]{:S(2)}) %collective-permute-start.19) | collective-permute-done | bytes 1048608 | tf_op jit(solution)/shard_map/cotangent_y/ppermute | solution.py:57
  99.9 9.0 %shard_map.205 = (bf16[2,1024,128]{2,1,0:T(8,128)(2,1)S(1)}, bf16[2,1024,128]{2,1,0:T(8,128)(2,1)S(1)}, bf16[2,1024,128]{2,1,0:T(8,128)(2,1)S(1)}, bf16[1024,128]{1,0:T(8,128)(2,1)S(1)}) custom-call(f32[2,2]{1,0:T(2,128)S(1)} %pad_maximum_fusion.33.bias_ref, bf16[512,1024]{1,0:T(8,128)(2,1)S(1)} %bitcast.365, ...), custom_call_target="tpu_custom_call" | custom-call | flops 1048576 | bytes 1024 | tf_op jit(solution)/shard_map/pallas_call | solution.py:273
  118.6 5.9 %collective-permute-done.11 = bf16[2,128,128]{2,1,0:T(8,128)(2,1)S(1)} collective-permute-done((bf16[2,128,128]{2,1,0:T(8,128)(2,1)S(1)}, bf16[2,128,128]{2,1,0:T(8,128)(2,1)S(1)}, u32[]{:S(2)}, u32[]{:S(2)}) %collective-permute-start.11) | collective-permute-done | bytes 65568 | tf_op jit(solution)/shard_map/attended_z/ppermute | solution.py:45
  132.4 5.4 %collective-permute-start.21 = (bf16[128,1024]{1,0:T(8,128)(2,1)S(1)}, bf16[128,1024]{1,0:T(8,128)(2,1)S(1)}, u32[]{:S(2)}, u32[]{:S(2)}) collective-permute-start(bf16[128,1024]{1,0:T(8,128)(2,1)S(1)} %multiply_convert_fusion), channel_id=1, source_target_pairs={{0,4},{4,0},{8,12},{12,8},{16,20},{20,16},{24,28},{28,24},{1,5},{5... | collective-permute-start | bytes 786440 | tf_op jit(solution)/shard_map/normed_xy/ppermute | solution.py:48
  139.3 5.6 %collective-permute-done.21 = bf16[128,1024]{1,0:T(8,128)(2,1)S(1)} collective-permute-done((bf16[128,1024]{1,0:T(8,128)(2,1)S(1)}, bf16[128,1024]{1,0:T(8,128)(2,1)S(1)}, u32[]{:S(2)}, u32[]{:S(2)}) %collective-permute-start.21) | collective-permute-done | bytes 262176 | tf_op jit(solution)/shard_map/normed_xy/ppermute | solution.py:48
  145.0 6.3 %collective-permute-done.23 = bf16[128,1024]{1,0:T(8,128)(2,1)S(1)} collective-permute-done((bf16[128,1024]{1,0:T(8,128)(2,1)S(1)}, bf16[128,1024]{1,0:T(8,128)(2,1)S(1)}, u32[]{:S(2)}, u32[]{:S(2)}) %collective-permute-start.23) | collective-permute-done | bytes 262176 | tf_op jit(solution)/shard_map/normed_xy/ppermute | solution.py:60
  154.1 5.6 %shard_map.208 = (bf16[512,512]{1,0:T(8,128)(2,1)S(1)}, bf16[512,1024]{1,0:T(8,128)(2,1)S(1)}, bf16[512,1024]{1,0:T(8,128)(2,1)}, bf16[512,1024]{1,0:T(8,128)(2,1)S(1)}) custom-call(bf16[512,1024]{1,0:T(8,128)(2,1)S(1)} %collective-permute-done.24.tokens_ref.refs_4_, bf16[4,256,1024]{2,1,0:T(8,128)(2,1)} %collective-permute-done.20.grads_ref.refs_5_, ...), custom_call_target="tpu_custom_call" | custom-call | flops 2684354560 | bytes 8388608 | tf_op jit(solution)/shard_map/pallas_call | solution.py:422
  160.9 4.0 %shard_map.207 = (bf16[512,512]{1,0:T(8,128)(2,1)S(1)}, bf16[512,1024]{1,0:T(8,128)(2,1)S(1)}, bf16[512,1024]{1,0:T(8,128)(2,1)S(1)}, bf16[512,1024]{1,0:T(8,128)(2,1)S(1)}) custom-call(bf16[512,1024]{1,0:T(8,128)(2,1)S(1)} %pad_maximum_fusion.3.tokens_ref.refs_0_, bf16[4,256,1024]{2,1,0:T(8,128)(2,1)S(1)} %bitcast.362, bf16[1024,1536]{1,0:T(8,128)(2,1)S(1)} %copy-done.25), custom_call_target="tpu_custom_call" | custom-call | flops 2684354560 | bytes 8388608 | tf_op jit(solution)/shard_map/pallas_call | solution.py:422
  165.9 5.3 %shard_map.209 = bf16[1024,1536]{1,0:T(8,128)(2,1)S(1)} custom-call(bf16[512,1024]{1,0:T(8,128)(2,1)S(1)} %pad_maximum_fusion.3.tokens_ref.refs_0_, bf16[4,256,1024]{2,1,0:T(8,128)(2,1)S(1)} %bitcast.363, bf16[512,512]{1,0:T(8,128)(2,1)S(1)} %get-tuple-element.96.refs_2_, bf16[512,1024]{1,0:T(8,128)(2,1)S(1)} %get-tuple-element.97.refs_3_, ...), custom_call_target="tpu_custom_call" | custom-call | flops 3221225472 | bytes 12582912 | tf_op jit(solution)/shard_map/pallas_call | solution.py:474
  178.6 5.9 %collective-permute-done.26 = bf16[128,1024]{1,0:T(8,128)(2,1)} collective-permute-done((bf16[128,1024]{1,0:T(8,128)(2,1)}, bf16[128,1024]{1,0:T(8,128)(2,1)}, u32[]{:S(2)}, u32[]{:S(2)}) %collective-permute-start.26) | collective-permute-done | bytes 262176 | tf_op jit(solution)/shard_map/up_xy/ppermute | solution.py:48
  184.5 5.7 %collective-permute-done.27 = bf16[128,1024]{1,0:T(8,128)(2,1)} collective-permute-done((bf16[128,1024]{1,0:T(8,128)(2,1)}, bf16[128,1024]{1,0:T(8,128)(2,1)}, u32[]{:S(2)}, u32[]{:S(2)}) %collective-permute-start.27) | collective-permute-done | bytes 262176 | tf_op jit(solution)/shard_map/up_xy/ppermute | solution.py:57
  200.6 3.7 %collective-permute-start.36 = (bf16[4,128,1024]{2,1,0:T(8,128)(2,1)S(1)}, bf16[4,128,1024]{2,1,0:T(8,128)(2,1)S(1)}, u32[]{:S(2)}, u32[]{:S(2)}) collective-permute-start(bf16[4,128,1024]{2,1,0:T(8,128)(2,1)S(1)} %bitcast.389), channel_id=1, source_target_pairs={{0,1},{1,0},{2,3},{3,2},{4,5},{5,4},{6,7},{7,6},{8,9},{9,8},{10,11... | collective-permute-start | bytes 3145736 | tf_op jit(solution)/shard_map/w_out_core/ppermute | solution.py:51
  212.9 5.0 %collective-permute-done.31 = bf16[2,128,128]{2,1,0:T(8,128)(2,1)S(1)} collective-permute-done((bf16[2,128,128]{2,1,0:T(8,128)(2,1)S(1)}, bf16[2,128,128]{2,1,0:T(8,128)(2,1)S(1)}, u32[]{:S(2)}, u32[]{:S(2)}) %collective-permute-start.31) | collective-permute-done | bytes 65568 | tf_op jit(solution)/shard_map/merged_z/ppermute | solution.py:45
  218.9 6.4 %collective-permute-done.35 = bf16[1,2,128,1024]{3,2,1,0:T(8,128)(2,1)S(1)} collective-permute-done((bf16[1,2,128,1024]{3,2,1,0:T(8,128)(2,1)S(1)}, bf16[1,2,128,1024]{3,2,1,0:T(8,128)(2,1)S(1)}, u32[]{:S(2)}, u32[]{:S(2)}) %collective-permute-start.35) | collective-permute-done | bytes 524320 | tf_op jit(solution)/shard_map/down_y/ppermute | solution.py:57
  226.6 11.6 %shard_map.211 = (bf16[512,1024]{1,0:T(8,128)(2,1)}, bf16[512,1024]{1,0:T(8,128)(2,1)}, bf16[1024,384]{1,0:T(8,128)(2,1)S(1)}, f32[2,2]{1,0:T(2,128)S(1)}) custom-call(bf16[2,1024,128]{2,1,0:T(8,128)(2,1)S(1)} %copy-done.20, bf16[2,1024,128]{2,1,0:T(8,128)(2,1)S(1)} %copy-done.22, bf16[2,1024,128]{2,1,0:T(8,128)(2,1)S(1)} %copy-done.24, ...), custom_call_target="tpu_custom_call" | custom-call | flops 1048576 | bytes 1024 | tf_op jit(solution)/shard_map/pallas_call | solution.py:384
  256.0 10.6 %collective-permute-done.39 = bf16[272,896]{1,0:T(8,128)(2,1)S(1)} collective-permute-done((bf16[272,896]{1,0:T(8,128)(2,1)}, bf16[272,896]{1,0:T(8,128)(2,1)S(1)}, u32[]{:S(2)}, u32[]{:S(2)}) %collective-permute-start.39) | collective-permute-done | bytes 487456 | tf_op jit(solution)/shard_map/grad_qkv_xy/ppermute | solution.py:57
  268.9 4.8 %collective-permute-done.47 = bf16[128,1536]{1,0:T(8,128)(2,1)} collective-permute-done((bf16[128,1536]{1,0:T(8,128)(2,1)}, bf16[128,1536]{1,0:T(8,128)(2,1)}, u32[]{:S(2)}, u32[]{:S(2)}) %collective-permute-start.47) | collective-permute-done | bytes 393248 | tf_op jit(solution)/shard_map/grad_ffn_x/ppermute | solution.py:48
  282.8 4.8 %collective-permute-done.43 = bf16[80,896]{1,0:T(8,128)(2,1)S(1)} collective-permute-done((bf16[80,896]{1,0:T(8,128)(2,1)S(1)}, bf16[80,896]{1,0:T(8,128)(2,1)S(1)}, u32[]{:S(2)}, u32[]{:S(2)}) %collective-permute-start.43) | collective-permute-done | bytes 143392 | tf_op jit(solution)/shard_map/grad_qkv_z/ppermute | solution.py:45
  287.6 12.5 %collective-permute-done.44 = bf16[80,896]{1,0:T(8,128)(2,1)S(1)} collective-permute-done((bf16[80,896]{1,0:T(8,128)(2,1)S(1)}, bf16[80,896]{1,0:T(8,128)(2,1)S(1)}, u32[]{:S(2)}, u32[]{:S(2)}) %collective-permute-start.44) | collective-permute-done | bytes 143392 | tf_op jit(solution)/shard_map/grad_qkv_z/ppermute | solution.py:45
  (508 shorter events, 140.1 us)
Async XLA Ops:
  7.2 118.9 %all-gather.2.cloned.1.call-start = ((), (), s32[]{:S(2)}) async-start(), calls=%async_computation.1 | async-start | bytes 3932160 | tf_op jit(solution)/shard_map/all_gather | solution.py:570
  12.9 22.5 %collective-permute-start.16 = (bf16[1,32,1024]{2,1,0:T(8,128)(2,1)S(1)}, bf16[1,32,1024]{2,1,0:T(8,128)(2,1)S(1)}, u32[]{:S(2)}, u32[]{:S(2)}) collective-permute-start(bf16[1,32,1024]{2,1,0:T(8,128)(2,1)S(1)} %bitcast.408), channel_id=1, source_target_pairs={{0,16},{4,20},{8,24},{12,28},{16,0},{20,4},{24,8},{28,12},{1,17},{... | collective-permute-start | bytes 196616 | tf_op jit(solution)/shard_map/out_z/ppermute | solution.py:45
  16.6 13.4 %collective-permute-start.5 = (bf16[80,384]{1,0:T(8,128)(2,1)S(1)}, bf16[80,384]{1,0:T(8,128)(2,1)S(1)}, u32[]{:S(2)}, u32[]{:S(2)}) collective-permute-start(bf16[80,384]{1,0:T(8,128)(2,1)S(1)} %get-tuple-element.281), channel_id=1, source_target_pairs={{0,8},{4,12},{8,0},{12,4},{16,24},{20,28},{24,16},{28,20},{1,9},{5... | collective-permute-start | bytes 184328 | tf_op jit(solution)/shard_map/qkv_z/ppermute | solution.py:45
  22.2 20.9 %collective-permute-start.4 = (bf16[128,1536]{1,0:T(8,128)(2,1)}, bf16[128,1536]{1,0:T(8,128)(2,1)}, u32[]{:S(2)}, u32[]{:S(2)}) collective-permute-start(bf16[128,1536]{1,0:T(8,128)(2,1)} %broadcast_select_fusion.4), channel_id=1, source_target_pairs={{0,4},{4,0},{8,12},{12,8},{16,20},{20,16},{24,28},{28,24},{1,5},{5... | collective-permute-start | bytes 1179656 | tf_op jit(solution)/shard_map/ffn_x/ppermute | solution.py:48
  35.4 23.5 %collective-permute-start.17 = (bf16[2,32,1024]{2,1,0:T(8,128)(2,1)S(1)}, bf16[2,32,1024]{2,1,0:T(8,128)(2,1)}, u32[]{:S(2)}, u32[]{:S(2)}) collective-permute-start(bf16[2,32,1024]{2,1,0:T(8,128)(2,1)S(1)} %pad_maximum_fusion.19), channel_id=1, source_target_pairs={{0,8},{4,12},{8,0},{12,4},{16,24},{20,28},{24,16},{28,20},{1,9},{5... | collective-permute-start | bytes 393224 | tf_op jit(solution)/shard_map/out_z/ppermute | solution.py:45
  43.0 13.9 %collective-permute-start.3 = (bf16[2,128,1024]{2,1,0:T(8,128)(2,1)S(1)}, bf16[2,128,1024]{2,1,0:T(8,128)(2,1)S(1)}, u32[]{:S(2)}, u32[]{:S(2)}) collective-permute-start(bf16[2,128,1024]{2,1,0:T(8,128)(2,1)S(1)} %pad_maximum_fusion.6), channel_id=1, source_target_pairs={{0,8},{4,12},{8,0},{12,4},{16,24},{20,28},{24,16},{28,20},{1,9},{5... | collective-permute-start | bytes 1572872 | tf_op jit(solution)/shard_map/tokens_z/ppermute | solution.py:45
  57.0 181.3 %reduce-scatter.2.cloned.1.call-start = ((), (), s32[]{:S(2)}) async-start(), calls=%async_computation.2 | async-start | bytes 3932160 | tf_op jit(solution)/shard_map/reduce_scatter | solution.py:667
  59.8 14.7 %collective-permute-start.18 = (bf16[1,256,1024]{2,1,0:T(8,128)(2,1)S(1)}, bf16[1,256,1024]{2,1,0:T(8,128)(2,1)S(1)}, u32[]{:S(2)}, u32[]{:S(2)}) collective-permute-start(bf16[1,256,1024]{2,1,0:T(8,128)(2,1)S(1)} %maximum_bitcast_fusion.1), channel_id=1, source_target_pairs={{0,4},{4,0},{8,12},{12,8},{16,20},{20,16},{24,28},{28,24},{1,5},{5... | collective-permute-start | bytes 1572872 | tf_op jit(solution)/shard_map/cotangent_x/ppermute | solution.py:48
  74.6 23.5 %collective-permute-start.19 = (bf16[1,2,256,1024]{3,2,1,0:T(8,128)(2,1)S(1)}, bf16[1,2,256,1024]{3,2,1,0:T(8,128)(2,1)}, u32[]{:S(2)}, u32[]{:S(2)}) collective-permute-start(bf16[1,2,256,1024]{3,2,1,0:T(8,128)(2,1)S(1)} %maximum_bitcast_fusion), channel_id=1, source_target_pairs={{0,2},{1,3},{2,0},{3,1},{4,6},{5,7},{6,4},{7,5},{8,10},{9,11},{10,... | collective-permute-start | bytes 3145736 | tf_op jit(solution)/shard_map/cotangent_y/ppermute | solution.py:57
  78.6 21.3 %collective-permute-start.10 = (bf16[512,1024]{1,0:T(8,128)(2,1)S(1)}, bf16[512,1024]{1,0:T(8,128)(2,1)}, u32[]{:S(2)}, u32[]{:S(2)}) collective-permute-start(bf16[512,1024]{1,0:T(8,128)(2,1)S(1)} %bitcast.364), channel_id=1, source_target_pairs={{0,1},{1,0},{2,3},{3,2},{4,5},{5,4},{6,7},{7,6},{8,9},{9,8},{10,11... | collective-permute-start | bytes 3145736 | tf_op jit(solution)/shard_map/tokens_core/ppermute | solution.py:51
  108.9 20.3 %collective-permute-start.20 = (bf16[4,256,1024]{2,1,0:T(8,128)(2,1)S(1)}, bf16[4,256,1024]{2,1,0:T(8,128)(2,1)}, u32[]{:S(2)}, u32[]{:S(2)}) collective-permute-start(bf16[4,256,1024]{2,1,0:T(8,128)(2,1)S(1)} %bitcast.360), channel_id=1, source_target_pairs={{0,1},{1,0},{2,3},{3,2},{4,5},{5,4},{6,7},{7,6},{8,9},{9,8},{10,11... | collective-permute-start | bytes 6291464 | tf_op jit(solution)/shard_map/cotangent_core/ppermute | solution.py:51
  176.0 14.3 %collective-permute-start.27 = (bf16[128,1024]{1,0:T(8,128)(2,1)}, bf16[128,1024]{1,0:T(8,128)(2,1)}, u32[]{:S(2)}, u32[]{:S(2)}) collective-permute-start(bf16[128,1024]{1,0:T(8,128)(2,1)} %get-tuple-element.193), channel_id=1, source_target_pairs={{0,2},{1,3},{2,0},{3,1},{4,6},{5,7},{6,4},{7,5},{8,10},{9,11},{10,... | collective-permute-start | bytes 786440 | tf_op jit(solution)/shard_map/up_xy/ppermute | solution.py:57
  195.9 15.6 %collective-permute-start.34 = (bf16[512,1024]{1,0:T(8,128)(2,1)S(1)}, bf16[512,1024]{1,0:T(8,128)(2,1)S(1)}, u32[]{:S(2)}, u32[]{:S(2)}) collective-permute-start(bf16[512,1024]{1,0:T(8,128)(2,1)S(1)} %copy-done.27), channel_id=1, source_target_pairs={{0,1},{1,0},{2,3},{3,2},{4,5},{5,4},{6,7},{7,6},{8,9},{9,8},{10,11... | collective-permute-start | bytes 3145736 | tf_op jit(solution)/shard_map/down_core/ppermute | solution.py:51
  200.6 17.8 %collective-permute-start.36 = (bf16[4,128,1024]{2,1,0:T(8,128)(2,1)S(1)}, bf16[4,128,1024]{2,1,0:T(8,128)(2,1)S(1)}, u32[]{:S(2)}, u32[]{:S(2)}) collective-permute-start(bf16[4,128,1024]{2,1,0:T(8,128)(2,1)S(1)} %bitcast.389), channel_id=1, source_target_pairs={{0,1},{1,0},{2,3},{3,2},{4,5},{5,4},{6,7},{7,6},{8,9},{9,8},{10,11... | collective-permute-start | bytes 3145736 | tf_op jit(solution)/shard_map/w_out_core/ppermute | solution.py:51
  240.5 14.1 %collective-permute-start.38 = (bf16[272,896]{1,0:T(8,128)(2,1)}, bf16[272,896]{1,0:T(8,128)(2,1)S(1)}, u32[]{:S(2)}, u32[]{:S(2)}) collective-permute-start(bf16[272,896]{1,0:T(8,128)(2,1)} %fusion.25), channel_id=1, source_target_pairs={{0,4},{4,0},{8,12},{12,8},{16,20},{20,16},{24,28},{28,24},{1,5},{5... | collective-permute-start | bytes 1462280 | tf_op jit(solution)/shard_map/grad_qkv_xy/ppermute | solution.py:48
  242.7 23.9 %collective-permute-start.39 = (bf16[272,896]{1,0:T(8,128)(2,1)}, bf16[272,896]{1,0:T(8,128)(2,1)S(1)}, u32[]{:S(2)}, u32[]{:S(2)}) collective-permute-start(bf16[272,896]{1,0:T(8,128)(2,1)} %fusion.28), channel_id=1, source_target_pairs={{0,2},{1,3},{2,0},{3,1},{4,6},{5,7},{6,4},{7,5},{8,10},{9,11},{10,... | collective-permute-start | bytes 1462280 | tf_op jit(solution)/shard_map/grad_qkv_xy/ppermute | solution.py:57
  244.2 22.4 %collective-permute-start.40 = (bf16[272,896]{1,0:T(8,128)(2,1)}, bf16[272,896]{1,0:T(8,128)(2,1)}, u32[]{:S(2)}, u32[]{:S(2)}) collective-permute-start(bf16[272,896]{1,0:T(8,128)(2,1)} %fusion.31), channel_id=1, source_target_pairs={{0,6},{1,7},{2,4},{3,5},{4,2},{5,3},{6,0},{7,1},{8,14},{9,15},{10,... | collective-permute-start | bytes 1462280 | tf_op jit(solution)/shard_map/grad_qkv_xy/ppermute | solution.py:60
  248.2 27.6 %collective-permute-start.42 = (bf16[2,128,1024]{2,1,0:T(8,128)(2,1)}, bf16[2,128,1024]{2,1,0:T(8,128)(2,1)}, u32[]{:S(2)}, u32[]{:S(2)}) collective-permute-start(bf16[2,128,1024]{2,1,0:T(8,128)(2,1)} %bitcast.107), channel_id=1, source_target_pairs={{0,8},{4,12},{8,0},{12,4},{16,24},{20,28},{24,16},{28,20},{1,9},{5... | collective-permute-start | bytes 1572872 | tf_op jit(solution)/shard_map/input_z/ppermute | solution.py:45
  249.1 24.5 %collective-permute-start.47 = (bf16[128,1536]{1,0:T(8,128)(2,1)}, bf16[128,1536]{1,0:T(8,128)(2,1)}, u32[]{:S(2)}, u32[]{:S(2)}) collective-permute-start(bf16[128,1536]{1,0:T(8,128)(2,1)} %broadcast_select_fusion.1), channel_id=1, source_target_pairs={{0,4},{4,0},{8,12},{12,8},{16,20},{20,16},{24,28},{28,24},{1,5},{5... | collective-permute-start | bytes 1179656 | tf_op jit(solution)/shard_map/grad_ffn_x/ppermute | solution.py:48
  254.6 67.7 %collective-permute-start.37 = (bf16[1,128,1024]{2,1,0:T(8,128)(2,1)}, bf16[1,128,1024]{2,1,0:T(8,128)(2,1)}, u32[]{:S(2)}, u32[]{:S(2)}) collective-permute-start(bf16[1,128,1024]{2,1,0:T(8,128)(2,1)} %slice.803), channel_id=1, source_target_pairs={{0,4},{4,0},{8,12},{12,8},{16,20},{20,16},{24,28},{28,24},{1,5},{5... | collective-permute-start | bytes 786440 | tf_op jit(solution)/shard_map/down_x/ppermute | solution.py:48
  277.3 26.9 %collective-permute-start.46 = (bf16[1,128,1024]{2,1,0:T(8,128)(2,1)S(1)}, bf16[1,128,1024]{2,1,0:T(8,128)(2,1)S(1)}, u32[]{:S(2)}, u32[]{:S(2)}) collective-permute-start(bf16[1,128,1024]{2,1,0:T(8,128)(2,1)S(1)} %slice.802), channel_id=1, source_target_pairs={{0,16},{4,20},{8,24},{12,28},{16,0},{20,4},{24,8},{28,12},{1,17},{... | collective-permute-start | bytes 786440 | tf_op jit(solution)/shard_map/input_z/ppermute | solution.py:45
  279.2 21.0 %collective-permute-start.44 = (bf16[80,896]{1,0:T(8,128)(2,1)S(1)}, bf16[80,896]{1,0:T(8,128)(2,1)S(1)}, u32[]{:S(2)}, u32[]{:S(2)}) collective-permute-start(bf16[80,896]{1,0:T(8,128)(2,1)S(1)} %fusion.53), channel_id=1, source_target_pairs={{0,16},{4,20},{8,24},{12,28},{16,0},{20,4},{24,8},{28,12},{1,17},{... | collective-permute-start | bytes 430088 | tf_op jit(solution)/shard_map/grad_qkv_z/ppermute | solution.py:45
  280.9 19.3 %collective-permute-start.45 = (bf16[80,896]{1,0:T(8,128)(2,1)S(1)}, bf16[80,896]{1,0:T(8,128)(2,1)S(1)}, u32[]{:S(2)}, u32[]{:S(2)}) collective-permute-start(bf16[80,896]{1,0:T(8,128)(2,1)S(1)} %fusion.55), channel_id=1, source_target_pairs={{0,24},{4,28},{8,16},{12,20},{16,8},{20,12},{24,0},{28,4},{1,25},{... | collective-permute-start | bytes 430088 | tf_op jit(solution)/shard_map/grad_qkv_z/ppermute | solution.py:45
  306.4 14.7 %collective-permute-start.48 = (bf16[128,1024]{1,0:T(8,128)(2,1)}, bf16[128,1024]{1,0:T(8,128)(2,1)}, u32[]{:S(2)}, u32[]{:S(2)}) collective-permute-start(bf16[128,1024]{1,0:T(8,128)(2,1)} %add_bitcast_fusion.1), channel_id=1, source_target_pairs={{0,0},{1,4},{2,2},{3,6},{4,1},{5,5},{6,3},{7,7},{8,8},{9,12},{10,1... | collective-permute-start | bytes 786440 | tf_op jit(solution)/shard_map/input_turn/ppermute | solution.py:71
  (98 other events, 1019.6 us)
Sparse Core Ops, SparseCore 0:
  57.1 68.6 all-gather.1
  173.0 62.2 reduce-scatter.1

commit v3 on v2

--- a/solution.py
+++ b/solution.py
@@ -16,6 +16,9 @@
 wide = jnp.float32
 lanes = 128
 half_lanes = 64
+attend_flops = 2**20
+attend_grad_flops = 4 * 10**9
+final_flops = 3 * 10**9
 
 
 def dot(a, b):
@@ -105,11 +108,12 @@
             held = jnp.concatenate([held, move(held)], axis=0)
         return held
 
-    def scatter_steps(self, held, moves):
+    def scatter_steps(self, addends, moves):
         for move in reversed(moves):
-            cut = held.shape[0] // 2
-            held = held[:cut].astype(wide) + move(held[cut:].astype(low)).astype(wide)
-        return held[0]
+            cut = addends[0].shape[0] // 2
+            received = move(total([value[cut:] for value in addends]).astype(low))
+            addends = [value[:cut] for value in addends] + [received]
+        return addends
 
     def xy_moves(self):
         steps = [1 << i for i in range(self.y_size.bit_length() - 1)]
@@ -129,6 +133,10 @@
 def called(name, move, *operands):
     with jax.named_scope(name):
         return move(*operands)
+
+
+def total(addends):
+    return functools.reduce(jnp.add, [value.astype(wide) for value in addends])
 
 
 def tied(*values):
@@ -186,6 +194,11 @@
     return jnp.where(first, pltpu.roll(value, lanes - 32, 1), pltpu.roll(value, 32, 1))
 
 
+def column_of(row):
+    wide_row = jnp.broadcast_to(row.astype(wide), (8, row.shape[1]))
+    return jnp.transpose(wide_row)[:, :1].astype(jnp.int32)
+
+
 def three_pieces(value):
     one = value.astype(low).astype(wide)
     rest = value - one
@@ -202,14 +215,15 @@
     cosine_ref,
     sine_ref,
     kinds_ref,
-    docs_col_ref,
-    docs_row_ref,
+    docs_ref,
     query_ref,
     key_ref,
     value_ref,
     out_ref,
+    docs_column_ref,
 ):
     rows = near_ref.shape[0]
+    docs_column_ref[...] = column_of(docs_ref[...])
     length = 2 * rows
     step = min(rows, 256)
     padded = w_ref.shape[1] // 3
@@ -219,7 +233,7 @@
             packed = dot(source[start : start + step, :], w_ref[...])
             cosine, sine = cosine_ref[at, :], sine_ref[at, :]
             lane = lane_ids(step)
-            kind = kinds_ref[at, :1]
+            kind = column_of(kinds_ref[:, at])
             own = (lane == 64 + kind).astype(wide)
             own_two = (lane == 68 + kind).astype(wide)
             extra_query = ((lane == 72 + kind) | (lane == 76)).astype(wide)
@@ -245,7 +259,7 @@
     @pl.loop(0, length // block)
     def _(i):
         at = pl.ds(pl.multiple_of(i * block, block), block)
-        allowed = docs_col_ref[at, :1] == docs_row_ref[...]
+        allowed = docs_column_ref[at, :] == docs_ref[...]
         done = []
         for head in range(heads):
             query = query_ref[head, at, :]
@@ -273,16 +287,51 @@
     return pl.pallas_call(
         functools.partial(attend_kernel, heads),
         out_shape=(whole, whole, whole, jax.ShapeDtypeStruct((length, padded), low)),
-        in_specs=[pl.BlockSpec(memory_space=pltpu.SMEM)] + [vmem] * 8,
+        in_specs=[pl.BlockSpec(memory_space=pltpu.SMEM)] + [vmem] * 7,
         out_specs=(vmem, vmem, vmem, vmem),
+        scratch_shapes=[pltpu.VMEM((length, 1), jnp.int32)],
         compiler_params=pltpu.CompilerParams(vmem_limit_bytes=48 * 2**20),
         cost_estimate=pl.CostEstimate(
-            flops=2**20, bytes_accessed=2**10, transcendentals=0
+            flops=attend_flops, bytes_accessed=2**20, transcendentals=0
         ),
     )(bias, near, far, w, cosine, sine, *ids)
 
 
 def attend_grad_kernel(
+    heads,
+    masks,
+    *refs,
+):
+    if masks:
+        place_ref, near_ref, far_ref, extra_ref, *refs = refs
+        *refs, messages_ref, total_ref = refs
+    attend_grad_body(heads, *refs)
+    if not masks:
+        return
+    packed_ref, bias_ref = refs[12:14]
+    half, width = near_ref.shape
+    share = (messages_ref.shape[1] - 16) // len(masks[0])
+    for start in range(0, width, 256):
+        here = slice(start, start + 256)
+        grads = t_dot(near_ref[:, here], packed_ref[:half, :]) + t_dot(far_ref[:, here], packed_ref[half:, :])
+        total_ref[here, :] = grads.astype(low)
+    columns = packed_ref.shape[1]
+    row = lax.broadcasted_iota(jnp.int32, (16, columns), 0)
+    lane = lax.broadcasted_iota(jnp.int32, (16, columns), 1)
+    biases = jnp.zeros((16, columns), wide)
+    for head in range(heads):
+        for i in range(2):
+            biases = jnp.where(lane == 2 * head + i, bias_ref[head, i], biases)
+    high = biases.astype(low).astype(wide)
+    biases = jnp.where(row == 0, high, jnp.where(row == 1, biases - high, 0.0))
+    for i, part in enumerate(masks):
+        for j, mask in enumerate(part):
+            start = pl.multiple_of(jnp.bitwise_xor(place_ref[0], mask) * share, share)
+            messages_ref[i, j * share : (j + 1) * share, :] = total_ref[pl.ds(start, share), :]
+        messages_ref[i, len(part) * share :, :] = (extra_ref[i].astype(wide) + biases).astype(low)
+
+
+def attend_grad_body(
     heads,
     query_ref,
     key_ref,
@@ -292,21 +341,19 @@
     cosine_ref,
     sine_ref,
     kinds_ref,
-    docs_col_ref,
-    docs_row_ref,
-    near_ref,
-    far_ref,
+    docs_ref,
     w_ref,
     near_up_ref,
     far_up_ref,
-    grad_w_ref,
+    packed_ref,
     bias_ref,
     grad_query_ref,
     grad_key_ref,
     grad_value_ref,
-    packed_ref,
+    docs_column_ref,
 ):
     length = query_ref.shape[1]
+    docs_column_ref[...] = column_of(docs_ref[...])
     padded = packed_ref.shape[1] // 3
     half = length // 2
     block = min(length, 256)
@@ -317,7 +364,7 @@
     @pl.loop(0, length // block)
     def _(i):
         at = pl.ds(pl.multiple_of(i * block, block), block)
-        allowed = docs_col_ref[:, :1] == docs_row_ref[:, at]
+        allowed = docs_column_ref[...] == docs_ref[:, at]
         for head in range(heads):
             columns = slice(head // 2 * lanes, (head // 2 + 1) * lanes)
             grad_out = grad_out_ref[at, columns].astype(wide)
@@ -361,13 +408,8 @@
         here = slice(start, start + block)
         far_up_ref[here, :] = dot_t(packed_ref[half + start : half + start + block, :], w_ref[...]).astype(low)
         near_up_ref[here, :] = dot_t(packed_ref[here, :], w_ref[...]).astype(low)
-    width = near_ref.shape[1]
-    for start in range(0, width, 256):
-        here = slice(start, start + 256)
-        grads = t_dot(near_ref[:, here], packed_ref[:half, :]) + t_dot(far_ref[:, here], packed_ref[half:, :])
-        grad_w_ref[here, :] = grads.astype(low)
     every = lane_ids(length)
-    kinds = kinds_ref[:, :1]
+    kinds = column_of(kinds_ref[...])
     for head in range(heads):
         grads = grad_key_ref[head]
         same = jnp.sum(jnp.where(every == 72 + kinds, grads, 0.0))
@@ -376,27 +418,42 @@
         bias_ref[head, 1] = total - same
 
 
-def attend_grad(query, key, value, out, grad_out, cosine, sine, ids, near, far, w):
+def attend_grad(query, key, value, out, grad_out, cosine, sine, ids, w, near, far, extra, place, masks):
     heads, length, _ = query.shape
-    half, width = near.shape
-    vmem = pl.BlockSpec(memory_space=pltpu.VMEM)
-    scratch = pltpu.VMEM((heads, length, lanes), wide)
+    half, width = length // 2, w.shape[0]
+    vmem, smem = pl.BlockSpec(memory_space=pltpu.VMEM), pl.BlockSpec(memory_space=pltpu.SMEM)
+    columns = w.shape[1]
+    out_shape = [
+        jax.ShapeDtypeStruct((half, width), low),
+        jax.ShapeDtypeStruct((half, width), low),
+        jax.ShapeDtypeStruct((length, columns), low),
+        jax.ShapeDtypeStruct((heads, 2), wide),
+    ]
+    scratch = [pltpu.VMEM((heads, length, lanes), wide)] * 3 + [pltpu.VMEM((length, 1), jnp.int32)]
+    in_specs, out_specs = [vmem] * 10, [vmem] * 3 + [smem]
+    operands = [query, key, value, out, grad_out, cosine, sine, *ids, w]
+    kernel = functools.partial(attend_grad_kernel, heads, masks)
+    if masks:
+        share = width // sum(map(len, masks))
+        in_specs = [smem, vmem, vmem, vmem] + in_specs
+        operands = [place.reshape(1).astype(jnp.int32), near, far, extra] + operands
+        out_shape.append(jax.ShapeDtypeStruct((len(masks), len(masks[0]) * share + 16, columns), low))
+        out_specs = out_specs + [vmem]
+        scratch = scratch + [pltpu.VMEM((width, columns), low)]
+
+        def kernel(*refs):
+            before, messages, after = refs[: len(in_specs) + 4], refs[len(in_specs) + 4], refs[len(in_specs) + 5 :]
+            attend_grad_kernel(heads, masks, *before, *after[:-1], messages, after[-1])
+
     return pl.pallas_call(
-        functools.partial(attend_grad_kernel, heads),
-        out_shape=(
-            jax.ShapeDtypeStruct((half, width), low),
-            jax.ShapeDtypeStruct((half, width), low),
-            jax.ShapeDtypeStruct(w.shape, low),
-            jax.ShapeDtypeStruct((heads, 2), wide),
-        ),
-        in_specs=[vmem] * 13,
-        out_specs=(vmem, vmem, vmem, pl.BlockSpec(memory_space=pltpu.SMEM)),
-        scratch_shapes=[scratch] * 3 + [pltpu.VMEM((length, w.shape[1]), low)],
+        kernel,
+        out_shape=out_shape,
+        in_specs=in_specs,
+        out_specs=out_specs,
+        scratch_shapes=scratch,
         compiler_params=pltpu.CompilerParams(vmem_limit_bytes=48 * 2**20),
-        cost_estimate=pl.CostEstimate(flops=2**20, bytes_accessed=2**10, transcendentals=0),
-    )(
-        query, key, value, out, grad_out, cosine, sine, *ids, near, far, w
-    )
+        cost_estimate=pl.CostEstimate(flops=attend_grad_flops, bytes_accessed=2**10, transcendentals=0),
+    )(*operands)
 
 
 def feed_kernel(units, tokens_ref, grads_ref, w_ref, hidden_ref, grad_units_ref, up_ref, down_ref):
@@ -439,7 +496,7 @@
             pl.BlockSpec((step, width), lambda i: (i, 0)),
             pl.BlockSpec((step, width), lambda i: (i, 0)),
         ),
-        compiler_params=pltpu.CompilerParams(vmem_limit_bytes=32 * 2**20),
+        compiler_params=pltpu.CompilerParams(vmem_limit_bytes=58 * 2**20),
         cost_estimate=pl.CostEstimate(
             flops=10 * count * width * units, bytes_accessed=8 * 2**20, transcendentals=count * units
         ),
@@ -477,11 +534,92 @@
         out_shape=jax.ShapeDtypeStruct((width, 3 * units), low),
         in_specs=part + part,
         out_specs=pl.BlockSpec((step, 3 * units), lambda i: (i, 0)),
-        compiler_params=pltpu.CompilerParams(vmem_limit_bytes=32 * 2**20),
+        compiler_params=pltpu.CompilerParams(vmem_limit_bytes=58 * 2**20),
         cost_estimate=pl.CostEstimate(
             flops=12 * count * width * units, bytes_accessed=12 * 2**20, transcendentals=0
         ),
     )(*near, *far)
+
+
+def finish_input_kernel(tokens_ref, upstream_ref, grads_ref, out_ref):
+    tokens = tokens_ref[...].astype(wide)
+    upstream = upstream_ref[...].astype(wide)
+    inverse = lax.rsqrt(jnp.mean(tokens * tokens, axis=-1, keepdims=True) + epsilon)
+    unit = tokens * inverse
+    mean = jnp.mean(upstream * unit, axis=-1, keepdims=True)
+    out_ref[...] = (grads_ref[...] + inverse * (upstream - unit * mean)).astype(low)
+
+
+def finish_input(tokens, upstream, grads):
+    return pl.pallas_call(
+        finish_input_kernel,
+        out_shape=jax.ShapeDtypeStruct(tokens.shape, low),
+        cost_estimate=pl.CostEstimate(flops=final_flops, bytes_accessed=2**20, transcendentals=0),
+    )(tokens, upstream, grads)
+
+
+def finish_qkv_kernel(group_ref, grads_ref, w_ref, gain_ref, out_ref, gain_out_ref):
+    share = w_ref.shape[0]
+    low_half = lane_ids(share) < half_lanes
+    gain = gain_ref[...].astype(wide)
+    total = jnp.zeros((share, lanes), wide)
+    for i in range(grads_ref.shape[0]):
+        query, key, value = (grads_ref[i, :, j * lanes : (j + 1) * lanes].astype(wide) for j in range(3))
+        key = pltpu.roll(key, half_lanes, 1)
+        start = jnp.bitwise_xor(group_ref[0], i) * (3 * lanes)
+        parts = (
+            jnp.where(low_half, query, key),
+            jnp.where(low_half, value, query),
+            jnp.where(low_half, key, value),
+        )
+        for j, part in enumerate(parts):
+            at = pl.ds(pl.multiple_of(start + j * lanes, lanes), lanes)
+            total += part * w_ref[:, at].astype(wide)
+            out_ref[:, at] = part * gain
+    column = jnp.broadcast_to(jnp.sum(total, axis=1, keepdims=True), (share, lanes))
+    gain_out_ref[...] = jnp.transpose(column)[:1, :]
+
+
+def finish_qkv(group, grads, w, gain):
+    vmem = pl.BlockSpec(memory_space=pltpu.VMEM)
+    return pl.pallas_call(
+        finish_qkv_kernel,
+        out_shape=(
+            jax.ShapeDtypeStruct(w.shape, wide),
+            jax.ShapeDtypeStruct((1, w.shape[0]), wide),
+        ),
+        in_specs=[pl.BlockSpec(memory_space=pltpu.SMEM)] + [vmem] * 3,
+        out_specs=(vmem, vmem),
+        cost_estimate=pl.CostEstimate(flops=final_flops, bytes_accessed=2**20, transcendentals=0),
+    )(group.reshape(1).astype(jnp.int32), grads, w, gain)
+
+
+def finish_feed_kernel(x_ref, mine_ref, other_ref, gate_ref, up_ref, down_ref):
+    units = mine_ref.shape[1] // 3
+    for ref, x in ((mine_ref, x_ref[0]), (other_ref, 1 - x_ref[0])):
+        at = pl.ds(pl.multiple_of(x * units, units), units)
+        parts = [ref[:, j * units : (j + 1) * units].astype(wide) for j in range(3)]
+        gate_ref[:, at], up_ref[:, at] = parts[:2]
+        if down_ref.shape[0] == 2 * units:
+            down_ref[at, :] = jnp.transpose(parts[2])
+        else:
+            down_ref[:, at] = parts[2]
+
+
+def finish_feed(x, mine, other):
+    vmem = pl.BlockSpec(memory_space=pltpu.VMEM)
+    depth, units = mine.shape[0], mine.shape[1] // 3
+    return pl.pallas_call(
+        finish_feed_kernel,
+        out_shape=(
+            jax.ShapeDtypeStruct((depth, 2 * units), wide),
+            jax.ShapeDtypeStruct((depth, 2 * units), wide),
+            jax.ShapeDtypeStruct((2 * units, depth) if depth % lanes == 0 else (depth, 2 * units), wide),
+        ),
+        in_specs=[pl.BlockSpec(memory_space=pltpu.SMEM), vmem, vmem],
+        out_specs=(vmem,) * 3,
+        cost_estimate=pl.CostEstimate(flops=final_flops, bytes_accessed=2**20, transcendentals=0),
+    )(x.reshape(1).astype(jnp.int32), mine, other)
 
 
 def rope_tables(stamps, dimension):
@@ -528,14 +666,6 @@
     turned = called("tokens_turn", at.turn, unit.astype(low))
 
     depth, units = w_gate.shape[0], w_gate.shape[1] // 2
-    turned, late_gate, late_up, late_down = tied(turned, w_gate, w_up, w_down)
-    down_t = with_layout_constraint(late_down.T, Layout(major_to_minor=(0, 1)))
-    firsts = jnp.concatenate([v[:, :units] for v in (late_gate, late_up, down_t)], axis=1)
-    seconds = jnp.concatenate([v[:, units:] for v in (late_gate, late_up, down_t)], axis=1)
-    mine = pick(at.x, firsts, seconds)
-    other = called("ffn_x", at.along_x, pick(at.x, seconds, firsts))
-    z_block = jnp.concatenate([pick(at.x, mine, other), pick(at.x, other, mine)], axis=0)
-
     gain_one = gain_attn.astype(wide)[:, None]
     scaled = (w_qkv.astype(wide) * gain_one).astype(low)
 
@@ -555,7 +685,7 @@
 
     core_got = called("qkv_core", at.along_c, with_extra(core_sent, gain_ffn))
     both = jnp.stack([core_own, core_got[:-16].reshape(core_own.shape)])
-    both, turned, w_out_early = tied(both, turned, w_out)
+    out_z = called("out_z", at.gather_steps, w_out, at.z_moves()).reshape(-1, width)
     gains = jnp.concatenate([gain_ffn, core_got[-16, :share]])
     sent = []
     for d in range(z_size):
@@ -564,11 +694,9 @@
     by_z = jnp.stack(called("qkv_z", at.scatter_z, sent))
     gains = by_z[:, -16, : 2 * share].reshape(-1)
     by_z = by_z[:, :-16].reshape(-1, 3 * padded)
-    out_z = called("out_z", at.gather_steps, w_out_early, at.z_moves()).reshape(-1, width)
+    turned, by_z, out_z = tied(turned, by_z, out_z)
     near = called("tokens_z", at.gather_steps, turned, at.z_moves()).reshape(-1, width)
-    near, z_block = tied(near, z_block)
-    w_ffn = lax.all_gather(z_block, "seq", axis=0, tiled=True, axis_index_groups=at.columns_z())
-    by_xy = called("qkv_xy", at.gather_steps, with_extra(by_z, gains), at.xy_moves())
+    by_xy = jnp.stack(called("qkv_xy", at.gather_xy, with_extra(by_z, gains)))
     gains = by_xy[:, -16, : gains.shape[0]].reshape(y_size, 2, z_size, 2, share)
     gains = gains.transpose(2, 1, 0, 3, 4).reshape(-1, share)
     by_xy = by_xy[:, :-16]
@@ -583,6 +711,22 @@
     ]
     w_heads = place(by_xy.reshape(-1, share, 3 * padded), device_id, masks).reshape(width, 3 * padded)
 
+    w_heads, late_gate, late_up, late_down = tied(w_heads, w_gate, w_up, w_down)
+    units = w_gate.shape[1] // 2
+    down_t = with_layout_constraint(late_down.T, Layout(major_to_minor=(0, 1)))
+    firsts = jnp.concatenate([v[:, :units] for v in (late_gate, late_up, down_t)], axis=1)
+    seconds = jnp.concatenate([v[:, units:] for v in (late_gate, late_up, down_t)], axis=1)
+    mine = pick(at.x, firsts, seconds)
+    other = called("ffn_x", at.along_x, pick(at.x, seconds, firsts))
+    z_block = jnp.concatenate([pick(at.x, mine, other), pick(at.x, other, mine)], axis=0)
+
+    grad_out = cotangent[0]
+    xy_rows = jnp.concatenate([grad_out, out_z], axis=0)
+    xy_rows = called("cotangent_x", at.gather_steps, xy_rows, at.xy_moves()[:1])
+
+    near, z_block, w_heads, xy_rows = tied(near, z_block, w_heads, xy_rows)
+    w_ffn = lax.all_gather(z_block, "seq", axis=0, tiled=True, axis_index_groups=at.columns_z())
+
     time_ids, variate_ids, seq_ids, by_z = tied(time_ids, variate_ids, seq_ids, by_z)
 
     def of_window(ids):
@@ -596,29 +740,23 @@
         ]
         return jnp.concatenate(order)
 
-    docs = of_window(seq_ids)
-    docs_columns = jnp.broadcast_to(docs[:, None], (docs.shape[0], lanes))
-    kinds = jnp.broadcast_to(of_window(variate_ids)[:, None], docs_columns.shape)
+    ids = (of_window(variate_ids).reshape(1, -1), of_window(seq_ids).reshape(1, -1))
     cosine, sine = rope_tables(of_window(time_ids), head_dim)
     local_bias = lax.dynamic_slice_in_dim(head_bias, group * heads, heads, 0)
     difference = local_bias[:, 0] - local_bias[:, 1]
     difference_high = difference.astype(low).astype(wide)
     bias = jnp.stack([difference_high, difference - difference_high])
 
-    grad_out = cotangent[0]
-    xy_rows = jnp.concatenate([grad_out, out_z], axis=0)
-    xy_rows = called("cotangent_x", at.gather_steps, xy_rows, at.xy_moves()[:1])
-
-    near, w_heads, cosine, sine, kinds, docs, docs_columns = tied(
-        near, w_heads, cosine, sine, kinds, docs, docs_columns
-    )
-    ids = (kinds, docs_columns, docs.reshape(1, -1))
-    xy_rows = called("cotangent_y", at.gather_steps, xy_rows, at.xy_moves()[1:])
-    xy_rows = xy_rows.reshape(2 * y_size, -1, width)
+    near, w_heads, cosine, sine, ids = tied(near, w_heads, cosine, sine, ids)
     far = called("tokens_core", at.along_c, near)
     query, key, value, attended = attend(bias, near, far, w_heads, cosine, sine, ids, heads)
 
-    xy_rows, query = tied(xy_rows, query)
+    held = xy_rows[None]
+    for move in at.xy_moves()[1:]:
+        received = called("cotangent_y", move, held)
+        received, query = tied(received, query)
+        held = jnp.concatenate([held, received], axis=0)
+    xy_rows = held.reshape(2 * y_size, -1, width)
     xy_rows_far = called("cotangent_core", at.along_c, xy_rows)
     out_blocks = jnp.stack([xy_rows[:, rows:], xy_rows_far[:, rows:]]).reshape(-1, share, width)
     out_masks = [
@@ -636,7 +774,6 @@
     kept = jnp.concatenate([block[0] for block in received], axis=1)
     passed = jnp.concatenate([block[1] for block in received], axis=1)
     passed = called("attended_core", at.along_c, passed)
-    passed, w_ffn = tied(passed, w_ffn)
     merged = called("attended_turn", at.turn, jnp.concatenate([kept, passed], axis=1))
 
     middle = tokens + dot(merged, out_rows)
@@ -646,22 +783,21 @@
     normed_near = jnp.concatenate(called("normed_xy", at.gather_xy, normed_two), axis=0)
     normed_far = called("normed_core", at.along_c, normed_near)
 
+    hidden_far, units_far, up_far, down_far = feed(normed_far, xy_rows_far, w_ffn)
     hidden_near, units_near, up_near, down_near = feed(normed_near, xy_rows, w_ffn)
-    hidden_far, units_far, up_far, down_far = feed(normed_far, xy_rows_far, w_ffn)
-
-    units_far, up_far = tied(units_far, up_far)
+
     grad_w_ffn = feed_grad(
         (normed_near, xy_rows, hidden_near, units_near),
         (normed_far, xy_rows_far, hidden_far, units_far),
     )
-    up_far = called("up_core", at.along_c, up_far)
-    up_far, grad_w_ffn = tied(up_far, grad_w_ffn)
-    kept = [
-        up_near[i * rows : (i + 1) * rows].astype(wide) + up_far[i * rows : (i + 1) * rows].astype(wide)
-        for i in range(2 * y_size)
-    ]
-    received = called("up_xy", at.scatter_xy, kept[:1] + [block.astype(low) for block in kept[1:]])
-    grad_two = functools.reduce(jnp.add, [block.astype(wide) for block in received])
+    blocks = (2 * y_size, rows, width)
+    up = up_near.reshape(blocks), called("up_core", at.along_c, up_far).reshape(blocks)
+    received = called(
+        "up_xy", at.scatter_xy, [total([part[i] for part in up]).astype(low) for i in range(2 * y_size)]
+    )
+    down = [down_near.reshape(blocks), called("down_core", at.along_c, down_far).reshape(blocks)]
+    received[0], down[1] = tied(received[0], down[1])
+    grad_two = total(received)
     gain_part = jnp.sum(grad_two * unit_two, axis=0)
     upstream = grad_two * gain_two
     grad_w_ffn = lax.psum_scatter(
@@ -689,79 +825,93 @@
     if padded > group_width:
         grad_attended = jnp.pad(grad_attended, ((0, 0), (0, padded - group_width)))
 
-    down_far, grad_branch = tied(down_far, grad_branch)
-    down = down_near.astype(wide) + called("down_core", at.along_c, down_far).astype(wide)
-    down = down.reshape(y_size, 2, rows, width)
-    down = called("down_y", at.scatter_steps, down, at.xy_moves()[1:])
+    moves = at.xy_moves()
+    down[1], grad_branch = tied(down[1], grad_branch)
+    down = called("down_y", at.scatter_steps, [part.reshape(y_size, 2, rows, width) for part in down], moves[1:])
 
     merged, grad_branch, turned_back = tied(merged, grad_branch, turned_back)
     grad_out_rows = t_dot(merged, grad_branch).astype(low)
     grad_out_rows = fetch(grad_out_rows.reshape(-1, share, width), at.head, out_masks)
-    grad_out_rows = grad_out_rows.reshape(2, 2 * y_size, z_size * share, width)
-    grad_out_far = called("w_out_core", at.along_c, grad_out_rows[1])
-    grad_out_rows = (grad_out_rows[0].astype(wide) + grad_out_far.astype(wide)).astype(low)
-
-    grad_attended, down, grad_out_rows = tied(grad_attended, down, grad_out_rows)
-    output = middle + called("down_x", at.scatter_steps, down, at.xy_moves()[:1])
-    upstream_near, upstream_far, grad_heads, bias_grad = attend_grad(
-        query, key, value, attended, grad_attended, cosine, sine, ids, near, far, w_heads
-    )
-
-    upstream_far, grad_w_ffn = tied(upstream_far, grad_w_ffn)
-    upstream_far = called("input_core", at.along_c, upstream_far)
-    upstream_near = upstream_near.astype(wide) + upstream_far.astype(wide)
-    z_moves = at.z_moves()
-    upstream_z = upstream_near.reshape(z_size, rows, width)
-    cut = z_size // 2
-    upstream_z = upstream_z[:cut] + called("input_z", z_moves[-1], upstream_z[cut:].astype(low)).astype(wide)
-
-    grad_heads = grad_heads.reshape(z_size, 2, y_size, 2, share, 3 * padded)
+    grad_out_rows = grad_out_rows.reshape(2, y_size, 2, z_size * share, width)
+    out_parts = [grad_out_rows[0], called("w_out_core", at.along_c, grad_out_rows[1])]
+    y_cut = y_size // 2
+    out_sent = total([part[y_cut:] for part in out_parts]).astype(low)
+    grad_attended, out_sent, down[-1] = tied(grad_attended, out_sent, down[-1])
+    out_parts = [part[:y_cut] for part in out_parts] + [called("w_out_y", moves[-1], out_sent)]
+    out_parts = called("w_out_y", at.scatter_steps, out_parts, moves[1:-1])
 
     def halves(values):
         high = values.astype(low)
         return high, (values - high.astype(wide)).astype(low)
 
+    gain_part = gain_part.reshape(z_size, 2, y_size, 2, share)
+    bias_count, gain_count = 2 * heads, 2 * z_size * share
+    extra, device_masks = [], []
+    for dx, dy in at.pairs():
+        x, y = jnp.bitwise_xor(at.x, dx), jnp.bitwise_xor(at.y, dy)
+        gain = lax.dynamic_slice(gain_part, (0, x, y, 0, 0), (z_size, 1, 1, 2, share)).reshape(-1)
+        none = jnp.zeros((0, 3 * padded), low)
+        extra.append(with_extra(none, *(jnp.zeros_like(v) for v in halves(gain)), *halves(gain)))
+        device_masks.append([
+            (2 * d + dx) * at.head_size + 2 * dy + e for d in range(z_size) for e in range(2)
+        ])
+    extra = jnp.stack(extra)
+    place_xy = at.x * at.head_size + 2 * at.y
+    in_kernel = share % 16 == 0
+    upstream_near, upstream_far, grad_packed, bias_grad, *messages = attend_grad(
+        query, key, value, attended, grad_attended, cosine, sine, ids, w_heads,
+        near, far, extra, place_xy, device_masks if in_kernel else None,
+    )
+    half = near.shape[0]
+    if in_kernel:
+        messages = [messages[0][i] for i in range(2 * y_size)]
+    else:
+        grad_heads = t_dot(near, grad_packed[:half]) + t_dot(far, grad_packed[half:])
+        grad_heads = grad_heads.astype(low).reshape(-1, share, 3 * padded)
+        none = jnp.zeros((0, 3 * padded), low)
+        biases = with_extra(none, *halves(bias_grad.reshape(-1)))
+        messages = [
+            jnp.concatenate([
+                lax.dynamic_index_in_dim(grad_heads, jnp.bitwise_xor(place_xy, mask), 0, False)
+                for mask in masks
+            ] + [extra[i] + biases])
+            for i, masks in enumerate(device_masks)
+        ]
+
+    upstream_far = called("input_core", at.along_c, upstream_far)
+    z_moves = at.z_moves()
+    blocks = (z_size, rows, width)
+    upstream_z = [upstream_near.reshape(blocks), upstream_far.reshape(blocks)]
+    upstream_z = called("input_z", at.scatter_steps, upstream_z, z_moves[-1:])
+
     def joined(block, row, count):
         return block[row, :count].astype(wide) + block[row + 1, :count].astype(wide)
 
-    gain_part = gain_part.reshape(z_size, 2, y_size, 2, share)
-    bias_count, gain_count = 2 * heads, 2 * z_size * share
-
-    grad_out_rows = grad_out_rows.reshape(2 * y_size, z_size, share, 2, width // 2)
-    grad_out_rows = grad_out_rows.transpose(0, 1, 3, 2, 4).reshape(2 * y_size, -1, width // 2)
-
-    def rows_of(index, dx, dy):
-        x, y = jnp.bitwise_xor(at.x, dx), jnp.bitwise_xor(at.y, dy)
-        picked = lax.dynamic_slice(
-            grad_heads, (0, x, y, 0, 0, 0), (z_size, 1, 1, 2, share, 3 * padded)
-        )
-        gain = lax.dynamic_slice(gain_part, (0, x, y, 0, 0), (z_size, 1, 1, 2, share)).reshape(-1)
-        block = with_extra(picked.reshape(-1, 3 * padded), *halves(bias_grad.reshape(-1)), *halves(gain))
-        return jnp.concatenate([block, jnp.pad(grad_out_rows[index], ((0, 16), (0, 0)))], axis=1)
-
-    received = called("grad_qkv_xy", at.scatter_xy, [rows_of(i, *d) for i, d in enumerate(at.pairs())])
+    received = called("grad_qkv_xy", at.scatter_xy, messages)
     summed = functools.reduce(jnp.add, [block.astype(wide) for block in received])
-    summed, upstream_z = tied(summed, upstream_z)
-    upstream_one = called("input_z", at.scatter_steps, upstream_z, z_moves[:-1])
+    depth = grad_w_ffn.shape[0] // 2
+    mine = pick(at.x, grad_w_ffn[:depth], grad_w_ffn[depth:])
+    other = called("grad_ffn_x", at.along_x, pick(at.x, grad_w_ffn[depth:], grad_w_ffn[:depth]))
+    summed, upstream_z[-1], other, down[-1], out_parts[-1] = tied(
+        summed, upstream_z[-1], other, down[-1], out_parts[-1]
+    )
+    upstream_one = total(called("input_z", at.scatter_steps, upstream_z, z_moves[:-1]))[0]
+    down = [part.reshape(2, rows, width) for part in down]
+    output = middle + total(called("down_x", at.scatter_steps, down, moves[:1]))[0]
+    out_parts = called("w_out_x", at.scatter_steps, [part.reshape(2, -1, width) for part in out_parts], moves[:1])
+    out_parts = [part.reshape(z_size, share, width) for part in out_parts]
+    grad_w_out = total(called("w_out_z", at.scatter_steps, out_parts, z_moves))[0]
     bias_sum = joined(summed[-16:], 0, bias_count)
     gain_sum = joined(summed[-16:], 2, gain_count).reshape(z_size, 2 * share)
-    out_sum = summed[:-16, 3 * padded :].astype(low).reshape(z_size, 2 * share, width // 2)
-    summed = summed[:-16, : 3 * padded].astype(low).reshape(z_size, 2 * share, 3 * padded)
+    summed = summed[:-16].astype(low).reshape(z_size, 2 * share, 3 * padded)
     sent = []
     for d in range(z_size):
         block, gain = (
             lax.dynamic_index_in_dim(v, jnp.bitwise_xor(at.z, d), axis=0, keepdims=False)
             for v in (summed, gain_sum)
         )
-        block = with_extra(block, *halves(bias_sum), *halves(gain))
-        out_block = jnp.pad(out_sum[places[d]], ((0, 16), (0, 0)))
-        sent.append(jnp.concatenate([block, out_block], axis=1))
+        sent.append(with_extra(block, *halves(bias_sum), *halves(gain)))
     received = called("grad_qkv_z", at.scatter_z, sent)
-    grad_w_out = functools.reduce(
-        jnp.add, [block[:-16, 3 * padded :].astype(wide) for block in received]
-    )
-    grad_w_out = grad_w_out.reshape(2, share, width // 2).transpose(1, 0, 2).reshape(share, width)
-    received = [block[:, : 3 * padded] for block in received]
     bias_z = jnp.concatenate([joined(block[-16:], 0, bias_count) for block in received])
     gain_sum = functools.reduce(jnp.add, [joined(block[-16:], 2, 2 * share) for block in received])
     received = jnp.stack([block[:-16] for block in received]).reshape(z_size, 2, share, 3 * padded)
@@ -770,14 +920,11 @@
     gain_own = pick(at.c, gain_sum[:share], gain_sum[share:])
     gain_sent = pick(at.c, gain_sum[share:], gain_sum[:share])
     core_sent, upstream_one = tied(core_sent, upstream_one)
-    mine = pick(at.x, grad_w_ffn[:depth], grad_w_ffn[depth:]).astype(wide)
-    other = pick(at.x, grad_w_ffn[depth:], grad_w_ffn[:depth])
-    other = called("grad_ffn_x", at.along_x, other).astype(wide)
-    upstream_one, other = tied(upstream_one.astype(low), other)
-    upstream_one = called("input_turn", at.turn, upstream_one).astype(wide)
-    grad_input = grad_middle + inverse_one * (
-        upstream_one - unit * jnp.mean(upstream_one * unit, axis=-1, keepdims=True)
-    )
+    grad_w_gate, grad_w_up, grad_w_down = finish_feed(at.x, mine, other)
+    if grad_w_down.shape != w_down.shape:
+        grad_w_down = grad_w_down.T
+    upstream_one = called("input_turn", at.turn, upstream_one.astype(low))
+    grad_input = finish_input(inputs[0], upstream_one, grad_middle)
     core_got = called(
         "grad_qkv_core", at.along_c, with_extra(core_sent, *halves(bias_z), *halves(gain_sent))
     )
@@ -787,19 +934,19 @@
     biases = list(biases.reshape(2, z_size, heads, 2).transpose(1, 0, 2, 3).reshape(groups, heads, 2))
     full_bias = jnp.concatenate(xor_list(biases, group), axis=0)
     by_group = jnp.stack([core_own, core_other], axis=1).reshape(groups, share, 3 * padded)
-    by_group = place(by_group, group, list(range(groups))).astype(wide).reshape(groups, share, 3, padded)
-    by_group = by_group[..., :group_width].reshape(groups, share, 3, heads, head_dim)
-    raw = by_group.transpose(1, 0, 3, 2, 4).reshape(share, 3 * width)
-    grad_w_qkv = raw * gain_one
-    grad_gain_attn = jnp.sum(raw * w_qkv.astype(wide), axis=1)
-    first, second = pick(at.x, mine, other), pick(at.x, other, mine)
-    grad_w_gate, grad_w_up, grad_w_down_t = (
-        jnp.concatenate([first[:, i * units : (i + 1) * units], second[:, i * units : (i + 1) * units]], axis=1)
-        for i in range(3)
-    )
+    if heads == 2 and head_dim == half_lanes:
+        grad_w_qkv, grad_gain_attn = finish_qkv(group, by_group, w_qkv, gain_attn[:, None])
+        grad_gain_attn = grad_gain_attn[0]
+    else:
+        by_group = place(by_group, group, list(range(groups))).astype(wide).reshape(groups, share, 3, padded)
+        by_group = by_group[..., :group_width].reshape(groups, share, 3, heads, head_dim)
+        raw = by_group.transpose(1, 0, 3, 2, 4).reshape(share, 3 * width)
+        grad_w_qkv = raw * gain_one
+        grad_gain_attn = jnp.sum(raw * w_qkv.astype(wide), axis=1)
+
     return (
         output.astype(low).reshape(1, rows, width),
-        grad_input.astype(low).reshape(1, rows, width),
+        grad_input.reshape(1, rows, width),
         grad_gain_attn,
         grad_w_qkv,
         full_bias,
@@ -807,7 +954,7 @@
         grad_gain_ffn,
         grad_w_gate,
         grad_w_up,
-        grad_w_down_t.T,
+        grad_w_down,
     )
 
 

time: 334 us -> 297 us (0.89)
  waiting for transfers between devices: 136 us -> 85.6 us
  Pallas kernels: 35.9 us -> 49 us
  local copies, waits for them, and re-layouts: 31.2 us -> 22.5 us
  starting transfers between devices: 69.7 us -> 77.2 us
  other arithmetic: 38.5 us -> 43.3 us
    ppermute x8 -> x9, waiting for transfers between devices: 31.3 us -> 14.2 us  [along_x(): lax.ppermute(value, 'seq', [(i, i ^ 1) for i in range(self.seq_size)])]
    ppermute x6 -> x7, waiting for transfers between devices: 41.8 us -> 25.4 us  [along_xy(): lax.ppermute(value, 'head', [(i, i ^ 2 * dy) for i in range(self.head_siz...]
    ppermute x18 -> x20, waiting for transfers between devices: 51 us -> 36.7 us  [along_z(): lax.ppermute(value, 'seq', [(i, i ^ 2 * step) for i in range(self.seq_siz...]
    ppermute x18 -> x20, starting transfers between devices: 24.5 us -> 36.2 us  [along_z(): lax.ppermute(value, 'seq', [(i, i ^ 2 * step) for i in range(self.seq_siz...]
    convert_element_type x3 -> x9, other arithmetic: 4.53 us -> 13.6 us  [the longest x7 10.2 us: scatter_steps(): received = move(total([value[cut:] for value in addends]).astype(low))]
    pallas_call x1 -> x4, Pallas kernels: 11.6 us -> 18.1 us  [the longest x1 11.5 us: attend_grad(): pl.pallas_call(kernel, out_shape=out_shape, in_specs=in_specs, out_specs=...]
    reshape x11 -> x4, local copies, waits for them, and re-layouts: 5.84 us -> 0.33 us  [shards(): lax.dynamic_slice(gain_part, (0, x, y, 0, 0), (z_size, 1, 1, 2, share))]
    unnamed x164 -> x110, local copies, waits for them, and re-layouts: 9.75 us -> 4.73 us
  transfers between devices with their start and end apart: 52 -> 57, of which waited for: 24 -> 26; matrix products, arithmetic and copies ran while one was open for 18% -> 20% of each run, Pallas kernels for 9% -> 13%
where the time goes in v3:
time: 297 us; the launch traced here: 296 us
  waiting for transfers between devices  85.6 us (29%)
  starting transfers between devices  77.2 us (26%)
  Pallas kernels  49 us (16%)
  other arithmetic  43.3 us (15%)
  local copies, waits for them, and re-layouts  22.5 us (8%)
  between operations  15.8 us (5%)
    ppermute x20, waiting for transfers between devices, along_z(): lax.ppermute(value, 'seq', [(i, i ^ 2 * step) for i in range(self.seq_siz...  36.7 us
    ppermute x20, starting transfers between devices, along_z(): lax.ppermute(value, 'seq', [(i, i ^ 2 * step) for i in range(self.seq_siz...  36.2 us
    ppermute x7, waiting for transfers between devices, along_xy(): lax.ppermute(value, 'head', [(i, i ^ 2 * dy) for i in range(self.head_siz...  25.4 us
    ppermute x9, starting transfers between devices, along_x(): lax.ppermute(value, 'seq', [(i, i ^ 1) for i in range(self.seq_size)])  16.4 us
    ppermute x9, waiting for transfers between devices, along_x(): lax.ppermute(value, 'seq', [(i, i ^ 1) for i in range(self.seq_size)])  14.2 us
    pallas_call x2, Pallas kernels, feed(): pl.pallas_call(functools.partial(feed_kernel, units), grid=(count // step...  13.9 us
    pallas_call x1, Pallas kernels, attend_grad(): pl.pallas_call(kernel, out_shape=out_shape, in_specs=in_specs, out_specs=...  11.5 us
    convert_element_type x7, other arithmetic, scatter_steps(): received = move(total([value[cut:] for value in addends]).astype(low))  10.2 us
  transfers between devices with their start and end apart: 57, of which 26 were waited for; matrix products, arithmetic and copies ran while one was open for 20% of the time, Pallas kernels for 13%

profile of v3, /device:TPU:0, one launch (start us, length us, event | category | flops | bytes accessed | tf_op | source)
XLA Modules:
  0.0 295.8 jit_solution(12902364533604668065)
XLA Ops:
  10.8 3.7 %collective-permute-start.5 = (bf16[1,32,1024]{2,1,0:T(8,128)(2,1)S(1)}, bf16[1,32,1024]{2,1,0:T(8,128)(2,1)S(1)}, u32[]{:S(2)}, u32[]{:S(2)}) collective-permute-start(bf16[1,32,1024]{2,1,0:T(8,128)(2,1)S(1)} %bitcast.471), channel_id=1, source_target_pairs={{0,16},{4,20},{8,24},{12,28},{16,0},{20,4},{24,8},{28,12},{1,17},{... | collective-permute-start | bytes 196616 | tf_op jit(solution)/shard_map/out_z/ppermute | solution.py:48
  19.7 3.4 %collective-permute-start.3 = (bf16[80,384]{1,0:T(8,128)(2,1)S(1)}, bf16[80,384]{1,0:T(8,128)(2,1)S(1)}, u32[]{:S(2)}, u32[]{:S(2)}) collective-permute-start(bf16[80,384]{1,0:T(8,128)(2,1)S(1)} %get-tuple-element.256), channel_id=1, source_target_pairs={{0,16},{4,20},{8,24},{12,28},{16,0},{20,4},{24,8},{28,12},{1,17},{... | collective-permute-start | bytes 184328 | tf_op jit(solution)/shard_map/qkv_z/ppermute | solution.py:48
  25.9 3.4 %collective-permute-done.4 = bf16[80,384]{1,0:T(8,128)(2,1)S(1)} collective-permute-done((bf16[80,384]{1,0:T(8,128)(2,1)S(1)}, bf16[80,384]{1,0:T(8,128)(2,1)S(1)}, u32[]{:S(2)}, u32[]{:S(2)}) %collective-permute-start.4) | collective-permute-done | bytes 61472 | tf_op jit(solution)/shard_map/qkv_z/ppermute | solution.py:48
  39.8 3.2 %collective-permute-done.11 = bf16[272,384]{1,0:T(8,128)(2,1)S(1)} collective-permute-done((bf16[272,384]{1,0:T(8,128)(2,1)S(1)}, bf16[272,384]{1,0:T(8,128)(2,1)S(1)}, u32[]{:S(2)}, u32[]{:S(2)}) %collective-permute-start.11) | collective-permute-done | bytes 208928 | tf_op jit(solution)/shard_map/qkv_xy/ppermute | solution.py:63
  55.5 4.0 %collective-permute-done.12 = bf16[128,1536]{1,0:T(8,128)(2,1)S(1)} collective-permute-done((bf16[128,1536]{1,0:T(8,128)(2,1)S(1)}, bf16[128,1536]{1,0:T(8,128)(2,1)S(1)}, u32[]{:S(2)}, u32[]{:S(2)}) %collective-permute-start.12) | collective-permute-done | bytes 393248 | tf_op jit(solution)/shard_map/ffn_x/ppermute | solution.py:51
  60.7 3.9 %collective-permute-done.8 = bf16[2,128,1024]{2,1,0:T(8,128)(2,1)} collective-permute-done((bf16[2,128,1024]{2,1,0:T(8,128)(2,1)}, bf16[2,128,1024]{2,1,0:T(8,128)(2,1)}, u32[]{:S(2)}, u32[]{:S(2)}) %collective-permute-start.8) | collective-permute-done | bytes 524320 | tf_op jit(solution)/shard_map/tokens_z/ppermute | solution.py:48
  68.9 9.0 %shard_map.205 = (bf16[2,1024,128]{2,1,0:T(8,128)(2,1)S(1)}, bf16[2,1024,128]{2,1,0:T(8,128)(2,1)S(1)}, bf16[2,1024,128]{2,1,0:T(8,128)(2,1)S(1)}, bf16[1024,128]{1,0:T(8,128)(2,1)S(1)}) custom-call(f32[2,2]{1,0:T(2,128)S(1)} %pad_maximum_fusion.31.bias_ref, bf16[512,1024]{1,0:T(8,128)(2,1)S(1)} %bitcast.430, ...), custom_call_target="tpu_custom_call" | custom-call | flops 1048576 | bytes 1048576 | tf_op jit(solution)/shard_map/pallas_call | solution.py:287
  77.9 14.0 %collective-permute-done.20 = bf16[1,2,256,1024]{3,2,1,0:T(8,128)(2,1)} collective-permute-done((bf16[1,2,256,1024]{3,2,1,0:T(8,128)(2,1)}, bf16[1,2,256,1024]{3,2,1,0:T(8,128)(2,1)}, u32[]{:S(2)}, u32[]{:S(2)}) %collective-permute-start.20) | collective-permute-done | bytes 1048608 | tf_op jit(solution)/shard_map/cotangent_y/ppermute | solution.py:60
  98.0 3.7 %collective-permute-done.17 = bf16[2,128,128]{2,1,0:T(8,128)(2,1)S(1)} collective-permute-done((bf16[2,128,128]{2,1,0:T(8,128)(2,1)S(1)}, bf16[2,128,128]{2,1,0:T(8,128)(2,1)S(1)}, u32[]{:S(2)}, u32[]{:S(2)}) %collective-permute-start.17) | collective-permute-done | bytes 65568 | tf_op jit(solution)/shard_map/attended_z/ppermute | solution.py:48
  101.7 3.4 %collective-permute-done.16 = bf16[2,128,128]{2,1,0:T(8,128)(2,1)S(1)} collective-permute-done((bf16[2,128,128]{2,1,0:T(8,128)(2,1)S(1)}, bf16[2,128,128]{2,1,0:T(8,128)(2,1)S(1)}, u32[]{:S(2)}, u32[]{:S(2)}) %collective-permute-start.16) | collective-permute-done | bytes 65568 | tf_op jit(solution)/shard_map/attended_z/ppermute | solution.py:48
  105.1 4.2 %collective-permute-done.15 = bf16[2,128,128]{2,1,0:T(8,128)(2,1)S(1)} collective-permute-done((bf16[2,128,128]{2,1,0:T(8,128)(2,1)S(1)}, bf16[2,128,128]{2,1,0:T(8,128)(2,1)S(1)}, u32[]{:S(2)}, u32[]{:S(2)}) %collective-permute-start.15) | collective-permute-done | bytes 65568 | tf_op jit(solution)/shard_map/attended_z/ppermute | solution.py:48
  114.6 5.2 %collective-permute-start.22 = (bf16[128,1024]{1,0:T(8,128)(2,1)S(1)}, bf16[128,1024]{1,0:T(8,128)(2,1)S(1)}, u32[]{:S(2)}, u32[]{:S(2)}) collective-permute-start(bf16[128,1024]{1,0:T(8,128)(2,1)S(1)} %multiply_convert_fusion), channel_id=1, source_target_pairs={{0,4},{4,0},{8,12},{12,8},{16,20},{20,16},{24,28},{28,24},{1,5},{5... | collective-permute-start | bytes 786440 | tf_op jit(solution)/shard_map/normed_xy/ppermute | solution.py:51
  121.4 5.1 %collective-permute-done.22 = bf16[128,1024]{1,0:T(8,128)(2,1)S(1)} collective-permute-done((bf16[128,1024]{1,0:T(8,128)(2,1)S(1)}, bf16[128,1024]{1,0:T(8,128)(2,1)S(1)}, u32[]{:S(2)}, u32[]{:S(2)}) %collective-permute-start.22) | collective-permute-done | bytes 262176 | tf_op jit(solution)/shard_map/normed_xy/ppermute | solution.py:51
  126.5 6.2 %collective-permute-done.23 = bf16[128,1024]{1,0:T(8,128)(2,1)S(1)} collective-permute-done((bf16[128,1024]{1,0:T(8,128)(2,1)S(1)}, bf16[128,1024]{1,0:T(8,128)(2,1)S(1)}, u32[]{:S(2)}, u32[]{:S(2)}) %collective-permute-start.23) | collective-permute-done | bytes 262176 | tf_op jit(solution)/shard_map/normed_xy/ppermute | solution.py:60
  137.3 6.9 %shard_map.208 = (bf16[512,512]{1,0:T(8,128)(2,1)}, bf16[512,1024]{1,0:T(8,128)(2,1)}, bf16[512,1024]{1,0:T(8,128)(2,1)}, bf16[512,1024]{1,0:T(8,128)(2,1)}) custom-call(bf16[512,1024]{1,0:T(8,128)(2,1)} %collective-permute-done.25.tokens_ref.refs_4_, bf16[4,256,1024]{2,1,0:T(8,128)(2,1)} %copy-done.20, bf16[1024,1536]{1,0:T(8,128)(2,1)} %all-gather.2.cloned.1.call-done.w_ref), custom_call_target="tpu_custom_call" | custom-call | flops 2684354560 | bytes 8388608 | tf_op jit(solution)/shard_map/pallas_call | solution.py:479
  144.7 6.9 %shard_map.207 = (bf16[512,512]{1,0:T(8,128)(2,1)}, bf16[512,1024]{1,0:T(8,128)(2,1)}, bf16[512,1024]{1,0:T(8,128)(2,1)}, bf16[512,1024]{1,0:T(8,128)(2,1)}) custom-call(bf16[512,1024]{1,0:T(8,128)(2,1)} %copy-done.21, bf16[4,256,1024]{2,1,0:T(8,128)(2,1)} %bitcast.445, bf16[1024,1536]{1,0:T(8,128)(2,1)} %all-gather.2.cloned.1.call-done.w_ref), custom_call_target="tpu_custom_call" | custom-call | flops 2684354560 | bytes 8388608 | tf_op jit(solution)/shard_map/pallas_call | solution.py:479
  157.5 7.7 %shard_map.211 = bf16[1024,1536]{1,0:T(8,128)(2,1)} custom-call(bf16[512,1024]{1,0:T(8,128)(2,1)} %copy-done.21, bf16[4,256,1024]{2,1,0:T(8,128)(2,1)} %bitcast.446, bf16[512,512]{1,0:T(8,128)(2,1)} %get-tuple-element.108.refs_2_, bf16[512,1024]{1,0:T(8,128)(2,1)} %get-tuple-element.109.refs_3_, ...), custom_call_target="tpu_custom_call" | custom-call | flops 3221225472 | bytes 12582912 | tf_op jit(solution)/shard_map/pallas_call | solution.py:531
  180.2 5.9 %collective-permute-start.36 = (bf16[2,2,128,1024]{3,2,1,0:T(8,128)(2,1)S(1)}, bf16[2,2,128,1024]{3,2,1,0:T(8,128)(2,1)S(1)}, u32[]{:S(2)}, u32[]{:S(2)}) collective-permute-start(bf16[2,2,128,1024]{3,2,1,0:T(8,128)(2,1)S(1)} %bitcast.453), channel_id=1, source_target_pairs={{0,1},{1,0},{2,3},{3,2},{4,5},{5,4},{6,7},{7,6},{8,9},{9,8},{10,11... | collective-permute-start | bytes 3145736 | tf_op jit(solution)/shard_map/w_out_core/ppermute | solution.py:54
  193.4 4.7 %collective-permute-done.33 = bf16[2,128,128]{2,1,0:T(8,128)(2,1)S(1)} collective-permute-done((bf16[2,128,128]{2,1,0:T(8,128)(2,1)S(1)}, bf16[2,128,128]{2,1,0:T(8,128)(2,1)S(1)}, u32[]{:S(2)}, u32[]{:S(2)}) %collective-permute-start.33) | collective-permute-done | bytes 65568 | tf_op jit(solution)/shard_map/merged_z/ppermute | solution.py:48
  202.1 11.5 %shard_map.210 = (bf16[512,1024]{1,0:T(8,128)(2,1)}, bf16[512,1024]{1,0:T(8,128)(2,1)}, bf16[1024,384]{1,0:T(8,128)(2,1)}, f32[2,2]{1,0:T(2,128)}, bf16[4,272,384]{2,1,0:T(8,128)(2,1)S(1)}) custom-call(s32[1]{0:T(128)} %bitcast.80.refs_0_, bf16[512,1024]{1,0:T(8,128)(2,1)} %bitcast.431, bf16[512,1024]{1,0:T(8,128)(2,1)} %collective-permute-done.14.far_ref.refs_2_, ...), custom_call_target="tpu_custom_call" | custom-call | flops 4000000000 | bytes 1024 | tf_op jit(solution)/shard_map/pallas_call | solution.py:448
  220.7 7.2 %collective-permute-start.42 = (bf16[2,128,1024]{2,1,0:T(8,128)(2,1)S(1)}, bf16[2,128,1024]{2,1,0:T(8,128)(2,1)}, u32[]{:S(2)}, u32[]{:S(2)}) collective-permute-start(bf16[2,128,1024]{2,1,0:T(8,128)(2,1)S(1)} %bitcast.465), channel_id=1, source_target_pairs={{0,8},{4,12},{8,0},{12,4},{16,24},{20,28},{24,16},{28,20},{1,9},{5... | collective-permute-start | bytes 1572872 | tf_op jit(solution)/shard_map/input_z/ppermute | solution.py:48
  236.1 3.3 %collective-permute-done.44 = bf16[1,2,128,1024]{3,2,1,0:T(8,128)(2,1)} collective-permute-done((bf16[1,2,128,1024]{3,2,1,0:T(8,128)(2,1)}, bf16[1,2,128,1024]{3,2,1,0:T(8,128)(2,1)}, u32[]{:S(2)}, u32[]{:S(2)}) %collective-permute-start.44) | collective-permute-done | bytes 524320 | tf_op jit(solution)/shard_map/w_out_y/ppermute | solution.py:60
  242.5 3.5 %collective-permute-start.46 = (bf16[80,384]{1,0:T(8,128)(2,1)S(1)}, bf16[80,384]{1,0:T(8,128)(2,1)S(1)}, u32[]{:S(2)}, u32[]{:S(2)}) collective-permute-start(bf16[80,384]{1,0:T(8,128)(2,1)S(1)} %fusion.35), channel_id=1, source_target_pairs={{0,8},{4,12},{8,0},{12,4},{16,24},{20,28},{24,16},{28,20},{1,9},{5... | collective-permute-start | bytes 184328 | tf_op jit(solution)/shard_map/grad_qkv_z/ppermute | solution.py:48
  281.1 4.0 %collective-permute-done.54 = bf16[1,32,1024]{2,1,0:T(8,128)(2,1)S(1)} collective-permute-done((bf16[1,32,1024]{2,1,0:T(8,128)(2,1)S(1)}, bf16[1,32,1024]{2,1,0:T(8,128)(2,1)S(1)}, u32[]{:S(2)}, u32[]{:S(2)}) %collective-permute-start.54) | collective-permute-done | bytes 65568 | tf_op jit(solution)/shard_map/w_out_z/ppermute | solution.py:48
  (446 shorter events, 146.0 us)
Async XLA Ops:
  7.2 130.0 %all-gather.2.cloned.1.call-start = ((), (), s32[]{:S(2)}) async-start(), calls=%async_computation.1 | async-start | bytes 3932160 | tf_op jit(solution)/shard_map/all_gather | solution.py:728
  14.8 14.8 %collective-permute-start = (bf16[128,1024]{1,0:T(8,128)(2,1)S(1)}, bf16[128,1024]{1,0:T(8,128)(2,1)}, u32[]{:S(2)}, u32[]{:S(2)}) collective-permute-start(bf16[128,1024]{1,0:T(8,128)(2,1)S(1)} %fusion.4), channel_id=1, source_target_pairs={{0,0},{1,4},{2,2},{3,6},{4,1},{5,5},{6,3},{7,7},{8,8},{9,12},{10,1... | collective-permute-start | bytes 786440 | tf_op jit(solution)/shard_map/tokens_turn/ppermute | solution.py:74
  35.1 18.3 %collective-permute-start.13 = (bf16[1,256,1024]{2,1,0:T(8,128)(2,1)S(1)}, bf16[1,256,1024]{2,1,0:T(8,128)(2,1)}, u32[]{:S(2)}, u32[]{:S(2)}) collective-permute-start(bf16[1,256,1024]{2,1,0:T(8,128)(2,1)S(1)} %maximum_bitcast_fusion), channel_id=1, source_target_pairs={{0,4},{4,0},{8,12},{12,8},{16,20},{20,16},{24,28},{28,24},{1,5},{5... | collective-permute-start | bytes 1572872 | tf_op jit(solution)/shard_map/cotangent_x/ppermute | solution.py:51
  45.3 14.3 %collective-permute-start.12 = (bf16[128,1536]{1,0:T(8,128)(2,1)S(1)}, bf16[128,1536]{1,0:T(8,128)(2,1)S(1)}, u32[]{:S(2)}, u32[]{:S(2)}) collective-permute-start(bf16[128,1536]{1,0:T(8,128)(2,1)S(1)} %broadcast_select_fusion.4), channel_id=1, source_target_pairs={{0,4},{4,0},{8,12},{12,8},{16,20},{20,16},{24,28},{28,24},{1,5},{5... | collective-permute-start | bytes 1179656 | tf_op jit(solution)/shard_map/ffn_x/ppermute | solution.py:51
  51.1 13.4 %collective-permute-start.8 = (bf16[2,128,1024]{2,1,0:T(8,128)(2,1)}, bf16[2,128,1024]{2,1,0:T(8,128)(2,1)}, u32[]{:S(2)}, u32[]{:S(2)}) collective-permute-start(bf16[2,128,1024]{2,1,0:T(8,128)(2,1)} %pad_maximum_fusion.7), channel_id=1, source_target_pairs={{0,8},{4,12},{8,0},{12,4},{16,24},{20,28},{24,16},{28,20},{1,9},{5... | collective-permute-start | bytes 1572872 | tf_op jit(solution)/shard_map/tokens_z/ppermute | solution.py:48
  66.0 25.9 %collective-permute-start.20 = (bf16[1,2,256,1024]{3,2,1,0:T(8,128)(2,1)}, bf16[1,2,256,1024]{3,2,1,0:T(8,128)(2,1)}, u32[]{:S(2)}, u32[]{:S(2)}) collective-permute-start(bf16[1,2,256,1024]{3,2,1,0:T(8,128)(2,1)} %bitcast.447), channel_id=1, source_target_pairs={{0,2},{1,3},{2,0},{3,1},{4,6},{5,7},{6,4},{7,5},{8,10},{9,11},{10,... | collective-permute-start | bytes 3145736 | tf_op jit(solution)/shard_map/cotangent_y/ppermute | solution.py:60
  68.8 160.2 %reduce-scatter.2.cloned.1.call-start = ((), (), s32[]{:S(2)}) async-start(), calls=%async_computation.2 | async-start | bytes 3932160 | tf_op jit(solution)/shard_map/reduce_scatter | solution.py:803
  93.3 18.3 %collective-permute-start.21 = (bf16[4,256,1024]{2,1,0:T(8,128)(2,1)S(1)}, bf16[4,256,1024]{2,1,0:T(8,128)(2,1)S(1)}, u32[]{:S(2)}, u32[]{:S(2)}) collective-permute-start(bf16[4,256,1024]{2,1,0:T(8,128)(2,1)S(1)} %bitcast.443), channel_id=1, source_target_pairs={{0,1},{1,0},{2,3},{3,2},{4,5},{5,4},{6,7},{7,6},{8,9},{9,8},{10,11... | collective-permute-start | bytes 6291464 | tf_op jit(solution)/shard_map/cotangent_core/ppermute | solution.py:54
  95.8 13.4 %collective-permute-start.15 = (bf16[2,128,128]{2,1,0:T(8,128)(2,1)S(1)}, bf16[2,128,128]{2,1,0:T(8,128)(2,1)S(1)}, u32[]{:S(2)}, u32[]{:S(2)}) collective-permute-start(bf16[2,128,128]{2,1,0:T(8,128)(2,1)S(1)} %get-tuple-element.197), channel_id=1, source_target_pairs={{0,16},{4,20},{8,24},{12,28},{16,0},{20,4},{24,8},{28,12},{1,17},{... | collective-permute-start | bytes 196616 | tf_op jit(solution)/shard_map/attended_z/ppermute | solution.py:48
  144.6 21.9 %collective-permute-start.27 = (bf16[512,1024]{1,0:T(8,128)(2,1)}, bf16[512,1024]{1,0:T(8,128)(2,1)}, u32[]{:S(2)}, u32[]{:S(2)}) collective-permute-start(bf16[512,1024]{1,0:T(8,128)(2,1)} %get-tuple-element.94), channel_id=1, source_target_pairs={{0,1},{1,0},{2,3},{3,2},{4,5},{5,4},{6,7},{7,6},{8,9},{9,8},{10,11... | collective-permute-start | bytes 3145736 | tf_op jit(solution)/shard_map/down_core/ppermute | solution.py:54
  155.4 13.1 %collective-permute-start.29 = (bf16[128,1024]{1,0:T(8,128)(2,1)}, bf16[128,1024]{1,0:T(8,128)(2,1)}, u32[]{:S(2)}, u32[]{:S(2)}) collective-permute-start(bf16[128,1024]{1,0:T(8,128)(2,1)} %get-tuple-element.182), channel_id=1, source_target_pairs={{0,2},{1,3},{2,0},{3,1},{4,6},{5,7},{6,4},{7,5},{8,10},{9,11},{10,... | collective-permute-start | bytes 786440 | tf_op jit(solution)/shard_map/up_xy/ppermute | solution.py:60
  175.2 26.8 %collective-permute-start.37 = (bf16[1,2,128,1024]{3,2,1,0:T(8,128)(2,1)}, bf16[1,2,128,1024]{3,2,1,0:T(8,128)(2,1)}, u32[]{:S(2)}, u32[]{:S(2)}) collective-permute-start(bf16[1,2,128,1024]{3,2,1,0:T(8,128)(2,1)} %fusion.5), channel_id=1, source_target_pairs={{0,2},{1,3},{2,0},{3,1},{4,6},{5,7},{6,4},{7,5},{8,10},{9,11},{10,... | collective-permute-start | bytes 1572872 | tf_op jit(solution)/shard_map/down_y/ppermute | solution.py:60
  180.2 20.7 %collective-permute-start.36 = (bf16[2,2,128,1024]{3,2,1,0:T(8,128)(2,1)S(1)}, bf16[2,2,128,1024]{3,2,1,0:T(8,128)(2,1)S(1)}, u32[]{:S(2)}, u32[]{:S(2)}) collective-permute-start(bf16[2,2,128,1024]{3,2,1,0:T(8,128)(2,1)S(1)} %bitcast.453), channel_id=1, source_target_pairs={{0,1},{1,0},{2,3},{3,2},{4,5},{5,4},{6,7},{7,6},{8,9},{9,8},{10,11... | collective-permute-start | bytes 3145736 | tf_op jit(solution)/shard_map/w_out_core/ppermute | solution.py:54
  214.6 16.5 %collective-permute-start.38 = (bf16[272,384]{1,0:T(8,128)(2,1)}, bf16[272,384]{1,0:T(8,128)(2,1)}, u32[]{:S(2)}, u32[]{:S(2)}) collective-permute-start(bf16[272,384]{1,0:T(8,128)(2,1)} %get-tuple-element.186), channel_id=1, source_target_pairs={{0,4},{4,0},{8,12},{12,8},{16,20},{20,16},{24,28},{28,24},{1,5},{5... | collective-permute-start | bytes 626696 | tf_op jit(solution)/shard_map/grad_qkv_xy/ppermute | solution.py:51
  216.0 18.8 %collective-permute-start.39 = (bf16[272,384]{1,0:T(8,128)(2,1)}, bf16[272,384]{1,0:T(8,128)(2,1)}, u32[]{:S(2)}, u32[]{:S(2)}) collective-permute-start(bf16[272,384]{1,0:T(8,128)(2,1)} %get-tuple-element.188), channel_id=1, source_target_pairs={{0,2},{1,3},{2,0},{3,1},{4,6},{5,7},{6,4},{7,5},{8,10},{9,11},{10,... | collective-permute-start | bytes 626696 | tf_op jit(solution)/shard_map/grad_qkv_xy/ppermute | solution.py:60
  216.5 18.3 %collective-permute-start.40 = (bf16[272,384]{1,0:T(8,128)(2,1)}, bf16[272,384]{1,0:T(8,128)(2,1)}, u32[]{:S(2)}, u32[]{:S(2)}) collective-permute-start(bf16[272,384]{1,0:T(8,128)(2,1)} %get-tuple-element.187), channel_id=1, source_target_pairs={{0,6},{1,7},{2,4},{3,5},{4,2},{5,3},{6,0},{7,1},{8,14},{9,15},{10,... | collective-permute-start | bytes 626696 | tf_op jit(solution)/shard_map/grad_qkv_xy/ppermute | solution.py:63
  218.1 21.3 %collective-permute-start.44 = (bf16[1,2,128,1024]{3,2,1,0:T(8,128)(2,1)}, bf16[1,2,128,1024]{3,2,1,0:T(8,128)(2,1)}, u32[]{:S(2)}, u32[]{:S(2)}) collective-permute-start(bf16[1,2,128,1024]{3,2,1,0:T(8,128)(2,1)} %fusion.1), channel_id=1, source_target_pairs={{0,2},{1,3},{2,0},{3,1},{4,6},{5,7},{6,4},{7,5},{8,10},{9,11},{10,... | collective-permute-start | bytes 1572872 | tf_op jit(solution)/shard_map/w_out_y/ppermute | solution.py:60
  220.7 18.6 %collective-permute-start.42 = (bf16[2,128,1024]{2,1,0:T(8,128)(2,1)S(1)}, bf16[2,128,1024]{2,1,0:T(8,128)(2,1)}, u32[]{:S(2)}, u32[]{:S(2)}) collective-permute-start(bf16[2,128,1024]{2,1,0:T(8,128)(2,1)S(1)} %bitcast.465), channel_id=1, source_target_pairs={{0,8},{4,12},{8,0},{12,4},{16,24},{20,28},{24,16},{28,20},{1,9},{5... | collective-permute-start | bytes 1572872 | tf_op jit(solution)/shard_map/input_z/ppermute | solution.py:48
  242.5 17.2 %collective-permute-start.46 = (bf16[80,384]{1,0:T(8,128)(2,1)S(1)}, bf16[80,384]{1,0:T(8,128)(2,1)S(1)}, u32[]{:S(2)}, u32[]{:S(2)}) collective-permute-start(bf16[80,384]{1,0:T(8,128)(2,1)S(1)} %fusion.35), channel_id=1, source_target_pairs={{0,8},{4,12},{8,0},{12,4},{16,24},{20,28},{24,16},{28,20},{1,9},{5... | collective-permute-start | bytes 184328 | tf_op jit(solution)/shard_map/grad_qkv_z/ppermute | solution.py:48
  246.1 15.3 %collective-permute-start.47 = (bf16[80,384]{1,0:T(8,128)(2,1)S(1)}, bf16[80,384]{1,0:T(8,128)(2,1)}, u32[]{:S(2)}, u32[]{:S(2)}) collective-permute-start(bf16[80,384]{1,0:T(8,128)(2,1)S(1)} %fusion.36), channel_id=1, source_target_pairs={{0,16},{4,20},{8,24},{12,28},{16,0},{20,4},{24,8},{28,12},{1,17},{... | collective-permute-start | bytes 184328 | tf_op jit(solution)/shard_map/grad_qkv_z/ppermute | solution.py:48
  247.1 14.2 %collective-permute-start.48 = (bf16[80,384]{1,0:T(8,128)(2,1)S(1)}, bf16[80,384]{1,0:T(8,128)(2,1)}, u32[]{:S(2)}, u32[]{:S(2)}) collective-permute-start(bf16[80,384]{1,0:T(8,128)(2,1)S(1)} %fusion.37), channel_id=1, source_target_pairs={{0,24},{4,28},{8,16},{12,20},{16,8},{20,12},{24,0},{28,4},{1,25},{... | collective-permute-start | bytes 184328 | tf_op jit(solution)/shard_map/grad_qkv_z/ppermute | solution.py:48
  249.9 16.4 %collective-permute-start.49 = (bf16[1,128,1024]{2,1,0:T(8,128)(2,1)S(1)}, bf16[1,128,1024]{2,1,0:T(8,128)(2,1)}, u32[]{:S(2)}, u32[]{:S(2)}) collective-permute-start(bf16[1,128,1024]{2,1,0:T(8,128)(2,1)S(1)} %fusion.13), channel_id=1, source_target_pairs={{0,16},{4,20},{8,24},{12,28},{16,0},{20,4},{24,8},{28,12},{1,17},{... | collective-permute-start | bytes 786440 | tf_op jit(solution)/shard_map/input_z/ppermute | solution.py:48
  254.8 13.0 %collective-permute-start.52 = (bf16[1,128,1024]{2,1,0:T(8,128)(2,1)}, bf16[1,128,1024]{2,1,0:T(8,128)(2,1)}, u32[]{:S(2)}, u32[]{:S(2)}) collective-permute-start(bf16[1,128,1024]{2,1,0:T(8,128)(2,1)} %fusion.6), channel_id=1, source_target_pairs={{0,4},{4,0},{8,12},{12,8},{16,20},{20,16},{24,28},{28,24},{1,5},{5... | collective-permute-start | bytes 786440 | tf_op jit(solution)/shard_map/w_out_x/ppermute | solution.py:51
  270.4 16.4 %collective-permute-start.50 = (bf16[128,1024]{1,0:T(8,128)(2,1)S(1)}, bf16[128,1024]{1,0:T(8,128)(2,1)}, u32[]{:S(2)}, u32[]{:S(2)}) collective-permute-start(bf16[128,1024]{1,0:T(8,128)(2,1)S(1)} %fusion.15), channel_id=1, source_target_pairs={{0,0},{1,4},{2,2},{3,6},{4,1},{5,5},{6,3},{7,7},{8,8},{9,12},{10,1... | collective-permute-start | bytes 786440 | tf_op jit(solution)/shard_map/input_turn/ppermute | solution.py:74
  (77 other events, 851.3 us)
Sparse Core Ops, SparseCore 0:
  68.9 66.9 all-gather.1
  165.4 63.5 reduce-scatter.1

commit v4 on v3

--- a/solution.py
+++ b/solution.py
@@ -16,9 +16,6 @@
 wide = jnp.float32
 lanes = 128
 half_lanes = 64
-attend_flops = 2**20
-attend_grad_flops = 4 * 10**9
-final_flops = 3 * 10**9
 
 
 def dot(a, b):
@@ -112,7 +109,11 @@
         for move in reversed(moves):
             cut = addends[0].shape[0] // 2
             received = move(total([value[cut:] for value in addends]).astype(low))
-            addends = [value[:cut] for value in addends] + [received]
+            if len(addends) > 2:
+                addends = [total([value[:cut] for value in addends])]
+            else:
+                addends = [value[:cut] for value in addends]
+            addends = addends + [received]
         return addends
 
     def xy_moves(self):
@@ -137,6 +138,10 @@
 
 def total(addends):
     return functools.reduce(jnp.add, [value.astype(wide) for value in addends])
+
+
+def after(value, *others):
+    return lax.optimization_barrier((value, others))[0]
 
 
 def tied(*values):
@@ -183,6 +188,20 @@
 
 def fetch(blocks, me, masks):
     return move_blocks(fetch_kernel, blocks, me, masks)
+
+
+def join_kernel(first_ref, second_ref, out_ref):
+    count = first_ref.shape[0]
+    out_ref[:count] = first_ref[...]
+    out_ref[count:] = second_ref[...]
+
+
+def join(first, second):
+    return pl.pallas_call(
+        join_kernel,
+        out_shape=jax.ShapeDtypeStruct((2 * first.shape[0],) + first.shape[1:], first.dtype),
+        cost_estimate=pl.CostEstimate(flops=1 << 20, bytes_accessed=2**10, transcendentals=0),
+    )(first, second)
 
 
 def lane_ids(rows):
@@ -292,7 +311,7 @@
         scratch_shapes=[pltpu.VMEM((length, 1), jnp.int32)],
         compiler_params=pltpu.CompilerParams(vmem_limit_bytes=48 * 2**20),
         cost_estimate=pl.CostEstimate(
-            flops=attend_flops, bytes_accessed=2**20, transcendentals=0
+            flops=1 << 20, bytes_accessed=2**20, transcendentals=0
         ),
     )(bias, near, far, w, cosine, sine, *ids)
 
@@ -452,8 +471,37 @@
         out_specs=out_specs,
         scratch_shapes=scratch,
         compiler_params=pltpu.CompilerParams(vmem_limit_bytes=48 * 2**20),
-        cost_estimate=pl.CostEstimate(flops=attend_grad_flops, bytes_accessed=2**10, transcendentals=0),
+        cost_estimate=pl.CostEstimate(flops=4000 << 20, bytes_accessed=2**10, transcendentals=0),
     )(*operands)
+
+
+def middle_grad_kernel(middle_ref, grad_out_ref, gain_ref, w_ref, *refs):
+    *parts, grads_ref, branch_ref, merged_ref, gain_out_ref = refs
+    middle = middle_ref[...]
+    inverse = lax.rsqrt(jnp.mean(middle * middle, axis=-1, keepdims=True) + epsilon)
+    unit = middle * inverse
+    grads = total([part[...] for part in parts])
+    gain_out_ref[...] = jnp.sum(grads * unit, axis=0, keepdims=True)
+    grads = grads * gain_ref[...]
+    mean = jnp.mean(grads * unit, axis=-1, keepdims=True)
+    grads = grad_out_ref[...].astype(wide) + inverse * (grads - unit * mean)
+    grads_ref[...] = grads
+    branch = grads.astype(low)
+    branch_ref[...] = branch
+    merged_ref[...] = dot_t(branch, w_ref[...]).astype(low)
+
+
+def middle_grad(middle, grad_out, gain, w, parts):
+    return pl.pallas_call(
+        middle_grad_kernel,
+        out_shape=(
+            jax.ShapeDtypeStruct(middle.shape, wide),
+            jax.ShapeDtypeStruct(middle.shape, low),
+            jax.ShapeDtypeStruct((middle.shape[0], w.shape[0]), low),
+            jax.ShapeDtypeStruct((1, middle.shape[1]), wide),
+        ),
+        cost_estimate=pl.CostEstimate(flops=1 << 20, bytes_accessed=2**10, transcendentals=0),
+    )(middle, grad_out, gain, w, *parts)
 
 
 def feed_kernel(units, tokens_ref, grads_ref, w_ref, hidden_ref, grad_units_ref, up_ref, down_ref):
@@ -498,7 +546,7 @@
         ),
         compiler_params=pltpu.CompilerParams(vmem_limit_bytes=58 * 2**20),
         cost_estimate=pl.CostEstimate(
-            flops=10 * count * width * units, bytes_accessed=8 * 2**20, transcendentals=count * units
+            flops=5000 << 20, bytes_accessed=2**10, transcendentals=0
         ),
     )(tokens, grads, w)
 
@@ -536,7 +584,7 @@
         out_specs=pl.BlockSpec((step, 3 * units), lambda i: (i, 0)),
         compiler_params=pltpu.CompilerParams(vmem_limit_bytes=58 * 2**20),
         cost_estimate=pl.CostEstimate(
-            flops=12 * count * width * units, bytes_accessed=12 * 2**20, transcendentals=0
+            flops=5000 << 20, bytes_accessed=2**10, transcendentals=0
         ),
     )(*near, *far)
 
@@ -554,51 +602,149 @@
     return pl.pallas_call(
         finish_input_kernel,
         out_shape=jax.ShapeDtypeStruct(tokens.shape, low),
-        cost_estimate=pl.CostEstimate(flops=final_flops, bytes_accessed=2**20, transcendentals=0),
+        cost_estimate=pl.CostEstimate(flops=3000 << 20, bytes_accessed=2**20, transcendentals=0),
     )(tokens, upstream, grads)
 
 
-def finish_qkv_kernel(group_ref, grads_ref, w_ref, gain_ref, out_ref, gain_out_ref):
-    share = w_ref.shape[0]
+def extra_rows(first, second):
+    shape = (16, first.shape[1])
+    row = lax.broadcasted_iota(jnp.int32, shape, 0)
+    result = jnp.zeros(shape, wide)
+    for i, value in enumerate((first, second)):
+        high = value.astype(low).astype(wide)
+        result = jnp.where(row == 2 * i, high, jnp.where(row == 2 * i + 1, value - high, result))
+    return result.astype(low)
+
+
+def moved(row, shift):
+    rows = jnp.broadcast_to(row, (8, row.shape[1]))
+    return pltpu.roll(rows, lax.rem(shift + row.shape[1], row.shape[1]), 1)[:1]
+
+
+def first_lanes(row, count):
+    return jnp.where(lax.broadcasted_iota(jnp.int32, row.shape, 1) < count, row, 0.0)
+
+
+def qkv_sum_kernel(z_size, z_ref, *refs):
+    *parts, out_ref, sum_ref = refs
+    sum_ref[...] = total([part[...] for part in parts])
+    count = (sum_ref.shape[0] - 16) // z_size
+    extra = sum_ref[sum_ref.shape[0] - 16 :, :]
+    bias, gain = extra[0:1] + extra[1:2], extra[2:3] + extra[3:4]
+    for d in range(z_size):
+        z = jnp.bitwise_xor(z_ref[0], d)
+        out_ref[d, :count, :] = sum_ref[pl.ds(pl.multiple_of(z * count, count), count), :].astype(low)
+        out_ref[d, count:, :] = extra_rows(bias, first_lanes(moved(gain, -z * count), count))
+
+
+def qkv_sum(z, z_size, parts):
+    rows, columns = parts[0].shape
+    vmem = pl.BlockSpec(memory_space=pltpu.VMEM)
+    return pl.pallas_call(
+        functools.partial(qkv_sum_kernel, z_size),
+        out_shape=jax.ShapeDtypeStruct((z_size, (rows - 16) // z_size + 16, columns), low),
+        in_specs=[pl.BlockSpec(memory_space=pltpu.SMEM)] + [vmem] * len(parts),
+        out_specs=vmem,
+        scratch_shapes=[pltpu.VMEM((rows, columns), wide)],
+        cost_estimate=pl.CostEstimate(flops=2**20, bytes_accessed=2**10, transcendentals=0),
+    )(z.reshape(1).astype(jnp.int32), *parts)
+
+
+def qkv_pack_kernel(biases, c_ref, *refs):
+    *parts, own_ref, sent_ref, extra_ref = refs
+    share = own_ref.shape[1]
+    c = c_ref[0]
+    bias, gain = 0.0, 0.0
+    for d, part in enumerate(parts):
+        own_ref[d] = part[pl.ds(pl.multiple_of(c * share, share), share), :]
+        sent_ref[d * share : (d + 1) * share, :] = part[pl.ds(pl.multiple_of((1 - c) * share, share), share), :]
+        extra = part[2 * share :, :].astype(wide)
+        bias += moved(first_lanes(extra[0:1] + extra[1:2], biases), d * biases)
+        gain += first_lanes(extra[2:3] + extra[3:4], 2 * share)
+    gain_sent = first_lanes(moved(gain, -(1 - c) * share), share)
+    sent_ref[len(parts) * share :, :] = extra_rows(bias, gain_sent)
+    row = lax.broadcasted_iota(jnp.int32, extra_ref.shape, 0)
+    gain_own = first_lanes(moved(gain, -c * share), share)
+    extra_ref[...] = jnp.where(row == 0, bias, jnp.where(row == 1, gain_own, 0.0))
+
+
+def qkv_pack(c, share, biases, parts):
+    columns = parts[0].shape[1]
+    vmem = pl.BlockSpec(memory_space=pltpu.VMEM)
+    return pl.pallas_call(
+        functools.partial(qkv_pack_kernel, biases),
+        out_shape=(
+            jax.ShapeDtypeStruct((len(parts), share, columns), low),
+            jax.ShapeDtypeStruct((len(parts) * share + 16, columns), low),
+            jax.ShapeDtypeStruct((8, columns), wide),
+        ),
+        in_specs=[pl.BlockSpec(memory_space=pltpu.SMEM)] + [vmem] * len(parts),
+        out_specs=(vmem, vmem, vmem),
+        cost_estimate=pl.CostEstimate(flops=2**20, bytes_accessed=2**10, transcendentals=0),
+    )(c.reshape(1).astype(jnp.int32), *parts)
+
+
+def finish_qkv_kernel(
+    biases, group_ref, own_ref, got_ref, extra_ref, w_ref, gain_ref, out_ref, gain_out_ref, gain_two_ref, bias_ref
+):
+    count, share, _ = own_ref.shape
     low_half = lane_ids(share) < half_lanes
     gain = gain_ref[...].astype(wide)
-    total = jnp.zeros((share, lanes), wide)
-    for i in range(grads_ref.shape[0]):
-        query, key, value = (grads_ref[i, :, j * lanes : (j + 1) * lanes].astype(wide) for j in range(3))
+    summed = jnp.zeros((share, lanes), wide)
+    extra = got_ref[count * share :, :].astype(wide)
+    bias_rows = extra_ref[0:1, :], extra[0:1] + extra[1:2]
+    bias = jnp.zeros((1, bias_rows[0].shape[1]), wide)
+    lane = lax.broadcasted_iota(jnp.int32, bias.shape, 1)
+    for i in range(2 * count):
+        d, e = i // 2, i % 2
+        place = jnp.bitwise_xor(group_ref[0], i)
+        parts = []
+        for j in range(3):
+            columns = slice(j * lanes, (j + 1) * lanes)
+            part = got_ref[d * share : (d + 1) * share, columns] if e else own_ref[d, :, columns]
+            parts.append(part.astype(wide))
+        query, key, value = parts
         key = pltpu.roll(key, half_lanes, 1)
-        start = jnp.bitwise_xor(group_ref[0], i) * (3 * lanes)
         parts = (
             jnp.where(low_half, query, key),
             jnp.where(low_half, value, query),
             jnp.where(low_half, key, value),
         )
         for j, part in enumerate(parts):
-            at = pl.ds(pl.multiple_of(start + j * lanes, lanes), lanes)
-            total += part * w_ref[:, at].astype(wide)
+            at = pl.ds(pl.multiple_of(place * (3 * lanes) + j * lanes, lanes), lanes)
+            summed += part * w_ref[:, at].astype(wide)
             out_ref[:, at] = part * gain
-    column = jnp.broadcast_to(jnp.sum(total, axis=1, keepdims=True), (share, lanes))
+        here = (lane >= place * biases) & (lane < (place + 1) * biases)
+        bias = jnp.where(here, moved(bias_rows[e], place * biases - d * biases), bias)
+    column = jnp.broadcast_to(jnp.sum(summed, axis=1, keepdims=True), (share, lanes))
     gain_out_ref[...] = jnp.transpose(column)[:1, :]
-
-
-def finish_qkv(group, grads, w, gain):
+    gain_two_ref[...] = (extra_ref[1:2, :] + extra[2:3] + extra[3:4])[:, :lanes]
+    bias_ref[...] = bias[:, :lanes]
+
+
+def finish_qkv(biases, group, own, got, extra, w, gain):
     vmem = pl.BlockSpec(memory_space=pltpu.VMEM)
+    share = w.shape[0]
     return pl.pallas_call(
-        finish_qkv_kernel,
+        functools.partial(finish_qkv_kernel, biases),
         out_shape=(
             jax.ShapeDtypeStruct(w.shape, wide),
-            jax.ShapeDtypeStruct((1, w.shape[0]), wide),
+            jax.ShapeDtypeStruct((1, share), wide),
+            jax.ShapeDtypeStruct((1, lanes), wide),
+            jax.ShapeDtypeStruct((1, lanes), wide),
         ),
-        in_specs=[pl.BlockSpec(memory_space=pltpu.SMEM)] + [vmem] * 3,
-        out_specs=(vmem, vmem),
-        cost_estimate=pl.CostEstimate(flops=final_flops, bytes_accessed=2**20, transcendentals=0),
-    )(group.reshape(1).astype(jnp.int32), grads, w, gain)
-
-
-def finish_feed_kernel(x_ref, mine_ref, other_ref, gate_ref, up_ref, down_ref):
-    units = mine_ref.shape[1] // 3
-    for ref, x in ((mine_ref, x_ref[0]), (other_ref, 1 - x_ref[0])):
+        in_specs=[pl.BlockSpec(memory_space=pltpu.SMEM)] + [vmem] * 5,
+        out_specs=(vmem,) * 4,
+        cost_estimate=pl.CostEstimate(flops=3000 << 20, bytes_accessed=2**20, transcendentals=0),
+    )(group.reshape(1).astype(jnp.int32), own, got, extra, w, gain)
+
+
+def finish_feed_kernel(x_ref, both_ref, other_ref, gate_ref, up_ref, down_ref):
+    depth, units = other_ref.shape[0], other_ref.shape[1] // 3
+    mine = pl.ds(pl.multiple_of(x_ref[0] * depth, depth), depth)
+    for value, x in ((both_ref[mine, :], x_ref[0]), (other_ref[...], 1 - x_ref[0])):
         at = pl.ds(pl.multiple_of(x * units, units), units)
-        parts = [ref[:, j * units : (j + 1) * units].astype(wide) for j in range(3)]
+        parts = [value[:, j * units : (j + 1) * units].astype(wide) for j in range(3)]
         gate_ref[:, at], up_ref[:, at] = parts[:2]
         if down_ref.shape[0] == 2 * units:
             down_ref[at, :] = jnp.transpose(parts[2])
@@ -606,9 +752,9 @@
             down_ref[:, at] = parts[2]
 
 
-def finish_feed(x, mine, other):
+def finish_feed(x, both, other):
     vmem = pl.BlockSpec(memory_space=pltpu.VMEM)
-    depth, units = mine.shape[0], mine.shape[1] // 3
+    depth, units = other.shape[0], other.shape[1] // 3
     return pl.pallas_call(
         finish_feed_kernel,
         out_shape=(
@@ -618,8 +764,8 @@
         ),
         in_specs=[pl.BlockSpec(memory_space=pltpu.SMEM), vmem, vmem],
         out_specs=(vmem,) * 3,
-        cost_estimate=pl.CostEstimate(flops=final_flops, bytes_accessed=2**20, transcendentals=0),
-    )(x.reshape(1).astype(jnp.int32), mine, other)
+        cost_estimate=pl.CostEstimate(flops=3000 << 20, bytes_accessed=2**20, transcendentals=0),
+    )(x.reshape(1).astype(jnp.int32), both, other)
 
 
 def rope_tables(stamps, dimension):
@@ -694,8 +840,20 @@
     by_z = jnp.stack(called("qkv_z", at.scatter_z, sent))
     gains = by_z[:, -16, : 2 * share].reshape(-1)
     by_z = by_z[:, :-16].reshape(-1, 3 * padded)
-    turned, by_z, out_z = tied(turned, by_z, out_z)
-    near = called("tokens_z", at.gather_steps, turned, at.z_moves()).reshape(-1, width)
+    late_gate, late_up, late_down = w_gate, w_up, w_down
+    by_z, late_gate, late_up, late_down = tied(by_z, w_gate, w_up, w_down)
+    units = w_gate.shape[1] // 2
+    down_t = with_layout_constraint(late_down.T, Layout(major_to_minor=(0, 1)))
+    firsts = jnp.concatenate([v[:, :units] for v in (late_gate, late_up, down_t)], axis=1)
+    seconds = jnp.concatenate([v[:, units:] for v in (late_gate, late_up, down_t)], axis=1)
+    mine = pick(at.x, firsts, seconds)
+    other = called("ffn_x", at.along_x, pick(at.x, seconds, firsts))
+    z_block = jnp.concatenate([pick(at.x, mine, other), pick(at.x, other, mine)], axis=0)
+
+    z_early = z_block
+    near = called("tokens_z", at.gather_steps, turned, at.z_moves()[:-1])
+    near = near
+    near = join(near, called("tokens_z", at.z_moves()[-1], near)).reshape(-1, width)
     by_xy = jnp.stack(called("qkv_xy", at.gather_xy, with_extra(by_z, gains)))
     gains = by_xy[:, -16, : gains.shape[0]].reshape(y_size, 2, z_size, 2, share)
     gains = gains.transpose(2, 1, 0, 3, 4).reshape(-1, share)
@@ -711,20 +869,14 @@
     ]
     w_heads = place(by_xy.reshape(-1, share, 3 * padded), device_id, masks).reshape(width, 3 * padded)
 
-    w_heads, late_gate, late_up, late_down = tied(w_heads, w_gate, w_up, w_down)
-    units = w_gate.shape[1] // 2
-    down_t = with_layout_constraint(late_down.T, Layout(major_to_minor=(0, 1)))
-    firsts = jnp.concatenate([v[:, :units] for v in (late_gate, late_up, down_t)], axis=1)
-    seconds = jnp.concatenate([v[:, units:] for v in (late_gate, late_up, down_t)], axis=1)
-    mine = pick(at.x, firsts, seconds)
-    other = called("ffn_x", at.along_x, pick(at.x, seconds, firsts))
-    z_block = jnp.concatenate([pick(at.x, mine, other), pick(at.x, other, mine)], axis=0)
+    out_xy = called("out_xy", at.gather_steps, out_z, at.xy_moves())
 
     grad_out = cotangent[0]
-    xy_rows = jnp.concatenate([grad_out, out_z], axis=0)
-    xy_rows = called("cotangent_x", at.gather_steps, xy_rows, at.xy_moves()[:1])
-
-    near, z_block, w_heads, xy_rows = tied(near, z_block, w_heads, xy_rows)
+    grad_out_near = called("cotangent_x", at.gather_steps, grad_out, at.xy_moves()[:1])
+
+    near, w_heads = tied(near, w_heads)
+    near, out_xy = tied(near, out_xy)
+    near, grad_out_near = tied(near, grad_out_near)
     w_ffn = lax.all_gather(z_block, "seq", axis=0, tiled=True, axis_index_groups=at.columns_z())
 
     time_ids, variate_ids, seq_ids, by_z = tied(time_ids, variate_ids, seq_ids, by_z)
@@ -751,14 +903,8 @@
     far = called("tokens_core", at.along_c, near)
     query, key, value, attended = attend(bias, near, far, w_heads, cosine, sine, ids, heads)
 
-    held = xy_rows[None]
-    for move in at.xy_moves()[1:]:
-        received = called("cotangent_y", move, held)
-        received, query = tied(received, query)
-        held = jnp.concatenate([held, received], axis=0)
-    xy_rows = held.reshape(2 * y_size, -1, width)
-    xy_rows_far = called("cotangent_core", at.along_c, xy_rows)
-    out_blocks = jnp.stack([xy_rows[:, rows:], xy_rows_far[:, rows:]]).reshape(-1, share, width)
+    out_far = called("out_core", at.along_c, out_xy)
+    out_blocks = jnp.stack([out_xy, out_far]).reshape(-1, share, width)
     out_masks = [
         (dx * z_size + d) * at.head_size + 2 * dy + e
         for e in range(2)
@@ -773,7 +919,16 @@
     received = [received[d] for d in at.z_order()]
     kept = jnp.concatenate([block[0] for block in received], axis=1)
     passed = jnp.concatenate([block[1] for block in received], axis=1)
+    held = grad_out_near[None]
+    for move in at.xy_moves()[1:]:
+        got = called("cotangent_y", move, held)
+        got, passed = tied(got, passed)
+        held = jnp.concatenate([held, got], axis=0)
+    grad_out_near = held.reshape(2 * y_size, rows, width)
+    grad_out_far = called("cotangent_core", at.along_c, grad_out_near)
+
     passed = called("attended_core", at.along_c, passed)
+
     merged = called("attended_turn", at.turn, jnp.concatenate([kept, passed], axis=1))
 
     middle = tokens + dot(merged, out_rows)
@@ -783,62 +938,60 @@
     normed_near = jnp.concatenate(called("normed_xy", at.gather_xy, normed_two), axis=0)
     normed_far = called("normed_core", at.along_c, normed_near)
 
-    hidden_far, units_far, up_far, down_far = feed(normed_far, xy_rows_far, w_ffn)
-    hidden_near, units_near, up_near, down_near = feed(normed_near, xy_rows, w_ffn)
-
-    grad_w_ffn = feed_grad(
-        (normed_near, xy_rows, hidden_near, units_near),
-        (normed_far, xy_rows_far, hidden_far, units_far),
-    )
+    hidden_far, units_far, up_far, down_far = feed(normed_far, grad_out_far, w_ffn)
+    hidden_near, units_near, up_near, down_near = feed(normed_near, grad_out_near, w_ffn)
+
     blocks = (2 * y_size, rows, width)
     up = up_near.reshape(blocks), called("up_core", at.along_c, up_far).reshape(blocks)
-    received = called(
-        "up_xy", at.scatter_xy, [total([part[i] for part in up]).astype(low) for i in range(2 * y_size)]
+    kept = [total([part[i] for part in up]).astype(low) for i in range(2 * y_size)]
+    grad_w_ffn = feed_grad(
+        (normed_near, grad_out_near, hidden_near, units_near),
+        (normed_far, grad_out_far, hidden_far, units_far),
     )
+    received = called("up_xy", at.scatter_xy, kept)
     down = [down_near.reshape(blocks), called("down_core", at.along_c, down_far).reshape(blocks)]
-    received[0], down[1] = tied(received[0], down[1])
-    grad_two = total(received)
-    gain_part = jnp.sum(grad_two * unit_two, axis=0)
-    upstream = grad_two * gain_two
+    moves = at.xy_moves()
+    y_cut = y_size // 2
+    down = [part.reshape(y_size, 2, rows, width) for part in down]
+    down_sent = total([part[y_cut:] for part in down]).astype(low)
+    received[0], down_sent = tied(received[0], down_sent)
+    down = [part[:y_cut] for part in down] + [called("down_y", moves[-1], down_sent)]
+    *received[1:], grad_w_ffn = tied(*received[1:], grad_w_ffn)
+    grad_middle, grad_branch, grad_merged, gain_part = middle_grad(middle, grad_out, gain_two, out_rows, received)
+
+    turned_back = called("merged_turn", at.turn, grad_merged)
     grad_w_ffn = lax.psum_scatter(
         grad_w_ffn, "seq", scatter_dimension=0, tiled=True, axis_index_groups=at.columns_z()
     )
-
-    grad_middle = (
-        grad_out.astype(wide)
-        + inverse_two * upstream
-        - unit_two * inverse_two * jnp.mean(upstream * unit_two, axis=-1, keepdims=True)
-    )
-    grad_branch = grad_middle.astype(low)
-    grad_merged = dot_t(grad_branch, out_rows).astype(low)
-
-    turned_back = called("merged_turn", at.turn, grad_merged)
     cut = width // 2
     kept, passed = turned_back[:, :cut], called("merged_core", at.along_c, turned_back[:, cut:])
+    merged, grad_branch, passed = tied(merged, grad_branch, passed)
     sent = []
     for d in range(z_size):
         columns = slice(places[d] * group_width, (places[d] + 1) * group_width)
         sent.append(jnp.stack([part[:, columns] for part in (kept, passed)]))
-    received = called("merged_z", at.scatter_z, sent)
-    received = jnp.stack([received[d] for d in at.z_order()], axis=1)
-    grad_attended = received.reshape(2 * z_size * rows, group_width)
-    if padded > group_width:
-        grad_attended = jnp.pad(grad_attended, ((0, 0), (0, padded - group_width)))
-
-    moves = at.xy_moves()
-    down[1], grad_branch = tied(down[1], grad_branch)
-    down = called("down_y", at.scatter_steps, [part.reshape(y_size, 2, rows, width) for part in down], moves[1:])
-
-    merged, grad_branch, turned_back = tied(merged, grad_branch, turned_back)
+    received_z = called("merged_z", at.scatter_z, sent)
+    received_one = received_z[1]
+
     grad_out_rows = t_dot(merged, grad_branch).astype(low)
     grad_out_rows = fetch(grad_out_rows.reshape(-1, share, width), at.head, out_masks)
     grad_out_rows = grad_out_rows.reshape(2, y_size, 2, z_size * share, width)
     out_parts = [grad_out_rows[0], called("w_out_core", at.along_c, grad_out_rows[1])]
-    y_cut = y_size // 2
     out_sent = total([part[y_cut:] for part in out_parts]).astype(low)
-    grad_attended, out_sent, down[-1] = tied(grad_attended, out_sent, down[-1])
-    out_parts = [part[:y_cut] for part in out_parts] + [called("w_out_y", moves[-1], out_sent)]
-    out_parts = called("w_out_y", at.scatter_steps, out_parts, moves[1:-1])
+    received_one, out_sent = tied(received_one, out_sent)
+    received_z[1] = received_one
+    received = jnp.stack([received_z[d] for d in at.z_order()], axis=1)
+    grad_attended = received.reshape(2 * z_size * rows, group_width)
+    if padded > group_width:
+        grad_attended = jnp.pad(grad_attended, ((0, 0), (0, padded - group_width)))
+    down = called("down_y", at.scatter_steps, down, moves[1:-1])
+    down = [part.reshape(2, rows, width) for part in down]
+    down_sent = total([part[1] for part in down]).astype(low)
+    down = [part[0] for part in down] + [called("down_x", moves[0], down_sent)]
+    grad_attended, out_sent = tied(grad_attended, out_sent)
+    grad_attended, down[-1] = tied(grad_attended, down[-1])
+    out_got = called("w_out_y", moves[-1], out_sent)
+    out_parts = [part[:y_cut] for part in out_parts] + [out_got]
 
     def halves(values):
         high = values.astype(low)
@@ -878,66 +1031,87 @@
             for i, masks in enumerate(device_masks)
         ]
 
+    upstream_far, out_parts[-1] = tied(upstream_far, out_parts[-1])
     upstream_far = called("input_core", at.along_c, upstream_far)
     z_moves = at.z_moves()
     blocks = (z_size, rows, width)
     upstream_z = [upstream_near.reshape(blocks), upstream_far.reshape(blocks)]
-    upstream_z = called("input_z", at.scatter_steps, upstream_z, z_moves[-1:])
+    z_cut = z_size // 2
+    upstream_sent = total([part[z_cut:] for part in upstream_z]).astype(low)
+    upstream_z = [part[:z_cut] for part in upstream_z] + [called("input_z", z_moves[-1], upstream_sent)]
+
+    out_parts = called("w_out_y", at.scatter_steps, out_parts, moves[1:-1])
+    out_parts = [part.reshape(2, -1, width) for part in out_parts]
+    out_parts = called("w_out_x", at.scatter_steps, out_parts, moves[:1])
+    out_parts[-1] = out_parts[-1]
 
     def joined(block, row, count):
         return block[row, :count].astype(wide) + block[row + 1, :count].astype(wide)
 
     received = called("grad_qkv_xy", at.scatter_xy, messages)
-    summed = functools.reduce(jnp.add, [block.astype(wide) for block in received])
+    fast = in_kernel and heads == 2 and head_dim == half_lanes
+    if fast:
+        sent = qkv_sum(at.z, z_size, received)
+    else:
+        summed = total(received)
+        bias_sum = joined(summed[-16:], 0, bias_count)
+        gain_sum = joined(summed[-16:], 2, gain_count).reshape(z_size, 2 * share)
+        summed = summed[:-16].astype(low).reshape(z_size, 2 * share, 3 * padded)
+        sent = []
+        for d in range(z_size):
+            block, gain = (
+                lax.dynamic_index_in_dim(v, jnp.bitwise_xor(at.z, d), axis=0, keepdims=False)
+                for v in (summed, gain_sum)
+            )
+            sent.append(with_extra(block, *halves(bias_sum), *halves(gain)))
     depth = grad_w_ffn.shape[0] // 2
-    mine = pick(at.x, grad_w_ffn[:depth], grad_w_ffn[depth:])
     other = called("grad_ffn_x", at.along_x, pick(at.x, grad_w_ffn[depth:], grad_w_ffn[:depth]))
-    summed, upstream_z[-1], other, down[-1], out_parts[-1] = tied(
-        summed, upstream_z[-1], other, down[-1], out_parts[-1]
-    )
-    upstream_one = total(called("input_z", at.scatter_steps, upstream_z, z_moves[:-1]))[0]
-    down = [part.reshape(2, rows, width) for part in down]
-    output = middle + total(called("down_x", at.scatter_steps, down, moves[:1]))[0]
-    out_parts = called("w_out_x", at.scatter_steps, [part.reshape(2, -1, width) for part in out_parts], moves[:1])
+    upstream_z[-1], other = tied(upstream_z[-1], other)
+    upstream_z[-1], sent = tied(upstream_z[-1], sent)
+    z_cut = z_cut // 2
+    upstream_sent = total([part[z_cut:] for part in upstream_z]).astype(low)
+    upstream_sent, sent = tied(upstream_sent, sent)
+    upstream_z = [part[:z_cut] for part in upstream_z] + [called("input_z", z_moves[-2], upstream_sent)]
+    grad_w_gate, grad_w_up, grad_w_down = finish_feed(at.x, grad_w_ffn, other)
+    if grad_w_down.shape != w_down.shape:
+        grad_w_down = grad_w_down.T
+    upstream_z[-1] = after(upstream_z[-1], grad_w_gate)
+    upstream_one = total(called("input_z", at.scatter_steps, upstream_z, z_moves[:-2]))[0]
+    out_parts[-1] = out_parts[-1]
+    output = middle + total(down)
     out_parts = [part.reshape(z_size, share, width) for part in out_parts]
     grad_w_out = total(called("w_out_z", at.scatter_steps, out_parts, z_moves))[0]
-    bias_sum = joined(summed[-16:], 0, bias_count)
-    gain_sum = joined(summed[-16:], 2, gain_count).reshape(z_size, 2 * share)
-    summed = summed[:-16].astype(low).reshape(z_size, 2 * share, 3 * padded)
-    sent = []
-    for d in range(z_size):
-        block, gain = (
-            lax.dynamic_index_in_dim(v, jnp.bitwise_xor(at.z, d), axis=0, keepdims=False)
-            for v in (summed, gain_sum)
+    received = called("grad_qkv_z", at.scatter_z, [sent[d] for d in range(z_size)])
+    upstream_one, received[0] = tied(upstream_one, received[0])
+    if fast:
+        core_own, core_sent, extra_own = qkv_pack(at.c, share, bias_count, received)
+    else:
+        bias_z = jnp.concatenate([joined(block[-16:], 0, bias_count) for block in received])
+        gain_sum = functools.reduce(jnp.add, [joined(block[-16:], 2, 2 * share) for block in received])
+        received = jnp.stack([block[:-16] for block in received]).reshape(z_size, 2, share, 3 * padded)
+        core_own = pick(at.c, received[:, 0], received[:, 1])
+        core_sent = pick(at.c, received[:, 1], received[:, 0]).reshape(-1, 3 * padded)
+        gain_own = pick(at.c, gain_sum[:share], gain_sum[share:])
+        gain_sent = pick(at.c, gain_sum[share:], gain_sum[:share])
+        core_sent = with_extra(core_sent, *halves(bias_z), *halves(gain_sent))
+    upstream_one = upstream_one.astype(low)
+    core_sent = core_sent
+    upstream_one = called("input_turn", at.turn, upstream_one)
+    grad_input = finish_input(inputs[0], upstream_one, grad_middle)
+    core_got = called("grad_qkv_core", at.along_c, core_sent)
+    if fast:
+        grad_w_qkv, grad_gain_attn, grad_gain_ffn, full_bias = finish_qkv(
+            bias_count, group, core_own, core_got, extra_own, w_qkv, gain_attn[:, None]
         )
-        sent.append(with_extra(block, *halves(bias_sum), *halves(gain)))
-    received = called("grad_qkv_z", at.scatter_z, sent)
-    bias_z = jnp.concatenate([joined(block[-16:], 0, bias_count) for block in received])
-    gain_sum = functools.reduce(jnp.add, [joined(block[-16:], 2, 2 * share) for block in received])
-    received = jnp.stack([block[:-16] for block in received]).reshape(z_size, 2, share, 3 * padded)
-    core_own = pick(at.c, received[:, 0], received[:, 1])
-    core_sent = pick(at.c, received[:, 1], received[:, 0]).reshape(-1, 3 * padded)
-    gain_own = pick(at.c, gain_sum[:share], gain_sum[share:])
-    gain_sent = pick(at.c, gain_sum[share:], gain_sum[:share])
-    core_sent, upstream_one = tied(core_sent, upstream_one)
-    grad_w_gate, grad_w_up, grad_w_down = finish_feed(at.x, mine, other)
-    if grad_w_down.shape != w_down.shape:
-        grad_w_down = grad_w_down.T
-    upstream_one = called("input_turn", at.turn, upstream_one.astype(low))
-    grad_input = finish_input(inputs[0], upstream_one, grad_middle)
-    core_got = called(
-        "grad_qkv_core", at.along_c, with_extra(core_sent, *halves(bias_z), *halves(gain_sent))
-    )
-    core_other = core_got[:-16].reshape(z_size, share, 3 * padded)
-    grad_gain_ffn = gain_own + joined(core_got[-16:], 2, share)
-    biases = jnp.stack([bias_z, joined(core_got[-16:], 0, z_size * bias_count)])
-    biases = list(biases.reshape(2, z_size, heads, 2).transpose(1, 0, 2, 3).reshape(groups, heads, 2))
-    full_bias = jnp.concatenate(xor_list(biases, group), axis=0)
-    by_group = jnp.stack([core_own, core_other], axis=1).reshape(groups, share, 3 * padded)
-    if heads == 2 and head_dim == half_lanes:
-        grad_w_qkv, grad_gain_attn = finish_qkv(group, by_group, w_qkv, gain_attn[:, None])
-        grad_gain_attn = grad_gain_attn[0]
+        grad_gain_attn, grad_gain_ffn = grad_gain_attn[0], grad_gain_ffn[0, :share]
+        full_bias = full_bias[0, : 2 * head_count].reshape(head_count, 2)
     else:
+        core_other = core_got[:-16].reshape(z_size, share, 3 * padded)
+        grad_gain_ffn = gain_own + joined(core_got[-16:], 2, share)
+        biases = jnp.stack([bias_z, joined(core_got[-16:], 0, z_size * bias_count)])
+        biases = list(biases.reshape(2, z_size, heads, 2).transpose(1, 0, 2, 3).reshape(groups, heads, 2))
+        full_bias = jnp.concatenate(xor_list(biases, group), axis=0)
+        by_group = jnp.stack([core_own, core_other], axis=1).reshape(groups, share, 3 * padded)
         by_group = place(by_group, group, list(range(groups))).astype(wide).reshape(groups, share, 3, padded)
         by_group = by_group[..., :group_width].reshape(groups, share, 3, heads, head_dim)
         raw = by_group.transpose(1, 0, 3, 2, 4).reshape(share, 3 * width)

time: 297 us -> 292 us (0.983)
  other arithmetic: 43.3 us -> 32 us
  Pallas kernels: 49 us -> 59.9 us
  waiting for transfers between devices: 85.6 us -> 79.2 us
    ppermute x7 -> x8, waiting for transfers between devices: 25.4 us -> 9.34 us  [along_xy(): lax.ppermute(value, 'head', [(i, i ^ 2 * dy) for i in range(self.head_siz...]
    all_gather x1, waiting for transfers between devices: 0.01 us -> 11.8 us  [shards(): lax.all_gather(z_block, 'seq', axis=0, tiled=True, axis_index_groups=at.c...]
    pallas_call x1 -> x5, Pallas kernels: 2 us -> 12.5 us  [the longest x1 4.47 us: middle_grad(): pl.pallas_call(middle_grad_kernel, out_shape=(jax.ShapeDtypeStruct(middle...]
    convert_element_type x7 -> x3, other arithmetic: 10.2 us -> 1.9 us  [scatter_steps(): received = move(total([value[cut:] for value in addends]).astype(low))]
    ppermute x4, starting transfers between devices: 2.9 us -> 10.7 us  [along_xy(): lax.ppermute(value, ('seq', 'head'), [(s * self.head_size + h, (s ^ dx) *...]
    ppermute x9 -> x10, starting transfers between devices: 16.4 us -> 9.26 us  [along_x(): lax.ppermute(value, 'seq', [(i, i ^ 1) for i in range(self.seq_size)])]
    slice x6 -> x1, local copies, waits for them, and re-layouts: 4.52 us -> 0.04 us  [scatter_steps(): received = move(total([value[cut:] for value in addends]).astype(low))]
    add x9 -> x0, other arithmetic: 4.09 us -> none  [the longest x6 1.52 us: joined(): return block[row, :count].astype(wide) + block[row + 1, :count].astype(wide)]
  transfers between devices with their start and end apart: 57 -> 60, of which waited for: 26 -> 23; matrix products, arithmetic and copies ran while one was open for 20% -> 15% of each run, Pallas kernels for 13% -> 18%
where the time goes in v4:
time: 292 us; the launch traced here: 288 us
  waiting for transfers between devices  79.2 us (27%)
  starting transfers between devices  79.1 us (27%)
  Pallas kernels  59.9 us (21%)
  other arithmetic  32 us (11%)
  local copies, waits for them, and re-layouts  19.9 us (7%)
  between operations  15.6 us (5%)
    ppermute x20, starting transfers between devices, along_z(): lax.ppermute(value, 'seq', [(i, i ^ 2 * step) for i in range(self.seq_siz...  36.6 us
    ppermute x20, waiting for transfers between devices, along_z(): lax.ppermute(value, 'seq', [(i, i ^ 2 * step) for i in range(self.seq_siz...  36.6 us
    pallas_call x2, Pallas kernels, feed(): pl.pallas_call(functools.partial(feed_kernel, units), grid=(count // step...  13.9 us
    all_gather x1, waiting for transfers between devices, shards(): lax.all_gather(z_block, 'seq', axis=0, tiled=True, axis_index_groups=at.c...  11.8 us
    pallas_call x1, Pallas kernels, attend_grad(): pl.pallas_call(kernel, out_shape=out_shape, in_specs=in_specs, out_specs=...  11.7 us
    ppermute x4, starting transfers between devices, along_xy(): lax.ppermute(value, ('seq', 'head'), [(s * self.head_size + h, (s ^ dx) *...  10.7 us
    ppermute x10, waiting for transfers between devices, along_x(): lax.ppermute(value, 'seq', [(i, i ^ 1) for i in range(self.seq_size)])  10.5 us
    ppermute x8, starting transfers between devices, along_xy(): lax.ppermute(value, 'head', [(i, i ^ 2 * dy) for i in range(self.head_siz...  9.76 us
  transfers between devices with their start and end apart: 60, of which 23 were waited for; matrix products, arithmetic and copies ran while one was open for 15% of the time, Pallas kernels for 18%

profile of v4, /device:TPU:0, one launch (start us, length us, event | category | flops | bytes accessed | tf_op | source)
XLA Modules:
  0.0 288.1 jit_solution(12195828589278318151)
XLA Ops:
  13.8 4.3 %collective-permute-start.3 = (bf16[144,384]{1,0:T(8,128)(2,1)S(1)}, bf16[144,384]{1,0:T(8,128)(2,1)S(1)}, u32[]{:S(2)}, u32[]{:S(2)}) collective-permute-start(bf16[144,384]{1,0:T(8,128)(2,1)S(1)} %fusion.23), channel_id=1, source_target_pairs={{0,1},{1,0},{2,3},{3,2},{4,5},{5,4},{6,7},{7,6},{8,9},{9,8},{10,11... | collective-permute-start | bytes 331784 | tf_op jit(solution)/shard_map/qkv_core/ppermute | solution.py:51
  47.9 5.4 %collective-permute-done.1 = bf16[1,128,1024]{2,1,0:T(8,128)(2,1)S(1)} collective-permute-done((bf16[1,128,1024]{2,1,0:T(8,128)(2,1)S(1)}, bf16[1,128,1024]{2,1,0:T(8,128)(2,1)S(1)}, u32[]{:S(2)}, u32[]{:S(2)}) %collective-permute-start.1) | collective-permute-done | bytes 262176 | tf_op jit(solution)/shard_map/tokens_z/ppermute | solution.py:45
  57.4 4.0 %collective-permute-done.7 = bf16[272,384]{1,0:T(8,128)(2,1)S(1)} collective-permute-done((bf16[272,384]{1,0:T(8,128)(2,1)}, bf16[272,384]{1,0:T(8,128)(2,1)S(1)}, u32[]{:S(2)}, u32[]{:S(2)}) %collective-permute-start.7) | collective-permute-done | bytes 208928 | tf_op jit(solution)/shard_map/qkv_xy/ppermute | solution.py:48
  63.0 3.4 %collective-permute-done.2.second_ref = bf16[2,128,1024]{2,1,0:T(8,128)(2,1)S(1)} collective-permute-done((bf16[2,128,1024]{2,1,0:T(8,128)(2,1)S(1)}, bf16[2,128,1024]{2,1,0:T(8,128)(2,1)S(1)}, u32[]{:S(2)}, u32[]{:S(2)}) %collective-permute-start.2) | collective-permute-done | bytes 524320 | tf_op jit(solution)/shard_map/tokens_z/ppermute | solution.py:45
  73.9 9.0 %shard_map.206 = (bf16[2,1024,128]{2,1,0:T(8,128)(2,1)S(1)}, bf16[2,1024,128]{2,1,0:T(8,128)(2,1)S(1)}, bf16[2,1024,128]{2,1,0:T(8,128)(2,1)S(1)}, bf16[1024,128]{1,0:T(8,128)(2,1)S(1)}) custom-call(f32[2,2]{1,0:T(2,128)S(1)} %pad_maximum_fusion.25.bias_ref, bf16[512,1024]{1,0:T(8,128)(2,1)S(1)} %bitcast.314, ...), custom_call_target="tpu_custom_call" | custom-call | flops 1048576 | bytes 1048576 | tf_op jit(solution)/shard_map/pallas_call | solution.py:306
  89.9 3.7 %collective-permute-done.18 = bf16[2,128,128]{2,1,0:T(8,128)(2,1)S(1)} collective-permute-done((bf16[2,128,128]{2,1,0:T(8,128)(2,1)S(1)}, bf16[2,128,128]{2,1,0:T(8,128)(2,1)S(1)}, u32[]{:S(2)}, u32[]{:S(2)}) %collective-permute-start.18) | collective-permute-done | bytes 65568 | tf_op jit(solution)/shard_map/attended_z/ppermute | solution.py:45
  96.3 4.5 %collective-permute-done.16 = bf16[2,128,128]{2,1,0:T(8,128)(2,1)S(1)} collective-permute-done((bf16[2,128,128]{2,1,0:T(8,128)(2,1)S(1)}, bf16[2,128,128]{2,1,0:T(8,128)(2,1)S(1)}, u32[]{:S(2)}, u32[]{:S(2)}) %collective-permute-start.16) | collective-permute-done | bytes 65568 | tf_op jit(solution)/shard_map/attended_z/ppermute | solution.py:45
  106.8 6.1 %collective-permute-start.25 = (bf16[128,1024]{1,0:T(8,128)(2,1)S(1)}, bf16[128,1024]{1,0:T(8,128)(2,1)S(1)}, u32[]{:S(2)}, u32[]{:S(2)}) collective-permute-start(bf16[128,1024]{1,0:T(8,128)(2,1)S(1)} %multiply_convert_fusion), channel_id=1, source_target_pairs={{0,6},{1,7},{2,4},{3,5},{4,2},{5,3},{6,0},{7,1},{8,14},{9,15},{10,... | collective-permute-start | bytes 786440 | tf_op jit(solution)/shard_map/normed_xy/ppermute | solution.py:60
  114.2 5.7 %collective-permute-done.25 = bf16[128,1024]{1,0:T(8,128)(2,1)S(1)} collective-permute-done((bf16[128,1024]{1,0:T(8,128)(2,1)S(1)}, bf16[128,1024]{1,0:T(8,128)(2,1)S(1)}, u32[]{:S(2)}, u32[]{:S(2)}) %collective-permute-start.25) | collective-permute-done | bytes 262176 | tf_op jit(solution)/shard_map/normed_xy/ppermute | solution.py:60
  119.9 5.3 %collective-permute-done.24 = bf16[128,1024]{1,0:T(8,128)(2,1)S(1)} collective-permute-done((bf16[128,1024]{1,0:T(8,128)(2,1)S(1)}, bf16[128,1024]{1,0:T(8,128)(2,1)S(1)}, u32[]{:S(2)}, u32[]{:S(2)}) %collective-permute-start.24) | collective-permute-done | bytes 262176 | tf_op jit(solution)/shard_map/normed_xy/ppermute | solution.py:57
  128.2 11.8 %all-gather.2.cloned.1.call-done.w_ref = bf16[1024,1536]{1,0:T(8,128)(2,1)} async-done(((bf16[256,1536]{1,0:T(8,128)(2,1)}), bf16[1024,1536]{1,0:T(8,128)(2,1)}) %all-gather.2.cloned.1.call-update) | async-done | bytes 3145744 | tf_op jit(solution)/shard_map/all_gather | solution.py:880
  140.0 7.0 %shard_map.209 = (bf16[512,512]{1,0:T(8,128)(2,1)}, bf16[512,1024]{1,0:T(8,128)(2,1)}, bf16[512,1024]{1,0:T(8,128)(2,1)}, bf16[512,1024]{1,0:T(8,128)(2,1)}) custom-call(bf16[512,1024]{1,0:T(8,128)(2,1)} %collective-permute-done.27.tokens_ref.refs_4_, bf16[4,128,1024]{2,1,0:T(8,128)(2,1)} %copy-done.48, bf16[1024,1536]{1,0:T(8,128)(2,1)} %all-gather.2.cloned.1.call-done.w_ref), custom_call_target="tpu_custom_call" | custom-call | flops 5242880000 | bytes 1024 | tf_op jit(solution)/shard_map/pallas_call | solution.py:527
  147.6 6.9 %shard_map.208 = (bf16[512,512]{1,0:T(8,128)(2,1)}, bf16[512,1024]{1,0:T(8,128)(2,1)}, bf16[512,1024]{1,0:T(8,128)(2,1)}, bf16[512,1024]{1,0:T(8,128)(2,1)}) custom-call(bf16[512,1024]{1,0:T(8,128)(2,1)} %copy-done.27, bf16[4,128,1024]{2,1,0:T(8,128)(2,1)} %bitcast.336, bf16[1024,1536]{1,0:T(8,128)(2,1)} %all-gather.2.cloned.1.call-done.w_ref), custom_call_target="tpu_custom_call" | custom-call | flops 5242880000 | bytes 1024 | tf_op jit(solution)/shard_map/pallas_call | solution.py:527
  160.5 7.8 %shard_map.210 = bf16[1024,1536]{1,0:T(8,128)(2,1)} custom-call(bf16[512,1024]{1,0:T(8,128)(2,1)} %copy-done.27, bf16[4,128,1024]{2,1,0:T(8,128)(2,1)} %bitcast.337, bf16[512,512]{1,0:T(8,128)(2,1)} %get-tuple-element.114.refs_2_, bf16[512,1024]{1,0:T(8,128)(2,1)} %get-tuple-element.115.refs_3_, ...), custom_call_target="tpu_custom_call" | custom-call | flops 5242880000 | bytes 1024 | tf_op jit(solution)/shard_map/pallas_call | solution.py:579
  168.4 4.0 %collective-permute-done.33.refs_2_ = bf16[128,1024]{1,0:T(8,128)(2,1)S(1)} collective-permute-done((bf16[128,1024]{1,0:T(8,128)(2,1)}, bf16[128,1024]{1,0:T(8,128)(2,1)S(1)}, u32[]{:S(2)}, u32[]{:S(2)}) %collective-permute-start.33) | collective-permute-done | bytes 262176 | tf_op jit(solution)/shard_map/up_xy/ppermute | solution.py:57
  174.9 4.5 %shard_map.211 = (f32[128,1024]{1,0:T(8,128)}, bf16[128,1024]{1,0:T(8,128)(2,1)}, bf16[128,1024]{1,0:T(8,128)(2,1)}, f32[1,1024]{1,0:T(1,128)}) custom-call(f32[128,1024]{1,0:T(8,128)} %copy-done.16, bf16[128,1024]{1,0:T(8,128)(2,1)} %bitcast.339, f32[1,1024]{1,0:T(1,128)} %reshape.654.gain_ref, bf16[1024,1024]{1,0:T(8,128)(2,1)} %bitcast.309, ...), custom_call_target="tpu_custom_call" | custom-call | flops 1048576 | bytes 1024 | tf_op jit(solution)/shard_map/pallas_call | solution.py:495
  193.3 3.4 %collective-permute-start.37 = (bf16[2,128,128]{2,1,0:T(8,128)(2,1)S(1)}, bf16[2,128,128]{2,1,0:T(8,128)(2,1)S(1)}, u32[]{:S(2)}, u32[]{:S(2)}) collective-permute-start(bf16[2,128,128]{2,1,0:T(8,128)(2,1)S(1)} %pad_maximum_fusion.16), channel_id=1, source_target_pairs={{0,16},{4,20},{8,24},{12,28},{16,0},{20,4},{24,8},{28,12},{1,17},{... | collective-permute-start | bytes 196616 | tf_op jit(solution)/shard_map/merged_z/ppermute | solution.py:45
  197.0 6.8 %collective-permute-done.38 = bf16[2,128,128]{2,1,0:T(8,128)(2,1)S(1)} collective-permute-done((bf16[2,128,128]{2,1,0:T(8,128)(2,1)S(1)}, bf16[2,128,128]{2,1,0:T(8,128)(2,1)S(1)}, u32[]{:S(2)}, u32[]{:S(2)}) %collective-permute-start.38) | collective-permute-done | bytes 65568 | tf_op jit(solution)/shard_map/merged_z/ppermute | solution.py:45
  207.9 11.7 %shard_map.213 = (bf16[512,1024]{1,0:T(8,128)(2,1)}, bf16[512,1024]{1,0:T(8,128)(2,1)}, bf16[1024,384]{1,0:T(8,128)(2,1)}, f32[2,2]{1,0:T(2,128)}, bf16[4,272,384]{2,1,0:T(8,128)(2,1)S(1)}) custom-call(s32[1]{0:T(128)} %bitcast.97.refs_0_, bf16[512,1024]{1,0:T(8,128)(2,1)} %bitcast.313, bf16[512,1024]{1,0:T(8,128)(2,1)} %collective-permute-done.15.far_ref.refs_2_, ...), custom_call_target="tpu_custom_call" | custom-call | flops 4194304000 | bytes 1024 | tf_op jit(solution)/shard_map/pallas_call | solution.py:467
  225.9 3.3 %collective-permute-done.55 = bf16[1,128,1024]{2,1,0:T(8,128)(2,1)S(1)} collective-permute-done((bf16[1,128,1024]{2,1,0:T(8,128)(2,1)S(1)}, bf16[1,128,1024]{2,1,0:T(8,128)(2,1)S(1)}, u32[]{:S(2)}, u32[]{:S(2)}) %collective-permute-start.55) | collective-permute-done | bytes 262176 | tf_op jit(solution)/shard_map/w_out_x/ppermute | solution.py:48
  243.4 4.6 %collective-permute-start.57 = (bf16[1,32,1024]{2,1,0:T(8,128)(2,1)S(1)}, bf16[1,32,1024]{2,1,0:T(8,128)(2,1)S(1)}, u32[]{:S(2)}, u32[]{:S(2)}) collective-permute-start(bf16[1,32,1024]{2,1,0:T(8,128)(2,1)S(1)} %fusion.18), channel_id=1, source_target_pairs={{0,16},{4,20},{8,24},{12,28},{16,0},{20,4},{24,8},{28,12},{1,17},{... | collective-permute-start | bytes 196616 | tf_op jit(solution)/shard_map/w_out_z/ppermute | solution.py:45
  249.2 4.0 %collective-permute-start.49 = (bf16[1,128,1024]{2,1,0:T(8,128)(2,1)S(1)}, bf16[1,128,1024]{2,1,0:T(8,128)(2,1)S(1)}, u32[]{:S(2)}, u32[]{:S(2)}) collective-permute-start(bf16[1,128,1024]{2,1,0:T(8,128)(2,1)S(1)} %fusion.9), channel_id=1, source_target_pairs={{0,16},{4,20},{8,24},{12,28},{16,0},{20,4},{24,8},{28,12},{1,17},{... | collective-permute-start | bytes 786440 | tf_op jit(solution)/shard_map/input_z/ppermute | solution.py:45
  255.9 3.2 %collective-permute-start.53 = (bf16[80,384]{1,0:T(8,128)(2,1)S(1)}, bf16[80,384]{1,0:T(8,128)(2,1)S(1)}, u32[]{:S(2)}, u32[]{:S(2)}) collective-permute-start(bf16[80,384]{1,0:T(8,128)(2,1)S(1)} %get-tuple-element.227), channel_id=1, source_target_pairs={{0,24},{4,28},{8,16},{12,20},{16,8},{20,12},{24,0},{28,4},{1,25},{... | collective-permute-start | bytes 184328 | tf_op jit(solution)/shard_map/grad_qkv_z/ppermute | solution.py:45
  261.6 5.7 %collective-permute-done.49 = bf16[1,128,1024]{2,1,0:T(8,128)(2,1)S(1)} collective-permute-done((bf16[1,128,1024]{2,1,0:T(8,128)(2,1)S(1)}, bf16[1,128,1024]{2,1,0:T(8,128)(2,1)S(1)}, u32[]{:S(2)}, u32[]{:S(2)}) %collective-permute-start.49) | collective-permute-done | bytes 262176 | tf_op jit(solution)/shard_map/input_z/ppermute | solution.py:45
  (391 shorter events, 136.1 us)
Async XLA Ops:
  7.2 132.8 %all-gather.2.cloned.1.call-start = ((), (), s32[]{:S(2)}) async-start(), calls=%async_computation.1 | async-start | bytes 3932160 | tf_op jit(solution)/shard_map/all_gather | solution.py:880
  9.5 30.4 %collective-permute-start = (bf16[128,1024]{1,0:T(8,128)(2,1)S(1)}, bf16[128,1024]{1,0:T(8,128)(2,1)S(1)}, u32[]{:S(2)}, u32[]{:S(2)}) collective-permute-start(bf16[128,1024]{1,0:T(8,128)(2,1)S(1)} %fusion.3), channel_id=1, source_target_pairs={{0,0},{1,4},{2,2},{3,6},{4,1},{5,5},{6,3},{7,7},{8,8},{9,12},{10,1... | collective-permute-start | bytes 786440 | tf_op jit(solution)/shard_map/tokens_turn/ppermute | solution.py:71
  20.8 32.7 %collective-permute-start.14 = (bf16[1,128,1024]{2,1,0:T(8,128)(2,1)S(1)}, bf16[1,128,1024]{2,1,0:T(8,128)(2,1)}, u32[]{:S(2)}, u32[]{:S(2)}) collective-permute-start(bf16[1,128,1024]{2,1,0:T(8,128)(2,1)S(1)} %copy-done.28), channel_id=1, source_target_pairs={{0,4},{4,0},{8,12},{12,8},{16,20},{20,16},{24,28},{28,24},{1,5},{5... | collective-permute-start | bytes 786440 | tf_op jit(solution)/shard_map/cotangent_x/ppermute | solution.py:48
  31.2 25.3 %collective-permute-start.9 = (bf16[272,384]{1,0:T(8,128)(2,1)}, bf16[272,384]{1,0:T(8,128)(2,1)S(1)}, u32[]{:S(2)}, u32[]{:S(2)}) collective-permute-start(bf16[272,384]{1,0:T(8,128)(2,1)} %get-tuple-element.232), channel_id=1, source_target_pairs={{0,6},{1,7},{2,4},{3,5},{4,2},{5,3},{6,0},{7,1},{8,14},{9,15},{10,... | collective-permute-start | bytes 626696 | tf_op jit(solution)/shard_map/qkv_xy/ppermute | solution.py:60
  33.9 23.5 %collective-permute-start.8 = (bf16[272,384]{1,0:T(8,128)(2,1)}, bf16[272,384]{1,0:T(8,128)(2,1)S(1)}, u32[]{:S(2)}, u32[]{:S(2)}) collective-permute-start(bf16[272,384]{1,0:T(8,128)(2,1)} %get-tuple-element.232), channel_id=1, source_target_pairs={{0,2},{1,3},{2,0},{3,1},{4,6},{5,7},{6,4},{7,5},{8,10},{9,11},{10,... | collective-permute-start | bytes 626696 | tf_op jit(solution)/shard_map/qkv_xy/ppermute | solution.py:57
  39.9 13.4 %collective-permute-start.1 = (bf16[1,128,1024]{2,1,0:T(8,128)(2,1)S(1)}, bf16[1,128,1024]{2,1,0:T(8,128)(2,1)S(1)}, u32[]{:S(2)}, u32[]{:S(2)}) collective-permute-start(bf16[1,128,1024]{2,1,0:T(8,128)(2,1)S(1)} %bitcast.352), channel_id=1, source_target_pairs={{0,16},{4,20},{8,24},{12,28},{16,0},{20,4},{24,8},{28,12},{1,17},{... | collective-permute-start | bytes 786440 | tf_op jit(solution)/shard_map/tokens_z/ppermute | solution.py:45
  46.3 15.5 %collective-permute-start.13 = (bf16[2,128,1024]{2,1,0:T(8,128)(2,1)S(1)}, bf16[2,128,1024]{2,1,0:T(8,128)(2,1)S(1)}, u32[]{:S(2)}, u32[]{:S(2)}) collective-permute-start(bf16[2,128,1024]{2,1,0:T(8,128)(2,1)S(1)} %pad_maximum_fusion.7), channel_id=1, source_target_pairs={{0,2},{1,3},{2,0},{3,1},{4,6},{5,7},{6,4},{7,5},{8,10},{9,11},{10,... | collective-permute-start | bytes 1572872 | tf_op jit(solution)/shard_map/out_xy/ppermute | solution.py:57
  72.0 162.6 %reduce-scatter.2.cloned.1.call-start = ((), (), s32[]{:S(2)}) async-start(), calls=%async_computation.2 | async-start | bytes 3932160 | tf_op jit(solution)/shard_map/reduce_scatter | solution.py:963
  72.1 28.8 %collective-permute-start.19 = (bf16[1,2,128,1024]{3,2,1,0:T(8,128)(2,1)}, bf16[1,2,128,1024]{3,2,1,0:T(8,128)(2,1)S(1)}, u32[]{:S(2)}, u32[]{:S(2)}) collective-permute-start(bf16[1,2,128,1024]{3,2,1,0:T(8,128)(2,1)} %bitcast.333), channel_id=1, source_target_pairs={{0,2},{1,3},{2,0},{3,1},{4,6},{5,7},{6,4},{7,5},{8,10},{9,11},{10,... | collective-permute-start | bytes 1572872 | tf_op jit(solution)/shard_map/cotangent_y/ppermute | solution.py:57
  73.6 29.8 %collective-permute-start.22 = (bf16[4,128,1024]{2,1,0:T(8,128)(2,1)}, bf16[4,128,1024]{2,1,0:T(8,128)(2,1)}, u32[]{:S(2)}, u32[]{:S(2)}) collective-permute-start(bf16[4,128,1024]{2,1,0:T(8,128)(2,1)} %pad_maximum_fusion.1), channel_id=1, source_target_pairs={{0,1},{1,0},{2,3},{3,2},{4,5},{5,4},{6,7},{7,6},{8,9},{9,8},{10,11... | collective-permute-start | bytes 3145736 | tf_op jit(solution)/shard_map/out_core/ppermute | solution.py:51
  87.0 13.8 %collective-permute-start.16 = (bf16[2,128,128]{2,1,0:T(8,128)(2,1)S(1)}, bf16[2,128,128]{2,1,0:T(8,128)(2,1)S(1)}, u32[]{:S(2)}, u32[]{:S(2)}) collective-permute-start(bf16[2,128,128]{2,1,0:T(8,128)(2,1)S(1)} %get-tuple-element.226), channel_id=1, source_target_pairs={{0,16},{4,20},{8,24},{12,28},{16,0},{20,4},{24,8},{28,12},{1,17},{... | collective-permute-start | bytes 196616 | tf_op jit(solution)/shard_map/attended_z/ppermute | solution.py:45
  147.1 26.0 %collective-permute-start.29 = (bf16[512,1024]{1,0:T(8,128)(2,1)}, bf16[512,1024]{1,0:T(8,128)(2,1)S(1)}, u32[]{:S(2)}, u32[]{:S(2)}) collective-permute-start(bf16[512,1024]{1,0:T(8,128)(2,1)} %get-tuple-element.109), channel_id=1, source_target_pairs={{0,1},{1,0},{2,3},{3,2},{4,5},{5,4},{6,7},{7,6},{8,9},{9,8},{10,11... | collective-permute-start | bytes 3145736 | tf_op jit(solution)/shard_map/down_core/ppermute | solution.py:51
  158.5 13.8 %collective-permute-start.33 = (bf16[128,1024]{1,0:T(8,128)(2,1)}, bf16[128,1024]{1,0:T(8,128)(2,1)S(1)}, u32[]{:S(2)}, u32[]{:S(2)}) collective-permute-start(bf16[128,1024]{1,0:T(8,128)(2,1)} %get-tuple-element.203), channel_id=1, source_target_pairs={{0,2},{1,3},{2,0},{3,1},{4,6},{5,7},{6,4},{7,5},{8,10},{9,11},{10,... | collective-permute-start | bytes 786440 | tf_op jit(solution)/shard_map/up_xy/ppermute | solution.py:57
  173.4 16.1 %collective-permute-start.31 = (bf16[1,2,128,1024]{3,2,1,0:T(8,128)(2,1)S(1)}, bf16[1,2,128,1024]{3,2,1,0:T(8,128)(2,1)}, u32[]{:S(2)}, u32[]{:S(2)}) collective-permute-start(bf16[1,2,128,1024]{3,2,1,0:T(8,128)(2,1)S(1)} %bitcast.350), channel_id=1, source_target_pairs={{0,2},{1,3},{2,0},{3,1},{4,6},{5,7},{6,4},{7,5},{8,10},{9,11},{10,... | collective-permute-start | bytes 1572872 | tf_op jit(solution)/shard_map/down_y/ppermute | solution.py:57
  190.5 16.6 %collective-permute-start.41 = (bf16[128,1024]{1,0:T(8,128)(2,1)S(1)}, bf16[128,1024]{1,0:T(8,128)(2,1)S(1)}, u32[]{:S(2)}, u32[]{:S(2)}) collective-permute-start(bf16[128,1024]{1,0:T(8,128)(2,1)S(1)} %fusion.5), channel_id=1, source_target_pairs={{0,4},{4,0},{8,12},{12,8},{16,20},{20,16},{24,28},{28,24},{1,5},{5... | collective-permute-start | bytes 786440 | tf_op jit(solution)/shard_map/down_x/ppermute | solution.py:48
  205.6 14.0 %collective-permute-start.42 = (bf16[1,2,128,1024]{3,2,1,0:T(8,128)(2,1)S(1)}, bf16[1,2,128,1024]{3,2,1,0:T(8,128)(2,1)S(1)}, u32[]{:S(2)}, u32[]{:S(2)}) collective-permute-start(bf16[1,2,128,1024]{3,2,1,0:T(8,128)(2,1)S(1)} %fusion), channel_id=1, source_target_pairs={{0,2},{1,3},{2,0},{3,1},{4,6},{5,7},{6,4},{7,5},{8,10},{9,11},{10,... | collective-permute-start | bytes 1572872 | tf_op jit(solution)/shard_map/w_out_y/ppermute | solution.py:57
  222.4 14.2 %collective-permute-start.46 = (bf16[272,384]{1,0:T(8,128)(2,1)}, bf16[272,384]{1,0:T(8,128)(2,1)}, u32[]{:S(2)}, u32[]{:S(2)}) collective-permute-start(bf16[272,384]{1,0:T(8,128)(2,1)} %get-tuple-element.212), channel_id=1, source_target_pairs={{0,4},{4,0},{8,12},{12,8},{16,20},{20,16},{24,28},{28,24},{1,5},{5... | collective-permute-start | bytes 626696 | tf_op jit(solution)/shard_map/grad_qkv_xy/ppermute | solution.py:48
  223.7 16.6 %collective-permute-start.47 = (bf16[272,384]{1,0:T(8,128)(2,1)}, bf16[272,384]{1,0:T(8,128)(2,1)}, u32[]{:S(2)}, u32[]{:S(2)}) collective-permute-start(bf16[272,384]{1,0:T(8,128)(2,1)} %get-tuple-element.211), channel_id=1, source_target_pairs={{0,2},{1,3},{2,0},{3,1},{4,6},{5,7},{6,4},{7,5},{8,10},{9,11},{10,... | collective-permute-start | bytes 626696 | tf_op jit(solution)/shard_map/grad_qkv_xy/ppermute | solution.py:57
  224.5 15.8 %collective-permute-start.48 = (bf16[272,384]{1,0:T(8,128)(2,1)}, bf16[272,384]{1,0:T(8,128)(2,1)}, u32[]{:S(2)}, u32[]{:S(2)}) collective-permute-start(bf16[272,384]{1,0:T(8,128)(2,1)} %get-tuple-element.210), channel_id=1, source_target_pairs={{0,6},{1,7},{2,4},{3,5},{4,2},{5,3},{6,0},{7,1},{8,14},{9,15},{10,... | collective-permute-start | bytes 626696 | tf_op jit(solution)/shard_map/grad_qkv_xy/ppermute | solution.py:60
  231.8 16.3 %collective-permute-start.44 = (bf16[2,128,1024]{2,1,0:T(8,128)(2,1)S(1)}, bf16[2,128,1024]{2,1,0:T(8,128)(2,1)S(1)}, u32[]{:S(2)}, u32[]{:S(2)}) collective-permute-start(bf16[2,128,1024]{2,1,0:T(8,128)(2,1)S(1)} %bitcast.351), channel_id=1, source_target_pairs={{0,8},{4,12},{8,0},{12,4},{16,24},{20,28},{24,16},{28,20},{1,9},{5... | collective-permute-start | bytes 1572872 | tf_op jit(solution)/shard_map/input_z/ppermute | solution.py:45
  243.4 27.5 %collective-permute-start.57 = (bf16[1,32,1024]{2,1,0:T(8,128)(2,1)S(1)}, bf16[1,32,1024]{2,1,0:T(8,128)(2,1)S(1)}, u32[]{:S(2)}, u32[]{:S(2)}) collective-permute-start(bf16[1,32,1024]{2,1,0:T(8,128)(2,1)S(1)} %fusion.18), channel_id=1, source_target_pairs={{0,16},{4,20},{8,24},{12,28},{16,0},{20,4},{24,8},{28,12},{1,17},{... | collective-permute-start | bytes 196616 | tf_op jit(solution)/shard_map/w_out_z/ppermute | solution.py:45
  249.2 18.1 %collective-permute-start.49 = (bf16[1,128,1024]{2,1,0:T(8,128)(2,1)S(1)}, bf16[1,128,1024]{2,1,0:T(8,128)(2,1)S(1)}, u32[]{:S(2)}, u32[]{:S(2)}) collective-permute-start(bf16[1,128,1024]{2,1,0:T(8,128)(2,1)S(1)} %fusion.9), channel_id=1, source_target_pairs={{0,16},{4,20},{8,24},{12,28},{16,0},{20,4},{24,8},{28,12},{1,17},{... | collective-permute-start | bytes 786440 | tf_op jit(solution)/shard_map/input_z/ppermute | solution.py:45
  254.8 13.8 %collective-permute-start.51 = (bf16[80,384]{1,0:T(8,128)(2,1)S(1)}, bf16[80,384]{1,0:T(8,128)(2,1)S(1)}, u32[]{:S(2)}, u32[]{:S(2)}) collective-permute-start(bf16[80,384]{1,0:T(8,128)(2,1)S(1)} %get-tuple-element.229), channel_id=1, source_target_pairs={{0,8},{4,12},{8,0},{12,4},{16,24},{20,28},{24,16},{28,20},{1,9},{5... | collective-permute-start | bytes 184328 | tf_op jit(solution)/shard_map/grad_qkv_z/ppermute | solution.py:45
  254.8 13.9 %collective-permute-start.52 = (bf16[80,384]{1,0:T(8,128)(2,1)S(1)}, bf16[80,384]{1,0:T(8,128)(2,1)S(1)}, u32[]{:S(2)}, u32[]{:S(2)}) collective-permute-start(bf16[80,384]{1,0:T(8,128)(2,1)S(1)} %get-tuple-element.228), channel_id=1, source_target_pairs={{0,16},{4,20},{8,24},{12,28},{16,0},{20,4},{24,8},{28,12},{1,17},{... | collective-permute-start | bytes 184328 | tf_op jit(solution)/shard_map/grad_qkv_z/ppermute | solution.py:45
  (87 other events, 846.1 us)
Sparse Core Ops, SparseCore 0:
  72.1 67.8 all-gather.1
  172.5 62.1 reduce-scatter.1

commit v5 on v4

--- a/solution.py
+++ b/solution.py
@@ -544,7 +544,7 @@
             pl.BlockSpec((step, width), lambda i: (i, 0)),
             pl.BlockSpec((step, width), lambda i: (i, 0)),
         ),
-        compiler_params=pltpu.CompilerParams(vmem_limit_bytes=58 * 2**20),
+        compiler_params=pltpu.CompilerParams(vmem_limit_bytes=40 * 2**20),
         cost_estimate=pl.CostEstimate(
             flops=5000 << 20, bytes_accessed=2**10, transcendentals=0
         ),
@@ -582,7 +582,7 @@
         out_shape=jax.ShapeDtypeStruct((width, 3 * units), low),
         in_specs=part + part,
         out_specs=pl.BlockSpec((step, 3 * units), lambda i: (i, 0)),
-        compiler_params=pltpu.CompilerParams(vmem_limit_bytes=58 * 2**20),
+        compiler_params=pltpu.CompilerParams(vmem_limit_bytes=40 * 2**20),
         cost_estimate=pl.CostEstimate(
             flops=5000 << 20, bytes_accessed=2**10, transcendentals=0
         ),
@@ -1065,7 +1065,8 @@
             )
             sent.append(with_extra(block, *halves(bias_sum), *halves(gain)))
     depth = grad_w_ffn.shape[0] // 2
-    other = called("grad_ffn_x", at.along_x, pick(at.x, grad_w_ffn[depth:], grad_w_ffn[:depth]))
+    other = lax.dynamic_slice_in_dim(grad_w_ffn, (1 - at.x) * depth, depth, 0)
+    other = called("grad_ffn_x", at.along_x, other)
     upstream_z[-1], other = tied(upstream_z[-1], other)
     upstream_z[-1], sent = tied(upstream_z[-1], sent)
     z_cut = z_cut // 2

time: 292 us -> 288 us (0.986)
  Pallas kernels: 59.9 us -> 52.2 us
  local copies, waits for them, and re-layouts: 19.9 us -> 24.9 us
  starting transfers between devices: 79.1 us -> 75.3 us
  waiting for transfers between devices: 79.2 us -> 82.6 us
    pallas_call x2, Pallas kernels: 13.9 us -> 8.7 us  [feed(): pl.pallas_call(functools.partial(feed_kernel, units), grid=(count // step...]
    ppermute x20, starting transfers between devices: 36.6 us -> 32.8 us  [along_z(): lax.ppermute(value, 'seq', [(i, i ^ 2 * step) for i in range(self.seq_siz...]
    unnamed x127 -> x129, local copies, waits for them, and re-layouts: 8.71 us -> 11.8 us
  transfers between devices with their start and end apart: 60 -> 60, of which waited for: 23 -> 23; matrix products, arithmetic and copies ran while one was open for 15% -> 16% of each run, Pallas kernels for 18% -> 16%
where the time goes in v5:
time: 288 us; the launch traced here: 285 us
  waiting for transfers between devices  82.6 us (29%)
  starting transfers between devices  75.3 us (26%)
  Pallas kernels  52.2 us (18%)
  other arithmetic  31.7 us (11%)
  local copies, waits for them, and re-layouts  24.9 us (9%)
  between operations  15.6 us (5%)
    ppermute x20, waiting for transfers between devices, along_z(): lax.ppermute(value, 'seq', [(i, i ^ 2 * step) for i in range(self.seq_siz...  39 us
    ppermute x20, starting transfers between devices, along_z(): lax.ppermute(value, 'seq', [(i, i ^ 2 * step) for i in range(self.seq_siz...  32.8 us
    unnamed x129, local copies, waits for them, and re-layouts  11.8 us
    pallas_call x1, Pallas kernels, attend_grad(): pl.pallas_call(kernel, out_shape=out_shape, in_specs=in_specs, out_specs=...  11.7 us
    ppermute x8, waiting for transfers between devices, along_xy(): lax.ppermute(value, 'head', [(i, i ^ 2 * dy) for i in range(self.head_siz...  11.6 us
    ppermute x4, starting transfers between devices, along_xy(): lax.ppermute(value, ('seq', 'head'), [(s * self.head_size + h, (s ^ dx) *...  11.2 us
    all_gather x1, waiting for transfers between devices, shards(): lax.all_gather(z_block, 'seq', axis=0, tiled=True, axis_index_groups=at.c...  11 us
    ppermute x10, waiting for transfers between devices, along_x(): lax.ppermute(value, 'seq', [(i, i ^ 1) for i in range(self.seq_size)])  10.5 us
  transfers between devices with their start and end apart: 60, of which 23 were waited for; matrix products, arithmetic and copies ran while one was open for 16% of the time, Pallas kernels for 16%

profile of v5, /device:TPU:0, one launch (start us, length us, event | category | flops | bytes accessed | tf_op | source)
XLA Modules:
  0.0 284.6 jit_solution(12866779983383240300)
XLA Ops:
  13.8 4.3 %collective-permute-start.3 = (bf16[144,384]{1,0:T(8,128)(2,1)S(1)}, bf16[144,384]{1,0:T(8,128)(2,1)S(1)}, u32[]{:S(2)}, u32[]{:S(2)}) collective-permute-start(bf16[144,384]{1,0:T(8,128)(2,1)S(1)} %fusion.23), channel_id=1, source_target_pairs={{0,1},{1,0},{2,3},{3,2},{4,5},{5,4},{6,7},{7,6},{8,9},{9,8},{10,11... | collective-permute-start | bytes 331784 | tf_op jit(solution)/shard_map/qkv_core/ppermute | solution.py:51
  39.9 3.2 %collective-permute-start.1 = (bf16[1,128,1024]{2,1,0:T(8,128)(2,1)S(1)}, bf16[1,128,1024]{2,1,0:T(8,128)(2,1)S(1)}, u32[]{:S(2)}, u32[]{:S(2)}) collective-permute-start(bf16[1,128,1024]{2,1,0:T(8,128)(2,1)S(1)} %bitcast.351), channel_id=1, source_target_pairs={{0,16},{4,20},{8,24},{12,28},{16,0},{20,4},{24,8},{28,12},{1,17},{... | collective-permute-start | bytes 786440 | tf_op jit(solution)/shard_map/tokens_z/ppermute | solution.py:45
  43.1 3.1 %collective-permute-done.12 = bf16[1,128,1024]{2,1,0:T(8,128)(2,1)S(1)} collective-permute-done((bf16[1,128,1024]{2,1,0:T(8,128)(2,1)S(1)}, bf16[1,128,1024]{2,1,0:T(8,128)(2,1)S(1)}, u32[]{:S(2)}, u32[]{:S(2)}) %collective-permute-start.12) | collective-permute-done | bytes 262176 | tf_op jit(solution)/shard_map/out_xy/ppermute | solution.py:48
  47.9 5.4 %collective-permute-done.1 = bf16[1,128,1024]{2,1,0:T(8,128)(2,1)S(1)} collective-permute-done((bf16[1,128,1024]{2,1,0:T(8,128)(2,1)S(1)}, bf16[1,128,1024]{2,1,0:T(8,128)(2,1)S(1)}, u32[]{:S(2)}, u32[]{:S(2)}) %collective-permute-start.1) | collective-permute-done | bytes 262176 | tf_op jit(solution)/shard_map/tokens_z/ppermute | solution.py:45
  57.4 4.0 %collective-permute-done.7 = bf16[272,384]{1,0:T(8,128)(2,1)S(1)} collective-permute-done((bf16[272,384]{1,0:T(8,128)(2,1)}, bf16[272,384]{1,0:T(8,128)(2,1)S(1)}, u32[]{:S(2)}, u32[]{:S(2)}) %collective-permute-start.7) | collective-permute-done | bytes 208928 | tf_op jit(solution)/shard_map/qkv_xy/ppermute | solution.py:48
  63.0 3.4 %collective-permute-done.2.second_ref = bf16[2,128,1024]{2,1,0:T(8,128)(2,1)S(1)} collective-permute-done((bf16[2,128,1024]{2,1,0:T(8,128)(2,1)S(1)}, bf16[2,128,1024]{2,1,0:T(8,128)(2,1)S(1)}, u32[]{:S(2)}, u32[]{:S(2)}) %collective-permute-start.2) | collective-permute-done | bytes 524320 | tf_op jit(solution)/shard_map/tokens_z/ppermute | solution.py:45
  73.9 9.0 %shard_map.206 = (bf16[2,1024,128]{2,1,0:T(8,128)(2,1)S(1)}, bf16[2,1024,128]{2,1,0:T(8,128)(2,1)S(1)}, bf16[2,1024,128]{2,1,0:T(8,128)(2,1)S(1)}, bf16[1024,128]{1,0:T(8,128)(2,1)S(1)}) custom-call(f32[2,2]{1,0:T(2,128)S(1)} %pad_maximum_fusion.25.bias_ref, bf16[512,1024]{1,0:T(8,128)(2,1)S(1)} %bitcast.314, ...), custom_call_target="tpu_custom_call" | custom-call | flops 1048576 | bytes 1048576 | tf_op jit(solution)/shard_map/pallas_call | solution.py:306
  89.8 3.7 %collective-permute-done.18 = bf16[2,128,128]{2,1,0:T(8,128)(2,1)S(1)} collective-permute-done((bf16[2,128,128]{2,1,0:T(8,128)(2,1)S(1)}, bf16[2,128,128]{2,1,0:T(8,128)(2,1)S(1)}, u32[]{:S(2)}, u32[]{:S(2)}) %collective-permute-start.18) | collective-permute-done | bytes 65568 | tf_op jit(solution)/shard_map/attended_z/ppermute | solution.py:45
  96.2 4.6 %collective-permute-done.16 = bf16[2,128,128]{2,1,0:T(8,128)(2,1)S(1)} collective-permute-done((bf16[2,128,128]{2,1,0:T(8,128)(2,1)S(1)}, bf16[2,128,128]{2,1,0:T(8,128)(2,1)S(1)}, u32[]{:S(2)}, u32[]{:S(2)}) %collective-permute-start.16) | collective-permute-done | bytes 65568 | tf_op jit(solution)/shard_map/attended_z/ppermute | solution.py:45
  106.8 6.2 %collective-permute-start.25 = (bf16[128,1024]{1,0:T(8,128)(2,1)S(1)}, bf16[128,1024]{1,0:T(8,128)(2,1)S(1)}, u32[]{:S(2)}, u32[]{:S(2)}) collective-permute-start(bf16[128,1024]{1,0:T(8,128)(2,1)S(1)} %multiply_convert_fusion), channel_id=1, source_target_pairs={{0,6},{1,7},{2,4},{3,5},{4,2},{5,3},{6,0},{7,1},{8,14},{9,15},{10,... | collective-permute-start | bytes 786440 | tf_op jit(solution)/shard_map/normed_xy/ppermute | solution.py:60
  114.2 5.8 %collective-permute-done.25 = bf16[128,1024]{1,0:T(8,128)(2,1)S(1)} collective-permute-done((bf16[128,1024]{1,0:T(8,128)(2,1)S(1)}, bf16[128,1024]{1,0:T(8,128)(2,1)S(1)}, u32[]{:S(2)}, u32[]{:S(2)}) %collective-permute-start.25) | collective-permute-done | bytes 262176 | tf_op jit(solution)/shard_map/normed_xy/ppermute | solution.py:60
  119.9 5.3 %collective-permute-done.24 = bf16[128,1024]{1,0:T(8,128)(2,1)S(1)} collective-permute-done((bf16[128,1024]{1,0:T(8,128)(2,1)S(1)}, bf16[128,1024]{1,0:T(8,128)(2,1)S(1)}, u32[]{:S(2)}, u32[]{:S(2)}) %collective-permute-start.24) | collective-permute-done | bytes 262176 | tf_op jit(solution)/shard_map/normed_xy/ppermute | solution.py:57
  129.0 11.0 %all-gather.2.cloned.1.call-done.w_ref = bf16[1024,1536]{1,0:T(8,128)(2,1)} async-done(((bf16[256,1536]{1,0:T(8,128)(2,1)}), bf16[1024,1536]{1,0:T(8,128)(2,1)}) %all-gather.2.cloned.1.call-update) | async-done | bytes 3145744 | tf_op jit(solution)/shard_map/all_gather | solution.py:880
  143.1 4.8 %shard_map.209 = (bf16[512,512]{1,0:T(8,128)(2,1)S(1)}, bf16[512,1024]{1,0:T(8,128)(2,1)S(1)}, bf16[512,1024]{1,0:T(8,128)(2,1)S(1)}, bf16[512,1024]{1,0:T(8,128)(2,1)}) custom-call(bf16[512,1024]{1,0:T(8,128)(2,1)S(1)} %copy-done.14, bf16[4,128,1024]{2,1,0:T(8,128)(2,1)S(1)} %collective-permute-done.28.grads_ref.refs_5_, bf16[1024,1536]{1,0:T(8,128)(2,1)S(1)} %copy-done.10), custom_call_target="tpu_custom_call" | custom-call | flops 5242880000 | bytes 1024 | tf_op jit(solution)/shard_map/pallas_call | solution.py:527
  148.4 4.0 %shard_map.208 = (bf16[512,512]{1,0:T(8,128)(2,1)S(1)}, bf16[512,1024]{1,0:T(8,128)(2,1)S(1)}, bf16[512,1024]{1,0:T(8,128)(2,1)S(1)}, bf16[512,1024]{1,0:T(8,128)(2,1)S(1)}) custom-call(bf16[512,1024]{1,0:T(8,128)(2,1)S(1)} %pad_maximum_fusion.2.tokens_ref.refs_0_, bf16[4,128,1024]{2,1,0:T(8,128)(2,1)S(1)} %bitcast.319, bf16[1024,1536]{1,0:T(8,128)(2,1)S(1)} %copy-done.10), custom_call_target="tpu_custom_call" | custom-call | flops 5242880000 | bytes 1024 | tf_op jit(solution)/shard_map/pallas_call | solution.py:527
  157.1 5.6 %shard_map.210 = bf16[1024,1536]{1,0:T(8,128)(2,1)} custom-call(bf16[512,1024]{1,0:T(8,128)(2,1)S(1)} %pad_maximum_fusion.2.tokens_ref.refs_0_, bf16[4,128,1024]{2,1,0:T(8,128)(2,1)S(1)} %bitcast.320, bf16[512,512]{1,0:T(8,128)(2,1)S(1)} %get-tuple-element.114.refs_2_, bf16[512,1024]{1,0:T(8,128)(2,1)S(1)} %get-tuple-element.115.refs_3_, ...), custom_call_target="tpu_custom_call" | custom-call | flops 5242880000 | bytes 1024 | tf_op jit(solution)/shard_map/pallas_call | solution.py:579
  163.1 5.8 %collective-permute-done.33.refs_2_ = bf16[128,1024]{1,0:T(8,128)(2,1)} collective-permute-done((bf16[128,1024]{1,0:T(8,128)(2,1)}, bf16[128,1024]{1,0:T(8,128)(2,1)}, u32[]{:S(2)}, u32[]{:S(2)}) %collective-permute-start.33) | collective-permute-done | bytes 262176 | tf_op jit(solution)/shard_map/up_xy/ppermute | solution.py:57
  172.5 4.2 %shard_map.211 = (f32[128,1024]{1,0:T(8,128)}, bf16[128,1024]{1,0:T(8,128)(2,1)}, bf16[128,1024]{1,0:T(8,128)(2,1)}, f32[1,1024]{1,0:T(1,128)}) custom-call(f32[128,1024]{1,0:T(8,128)} %copy-done.21, bf16[128,1024]{1,0:T(8,128)(2,1)} %bitcast.339, f32[1,1024]{1,0:T(1,128)} %reshape.654.gain_ref, bf16[1024,1024]{1,0:T(8,128)(2,1)} %bitcast.309, ...), custom_call_target="tpu_custom_call" | custom-call | flops 1048576 | bytes 1024 | tf_op jit(solution)/shard_map/pallas_call | solution.py:495
  180.9 3.4 %collective-permute-start.36 = (bf16[128,512]{1,0:T(8,128)(2,1)S(1)}, bf16[128,512]{1,0:T(8,128)(2,1)S(1)}, u32[]{:S(2)}, u32[]{:S(2)}) collective-permute-start(bf16[128,512]{1,0:T(8,128)(2,1)S(1)} %slice.458), channel_id=1, source_target_pairs={{0,1},{1,0},{2,3},{3,2},{4,5},{5,4},{6,7},{7,6},{8,9},{9,8},{10,11... | collective-permute-start | bytes 393224 | tf_op jit(solution)/shard_map/merged_core/ppermute | solution.py:51
  191.2 3.9 %collective-permute-start.37 = (bf16[2,128,128]{2,1,0:T(8,128)(2,1)S(1)}, bf16[2,128,128]{2,1,0:T(8,128)(2,1)S(1)}, u32[]{:S(2)}, u32[]{:S(2)}) collective-permute-start(bf16[2,128,128]{2,1,0:T(8,128)(2,1)S(1)} %pad_maximum_fusion.16), channel_id=1, source_target_pairs={{0,16},{4,20},{8,24},{12,28},{16,0},{20,4},{24,8},{28,12},{1,17},{... | collective-permute-start | bytes 196616 | tf_op jit(solution)/shard_map/merged_z/ppermute | solution.py:45
  195.4 7.2 %collective-permute-done.38 = bf16[2,128,128]{2,1,0:T(8,128)(2,1)S(1)} collective-permute-done((bf16[2,128,128]{2,1,0:T(8,128)(2,1)S(1)}, bf16[2,128,128]{2,1,0:T(8,128)(2,1)S(1)}, u32[]{:S(2)}, u32[]{:S(2)}) %collective-permute-start.38) | collective-permute-done | bytes 65568 | tf_op jit(solution)/shard_map/merged_z/ppermute | solution.py:45
  204.2 11.7 %shard_map.213 = (bf16[512,1024]{1,0:T(8,128)(2,1)}, bf16[512,1024]{1,0:T(8,128)(2,1)}, bf16[1024,384]{1,0:T(8,128)(2,1)}, f32[2,2]{1,0:T(2,128)}, bf16[4,272,384]{2,1,0:T(8,128)(2,1)S(1)}) custom-call(s32[1]{0:T(128)} %bitcast.97.refs_0_, bf16[512,1024]{1,0:T(8,128)(2,1)} %bitcast.313, bf16[512,1024]{1,0:T(8,128)(2,1)} %collective-permute-done.15.far_ref.refs_2_, ...), custom_call_target="tpu_custom_call" | custom-call | flops 4194304000 | bytes 1024 | tf_op jit(solution)/shard_map/pallas_call | solution.py:467
  242.3 4.0 %collective-permute-done.44 = bf16[2,128,1024]{2,1,0:T(8,128)(2,1)} collective-permute-done((bf16[2,128,1024]{2,1,0:T(8,128)(2,1)}, bf16[2,128,1024]{2,1,0:T(8,128)(2,1)}, u32[]{:S(2)}, u32[]{:S(2)}) %collective-permute-start.44) | collective-permute-done | bytes 524320 | tf_op jit(solution)/shard_map/input_z/ppermute | solution.py:45
  258.4 5.6 %collective-permute-done.49 = bf16[1,128,1024]{2,1,0:T(8,128)(2,1)S(1)} collective-permute-done((bf16[1,128,1024]{2,1,0:T(8,128)(2,1)S(1)}, bf16[1,128,1024]{2,1,0:T(8,128)(2,1)S(1)}, u32[]{:S(2)}, u32[]{:S(2)}) %collective-permute-start.49) | collective-permute-done | bytes 262176 | tf_op jit(solution)/shard_map/input_z/ppermute | solution.py:45
  (393 shorter events, 140.0 us)
Async XLA Ops:
  7.2 132.8 %all-gather.2.cloned.1.call-start = ((), (), s32[]{:S(2)}) async-start(), calls=%async_computation.1 | async-start | bytes 3932160 | tf_op jit(solution)/shard_map/all_gather | solution.py:880
  9.5 30.4 %collective-permute-start = (bf16[128,1024]{1,0:T(8,128)(2,1)S(1)}, bf16[128,1024]{1,0:T(8,128)(2,1)S(1)}, u32[]{:S(2)}, u32[]{:S(2)}) collective-permute-start(bf16[128,1024]{1,0:T(8,128)(2,1)S(1)} %fusion.3), channel_id=1, source_target_pairs={{0,0},{1,4},{2,2},{3,6},{4,1},{5,5},{6,3},{7,7},{8,8},{9,12},{10,1... | collective-permute-start | bytes 786440 | tf_op jit(solution)/shard_map/tokens_turn/ppermute | solution.py:71
  20.8 32.7 %collective-permute-start.14 = (bf16[1,128,1024]{2,1,0:T(8,128)(2,1)S(1)}, bf16[1,128,1024]{2,1,0:T(8,128)(2,1)}, u32[]{:S(2)}, u32[]{:S(2)}) collective-permute-start(bf16[1,128,1024]{2,1,0:T(8,128)(2,1)S(1)} %copy-done.31), channel_id=1, source_target_pairs={{0,4},{4,0},{8,12},{12,8},{16,20},{20,16},{24,28},{28,24},{1,5},{5... | collective-permute-start | bytes 786440 | tf_op jit(solution)/shard_map/cotangent_x/ppermute | solution.py:48
  31.2 25.3 %collective-permute-start.9 = (bf16[272,384]{1,0:T(8,128)(2,1)}, bf16[272,384]{1,0:T(8,128)(2,1)S(1)}, u32[]{:S(2)}, u32[]{:S(2)}) collective-permute-start(bf16[272,384]{1,0:T(8,128)(2,1)} %get-tuple-element.232), channel_id=1, source_target_pairs={{0,6},{1,7},{2,4},{3,5},{4,2},{5,3},{6,0},{7,1},{8,14},{9,15},{10,... | collective-permute-start | bytes 626696 | tf_op jit(solution)/shard_map/qkv_xy/ppermute | solution.py:60
  33.9 23.5 %collective-permute-start.8 = (bf16[272,384]{1,0:T(8,128)(2,1)}, bf16[272,384]{1,0:T(8,128)(2,1)S(1)}, u32[]{:S(2)}, u32[]{:S(2)}) collective-permute-start(bf16[272,384]{1,0:T(8,128)(2,1)} %get-tuple-element.232), channel_id=1, source_target_pairs={{0,2},{1,3},{2,0},{3,1},{4,6},{5,7},{6,4},{7,5},{8,10},{9,11},{10,... | collective-permute-start | bytes 626696 | tf_op jit(solution)/shard_map/qkv_xy/ppermute | solution.py:57
  39.9 13.4 %collective-permute-start.1 = (bf16[1,128,1024]{2,1,0:T(8,128)(2,1)S(1)}, bf16[1,128,1024]{2,1,0:T(8,128)(2,1)S(1)}, u32[]{:S(2)}, u32[]{:S(2)}) collective-permute-start(bf16[1,128,1024]{2,1,0:T(8,128)(2,1)S(1)} %bitcast.351), channel_id=1, source_target_pairs={{0,16},{4,20},{8,24},{12,28},{16,0},{20,4},{24,8},{28,12},{1,17},{... | collective-permute-start | bytes 786440 | tf_op jit(solution)/shard_map/tokens_z/ppermute | solution.py:45
  46.3 15.5 %collective-permute-start.13 = (bf16[2,128,1024]{2,1,0:T(8,128)(2,1)S(1)}, bf16[2,128,1024]{2,1,0:T(8,128)(2,1)S(1)}, u32[]{:S(2)}, u32[]{:S(2)}) collective-permute-start(bf16[2,128,1024]{2,1,0:T(8,128)(2,1)S(1)} %pad_maximum_fusion.7), channel_id=1, source_target_pairs={{0,2},{1,3},{2,0},{3,1},{4,6},{5,7},{6,4},{7,5},{8,10},{9,11},{10,... | collective-permute-start | bytes 1572872 | tf_op jit(solution)/shard_map/out_xy/ppermute | solution.py:57
  72.0 159.8 %reduce-scatter.2.cloned.1.call-start = ((), (), s32[]{:S(2)}) async-start(), calls=%async_computation.2 | async-start | bytes 3932160 | tf_op jit(solution)/shard_map/reduce_scatter | solution.py:963
  72.0 28.8 %collective-permute-start.19 = (bf16[1,2,128,1024]{3,2,1,0:T(8,128)(2,1)}, bf16[1,2,128,1024]{3,2,1,0:T(8,128)(2,1)S(1)}, u32[]{:S(2)}, u32[]{:S(2)}) collective-permute-start(bf16[1,2,128,1024]{3,2,1,0:T(8,128)(2,1)} %bitcast.336), channel_id=1, source_target_pairs={{0,2},{1,3},{2,0},{3,1},{4,6},{5,7},{6,4},{7,5},{8,10},{9,11},{10,... | collective-permute-start | bytes 1572872 | tf_op jit(solution)/shard_map/cotangent_y/ppermute | solution.py:57
  73.6 29.8 %collective-permute-start.22 = (bf16[4,128,1024]{2,1,0:T(8,128)(2,1)}, bf16[4,128,1024]{2,1,0:T(8,128)(2,1)}, u32[]{:S(2)}, u32[]{:S(2)}) collective-permute-start(bf16[4,128,1024]{2,1,0:T(8,128)(2,1)} %pad_maximum_fusion.1), channel_id=1, source_target_pairs={{0,1},{1,0},{2,3},{3,2},{4,5},{5,4},{6,7},{7,6},{8,9},{9,8},{10,11... | collective-permute-start | bytes 3145736 | tf_op jit(solution)/shard_map/out_core/ppermute | solution.py:51
  87.0 13.8 %collective-permute-start.16 = (bf16[2,128,128]{2,1,0:T(8,128)(2,1)S(1)}, bf16[2,128,128]{2,1,0:T(8,128)(2,1)S(1)}, u32[]{:S(2)}, u32[]{:S(2)}) collective-permute-start(bf16[2,128,128]{2,1,0:T(8,128)(2,1)S(1)} %get-tuple-element.226), channel_id=1, source_target_pairs={{0,16},{4,20},{8,24},{12,28},{16,0},{20,4},{24,8},{28,12},{1,17},{... | collective-permute-start | bytes 196616 | tf_op jit(solution)/shard_map/attended_z/ppermute | solution.py:45
  147.9 21.8 %collective-permute-start.29 = (bf16[512,1024]{1,0:T(8,128)(2,1)}, bf16[512,1024]{1,0:T(8,128)(2,1)}, u32[]{:S(2)}, u32[]{:S(2)}) collective-permute-start(bf16[512,1024]{1,0:T(8,128)(2,1)} %get-tuple-element.109), channel_id=1, source_target_pairs={{0,1},{1,0},{2,3},{3,2},{4,5},{5,4},{6,7},{7,6},{8,9},{9,8},{10,11... | collective-permute-start | bytes 3145736 | tf_op jit(solution)/shard_map/down_core/ppermute | solution.py:51
  155.1 13.9 %collective-permute-start.33 = (bf16[128,1024]{1,0:T(8,128)(2,1)}, bf16[128,1024]{1,0:T(8,128)(2,1)}, u32[]{:S(2)}, u32[]{:S(2)}) collective-permute-start(bf16[128,1024]{1,0:T(8,128)(2,1)} %get-tuple-element.203), channel_id=1, source_target_pairs={{0,2},{1,3},{2,0},{3,1},{4,6},{5,7},{6,4},{7,5},{8,10},{9,11},{10,... | collective-permute-start | bytes 786440 | tf_op jit(solution)/shard_map/up_xy/ppermute | solution.py:57
  171.0 16.7 %collective-permute-start.31 = (bf16[1,2,128,1024]{3,2,1,0:T(8,128)(2,1)S(1)}, bf16[1,2,128,1024]{3,2,1,0:T(8,128)(2,1)S(1)}, u32[]{:S(2)}, u32[]{:S(2)}) collective-permute-start(bf16[1,2,128,1024]{3,2,1,0:T(8,128)(2,1)S(1)} %bitcast.350), channel_id=1, source_target_pairs={{0,2},{1,3},{2,0},{3,1},{4,6},{5,7},{6,4},{7,5},{8,10},{9,11},{10,... | collective-permute-start | bytes 1572872 | tf_op jit(solution)/shard_map/down_y/ppermute | solution.py:57
  188.9 14.6 %collective-permute-start.41 = (bf16[128,1024]{1,0:T(8,128)(2,1)S(1)}, bf16[128,1024]{1,0:T(8,128)(2,1)S(1)}, u32[]{:S(2)}, u32[]{:S(2)}) collective-permute-start(bf16[128,1024]{1,0:T(8,128)(2,1)S(1)} %fusion.5), channel_id=1, source_target_pairs={{0,4},{4,0},{8,12},{12,8},{16,20},{20,16},{24,28},{28,24},{1,5},{5... | collective-permute-start | bytes 786440 | tf_op jit(solution)/shard_map/down_x/ppermute | solution.py:48
  202.6 13.8 %collective-permute-start.42 = (bf16[1,2,128,1024]{3,2,1,0:T(8,128)(2,1)S(1)}, bf16[1,2,128,1024]{3,2,1,0:T(8,128)(2,1)S(1)}, u32[]{:S(2)}, u32[]{:S(2)}) collective-permute-start(bf16[1,2,128,1024]{3,2,1,0:T(8,128)(2,1)S(1)} %fusion), channel_id=1, source_target_pairs={{0,2},{1,3},{2,0},{3,1},{4,6},{5,7},{6,4},{7,5},{8,10},{9,11},{10,... | collective-permute-start | bytes 1572872 | tf_op jit(solution)/shard_map/w_out_y/ppermute | solution.py:57
  216.4 13.2 %collective-permute-start.43 = (bf16[512,1024]{1,0:T(8,128)(2,1)}, bf16[512,1024]{1,0:T(8,128)(2,1)}, u32[]{:S(2)}, u32[]{:S(2)}) collective-permute-start(bf16[512,1024]{1,0:T(8,128)(2,1)} %get-tuple-element.138), channel_id=1, source_target_pairs={{0,1},{1,0},{2,3},{3,2},{4,5},{5,4},{6,7},{7,6},{8,9},{9,8},{10,11... | collective-permute-start | bytes 3145736 | tf_op jit(solution)/shard_map/input_core/ppermute | solution.py:51
  219.7 14.0 %collective-permute-start.46 = (bf16[272,384]{1,0:T(8,128)(2,1)}, bf16[272,384]{1,0:T(8,128)(2,1)}, u32[]{:S(2)}, u32[]{:S(2)}) collective-permute-start(bf16[272,384]{1,0:T(8,128)(2,1)} %get-tuple-element.212), channel_id=1, source_target_pairs={{0,4},{4,0},{8,12},{12,8},{16,20},{20,16},{24,28},{28,24},{1,5},{5... | collective-permute-start | bytes 626696 | tf_op jit(solution)/shard_map/grad_qkv_xy/ppermute | solution.py:48
  220.4 16.3 %collective-permute-start.47 = (bf16[272,384]{1,0:T(8,128)(2,1)}, bf16[272,384]{1,0:T(8,128)(2,1)}, u32[]{:S(2)}, u32[]{:S(2)}) collective-permute-start(bf16[272,384]{1,0:T(8,128)(2,1)} %get-tuple-element.211), channel_id=1, source_target_pairs={{0,2},{1,3},{2,0},{3,1},{4,6},{5,7},{6,4},{7,5},{8,10},{9,11},{10,... | collective-permute-start | bytes 626696 | tf_op jit(solution)/shard_map/grad_qkv_xy/ppermute | solution.py:57
  221.3 15.5 %collective-permute-start.48 = (bf16[272,384]{1,0:T(8,128)(2,1)}, bf16[272,384]{1,0:T(8,128)(2,1)}, u32[]{:S(2)}, u32[]{:S(2)}) collective-permute-start(bf16[272,384]{1,0:T(8,128)(2,1)} %get-tuple-element.210), channel_id=1, source_target_pairs={{0,6},{1,7},{2,4},{3,5},{4,2},{5,3},{6,0},{7,1},{8,14},{9,15},{10,... | collective-permute-start | bytes 626696 | tf_op jit(solution)/shard_map/grad_qkv_xy/ppermute | solution.py:60
  231.8 14.6 %collective-permute-start.44 = (bf16[2,128,1024]{2,1,0:T(8,128)(2,1)}, bf16[2,128,1024]{2,1,0:T(8,128)(2,1)}, u32[]{:S(2)}, u32[]{:S(2)}) collective-permute-start(bf16[2,128,1024]{2,1,0:T(8,128)(2,1)} %bitcast.103), channel_id=1, source_target_pairs={{0,8},{4,12},{8,0},{12,4},{16,24},{20,28},{24,16},{28,20},{1,9},{5... | collective-permute-start | bytes 1572872 | tf_op jit(solution)/shard_map/input_z/ppermute | solution.py:45
  239.9 27.6 %collective-permute-start.57 = (bf16[1,32,1024]{2,1,0:T(8,128)(2,1)S(1)}, bf16[1,32,1024]{2,1,0:T(8,128)(2,1)S(1)}, u32[]{:S(2)}, u32[]{:S(2)}) collective-permute-start(bf16[1,32,1024]{2,1,0:T(8,128)(2,1)S(1)} %fusion.18), channel_id=1, source_target_pairs={{0,16},{4,20},{8,24},{12,28},{16,0},{20,4},{24,8},{28,12},{1,17},{... | collective-permute-start | bytes 196616 | tf_op jit(solution)/shard_map/w_out_z/ppermute | solution.py:45
  247.6 16.4 %collective-permute-start.49 = (bf16[1,128,1024]{2,1,0:T(8,128)(2,1)S(1)}, bf16[1,128,1024]{2,1,0:T(8,128)(2,1)S(1)}, u32[]{:S(2)}, u32[]{:S(2)}) collective-permute-start(bf16[1,128,1024]{2,1,0:T(8,128)(2,1)S(1)} %fusion.9), channel_id=1, source_target_pairs={{0,16},{4,20},{8,24},{12,28},{16,0},{20,4},{24,8},{28,12},{1,17},{... | collective-permute-start | bytes 786440 | tf_op jit(solution)/shard_map/input_z/ppermute | solution.py:45
  251.5 13.6 %collective-permute-start.51 = (bf16[80,384]{1,0:T(8,128)(2,1)S(1)}, bf16[80,384]{1,0:T(8,128)(2,1)S(1)}, u32[]{:S(2)}, u32[]{:S(2)}) collective-permute-start(bf16[80,384]{1,0:T(8,128)(2,1)S(1)} %get-tuple-element.229), channel_id=1, source_target_pairs={{0,8},{4,12},{8,0},{12,4},{16,24},{20,28},{24,16},{28,20},{1,9},{5... | collective-permute-start | bytes 184328 | tf_op jit(solution)/shard_map/grad_qkv_z/ppermute | solution.py:45
  (88 other events, 831.5 us)
Sparse Core Ops, SparseCore 0:
  72.1 67.8 all-gather.1
  169.1 62.1 reduce-scatter.1

commit v6 on v5

--- a/solution.py
+++ b/solution.py
@@ -523,7 +523,7 @@
     count, width = tokens.shape
     rows = count // grads.shape[0]
     units = w.shape[1] // 3
-    step = min(count, 256)
+    step = min(count, 512)
     return pl.pallas_call(
         functools.partial(feed_kernel, units),
         grid=(count // step,),

time: 288 us -> 287 us (level)
  no operation moved by 1% of the time
where the time goes in v6:
time: 287 us; the launch traced here: 284 us
  waiting for transfers between devices  83 us (29%)
  starting transfers between devices  74.9 us (26%)
  Pallas kernels  51.6 us (18%)
  other arithmetic  31.7 us (11%)
  local copies, waits for them, and re-layouts  24.9 us (9%)
  between operations  15.6 us (5%)
    ppermute x20, waiting for transfers between devices, along_z(): lax.ppermute(value, 'seq', [(i, i ^ 2 * step) for i in range(self.seq_siz...  39.2 us
    ppermute x20, starting transfers between devices, along_z(): lax.ppermute(value, 'seq', [(i, i ^ 2 * step) for i in range(self.seq_siz...  32.7 us
    unnamed x129, local copies, waits for them, and re-layouts  11.8 us
    ppermute x8, waiting for transfers between devices, along_xy(): lax.ppermute(value, 'head', [(i, i ^ 2 * dy) for i in range(self.head_siz...  11.7 us
    pallas_call x1, Pallas kernels, attend_grad(): pl.pallas_call(kernel, out_shape=out_shape, in_specs=in_specs, out_specs=...  11.7 us
    ppermute x4, starting transfers between devices, along_xy(): lax.ppermute(value, ('seq', 'head'), [(s * self.head_size + h, (s ^ dx) *...  11.1 us
    all_gather x1, waiting for transfers between devices, shards(): lax.all_gather(z_block, 'seq', axis=0, tiled=True, axis_index_groups=at.c...  11 us
    ppermute x10, waiting for transfers between devices, along_x(): lax.ppermute(value, 'seq', [(i, i ^ 1) for i in range(self.seq_size)])  10.6 us
  transfers between devices with their start and end apart: 60, of which 23 were waited for; matrix products, arithmetic and copies ran while one was open for 16% of the time, Pallas kernels for 16%

profile of v6, /device:TPU:0, one launch (start us, length us, event | category | flops | bytes accessed | tf_op | source)
XLA Modules:
  0.0 284.2 jit_solution(16487295883254148422)
XLA Ops:
  13.8 4.3 %collective-permute-start.3 = (bf16[144,384]{1,0:T(8,128)(2,1)S(1)}, bf16[144,384]{1,0:T(8,128)(2,1)S(1)}, u32[]{:S(2)}, u32[]{:S(2)}) collective-permute-start(bf16[144,384]{1,0:T(8,128)(2,1)S(1)} %fusion.23), channel_id=1, source_target_pairs={{0,1},{1,0},{2,3},{3,2},{4,5},{5,4},{6,7},{7,6},{8,9},{9,8},{10,11... | collective-permute-start | bytes 331784 | tf_op jit(solution)/shard_map/qkv_core/ppermute | solution.py:51
  39.9 3.2 %collective-permute-start.1 = (bf16[1,128,1024]{2,1,0:T(8,128)(2,1)S(1)}, bf16[1,128,1024]{2,1,0:T(8,128)(2,1)S(1)}, u32[]{:S(2)}, u32[]{:S(2)}) collective-permute-start(bf16[1,128,1024]{2,1,0:T(8,128)(2,1)S(1)} %bitcast.351), channel_id=1, source_target_pairs={{0,16},{4,20},{8,24},{12,28},{16,0},{20,4},{24,8},{28,12},{1,17},{... | collective-permute-start | bytes 786440 | tf_op jit(solution)/shard_map/tokens_z/ppermute | solution.py:45
  43.1 3.1 %collective-permute-done.12 = bf16[1,128,1024]{2,1,0:T(8,128)(2,1)S(1)} collective-permute-done((bf16[1,128,1024]{2,1,0:T(8,128)(2,1)S(1)}, bf16[1,128,1024]{2,1,0:T(8,128)(2,1)S(1)}, u32[]{:S(2)}, u32[]{:S(2)}) %collective-permute-start.12) | collective-permute-done | bytes 262176 | tf_op jit(solution)/shard_map/out_xy/ppermute | solution.py:48
  47.9 5.4 %collective-permute-done.1 = bf16[1,128,1024]{2,1,0:T(8,128)(2,1)S(1)} collective-permute-done((bf16[1,128,1024]{2,1,0:T(8,128)(2,1)S(1)}, bf16[1,128,1024]{2,1,0:T(8,128)(2,1)S(1)}, u32[]{:S(2)}, u32[]{:S(2)}) %collective-permute-start.1) | collective-permute-done | bytes 262176 | tf_op jit(solution)/shard_map/tokens_z/ppermute | solution.py:45
  57.4 4.0 %collective-permute-done.7 = bf16[272,384]{1,0:T(8,128)(2,1)S(1)} collective-permute-done((bf16[272,384]{1,0:T(8,128)(2,1)}, bf16[272,384]{1,0:T(8,128)(2,1)S(1)}, u32[]{:S(2)}, u32[]{:S(2)}) %collective-permute-start.7) | collective-permute-done | bytes 208928 | tf_op jit(solution)/shard_map/qkv_xy/ppermute | solution.py:48
  63.0 3.4 %collective-permute-done.2.second_ref = bf16[2,128,1024]{2,1,0:T(8,128)(2,1)S(1)} collective-permute-done((bf16[2,128,1024]{2,1,0:T(8,128)(2,1)S(1)}, bf16[2,128,1024]{2,1,0:T(8,128)(2,1)S(1)}, u32[]{:S(2)}, u32[]{:S(2)}) %collective-permute-start.2) | collective-permute-done | bytes 524320 | tf_op jit(solution)/shard_map/tokens_z/ppermute | solution.py:45
  73.9 9.0 %shard_map.206 = (bf16[2,1024,128]{2,1,0:T(8,128)(2,1)S(1)}, bf16[2,1024,128]{2,1,0:T(8,128)(2,1)S(1)}, bf16[2,1024,128]{2,1,0:T(8,128)(2,1)S(1)}, bf16[1024,128]{1,0:T(8,128)(2,1)S(1)}) custom-call(f32[2,2]{1,0:T(2,128)S(1)} %pad_maximum_fusion.25.bias_ref, bf16[512,1024]{1,0:T(8,128)(2,1)S(1)} %bitcast.314, ...), custom_call_target="tpu_custom_call" | custom-call | flops 1048576 | bytes 1048576 | tf_op jit(solution)/shard_map/pallas_call | solution.py:306
  89.8 3.7 %collective-permute-done.18 = bf16[2,128,128]{2,1,0:T(8,128)(2,1)S(1)} collective-permute-done((bf16[2,128,128]{2,1,0:T(8,128)(2,1)S(1)}, bf16[2,128,128]{2,1,0:T(8,128)(2,1)S(1)}, u32[]{:S(2)}, u32[]{:S(2)}) %collective-permute-start.18) | collective-permute-done | bytes 65568 | tf_op jit(solution)/shard_map/attended_z/ppermute | solution.py:45
  96.2 4.6 %collective-permute-done.16 = bf16[2,128,128]{2,1,0:T(8,128)(2,1)S(1)} collective-permute-done((bf16[2,128,128]{2,1,0:T(8,128)(2,1)S(1)}, bf16[2,128,128]{2,1,0:T(8,128)(2,1)S(1)}, u32[]{:S(2)}, u32[]{:S(2)}) %collective-permute-start.16) | collective-permute-done | bytes 65568 | tf_op jit(solution)/shard_map/attended_z/ppermute | solution.py:45
  106.8 6.2 %collective-permute-start.25 = (bf16[128,1024]{1,0:T(8,128)(2,1)S(1)}, bf16[128,1024]{1,0:T(8,128)(2,1)S(1)}, u32[]{:S(2)}, u32[]{:S(2)}) collective-permute-start(bf16[128,1024]{1,0:T(8,128)(2,1)S(1)} %multiply_convert_fusion), channel_id=1, source_target_pairs={{0,6},{1,7},{2,4},{3,5},{4,2},{5,3},{6,0},{7,1},{8,14},{9,15},{10,... | collective-permute-start | bytes 786440 | tf_op jit(solution)/shard_map/normed_xy/ppermute | solution.py:60
  114.2 5.8 %collective-permute-done.25 = bf16[128,1024]{1,0:T(8,128)(2,1)S(1)} collective-permute-done((bf16[128,1024]{1,0:T(8,128)(2,1)S(1)}, bf16[128,1024]{1,0:T(8,128)(2,1)S(1)}, u32[]{:S(2)}, u32[]{:S(2)}) %collective-permute-start.25) | collective-permute-done | bytes 262176 | tf_op jit(solution)/shard_map/normed_xy/ppermute | solution.py:60
  119.9 5.3 %collective-permute-done.24 = bf16[128,1024]{1,0:T(8,128)(2,1)S(1)} collective-permute-done((bf16[128,1024]{1,0:T(8,128)(2,1)S(1)}, bf16[128,1024]{1,0:T(8,128)(2,1)S(1)}, u32[]{:S(2)}, u32[]{:S(2)}) %collective-permute-start.24) | collective-permute-done | bytes 262176 | tf_op jit(solution)/shard_map/normed_xy/ppermute | solution.py:57
  129.0 11.0 %all-gather.2.cloned.1.call-done.w_ref = bf16[1024,1536]{1,0:T(8,128)(2,1)} async-done(((bf16[256,1536]{1,0:T(8,128)(2,1)}), bf16[1024,1536]{1,0:T(8,128)(2,1)}) %all-gather.2.cloned.1.call-update) | async-done | bytes 3145744 | tf_op jit(solution)/shard_map/all_gather | solution.py:880
  143.1 4.6 %shard_map.209 = (bf16[512,512]{1,0:T(8,128)(2,1)S(1)}, bf16[512,1024]{1,0:T(8,128)(2,1)S(1)}, bf16[512,1024]{1,0:T(8,128)(2,1)S(1)}, bf16[512,1024]{1,0:T(8,128)(2,1)}) custom-call(bf16[512,1024]{1,0:T(8,128)(2,1)S(1)} %copy-done.14, bf16[4,128,1024]{2,1,0:T(8,128)(2,1)S(1)} %collective-permute-done.28.grads_ref.refs_5_, bf16[1024,1536]{1,0:T(8,128)(2,1)S(1)} %copy-done.10), custom_call_target="tpu_custom_call" | custom-call | flops 5242880000 | bytes 1024 | tf_op jit(solution)/shard_map/pallas_call | solution.py:527
  148.2 3.6 %shard_map.208 = (bf16[512,512]{1,0:T(8,128)(2,1)S(1)}, bf16[512,1024]{1,0:T(8,128)(2,1)S(1)}, bf16[512,1024]{1,0:T(8,128)(2,1)S(1)}, bf16[512,1024]{1,0:T(8,128)(2,1)S(1)}) custom-call(bf16[512,1024]{1,0:T(8,128)(2,1)S(1)} %pad_maximum_fusion.2.tokens_ref.refs_0_, bf16[4,128,1024]{2,1,0:T(8,128)(2,1)S(1)} %bitcast.319, bf16[1024,1536]{1,0:T(8,128)(2,1)S(1)} %copy-done.10), custom_call_target="tpu_custom_call" | custom-call | flops 5242880000 | bytes 1024 | tf_op jit(solution)/shard_map/pallas_call | solution.py:527
  156.6 5.6 %shard_map.210 = bf16[1024,1536]{1,0:T(8,128)(2,1)} custom-call(bf16[512,1024]{1,0:T(8,128)(2,1)S(1)} %pad_maximum_fusion.2.tokens_ref.refs_0_, bf16[4,128,1024]{2,1,0:T(8,128)(2,1)S(1)} %bitcast.320, bf16[512,512]{1,0:T(8,128)(2,1)S(1)} %get-tuple-element.114.refs_2_, bf16[512,1024]{1,0:T(8,128)(2,1)S(1)} %get-tuple-element.115.refs_3_, ...), custom_call_target="tpu_custom_call" | custom-call | flops 5242880000 | bytes 1024 | tf_op jit(solution)/shard_map/pallas_call | solution.py:579
  162.6 6.0 %collective-permute-done.33.refs_2_ = bf16[128,1024]{1,0:T(8,128)(2,1)} collective-permute-done((bf16[128,1024]{1,0:T(8,128)(2,1)}, bf16[128,1024]{1,0:T(8,128)(2,1)}, u32[]{:S(2)}, u32[]{:S(2)}) %collective-permute-start.33) | collective-permute-done | bytes 262176 | tf_op jit(solution)/shard_map/up_xy/ppermute | solution.py:57
  172.1 4.1 %shard_map.211 = (f32[128,1024]{1,0:T(8,128)}, bf16[128,1024]{1,0:T(8,128)(2,1)}, bf16[128,1024]{1,0:T(8,128)(2,1)}, f32[1,1024]{1,0:T(1,128)}) custom-call(f32[128,1024]{1,0:T(8,128)} %copy-done.21, bf16[128,1024]{1,0:T(8,128)(2,1)} %bitcast.339, f32[1,1024]{1,0:T(1,128)} %reshape.654.gain_ref, bf16[1024,1024]{1,0:T(8,128)(2,1)} %bitcast.309, ...), custom_call_target="tpu_custom_call" | custom-call | flops 1048576 | bytes 1024 | tf_op jit(solution)/shard_map/pallas_call | solution.py:495
  180.5 3.5 %collective-permute-start.36 = (bf16[128,512]{1,0:T(8,128)(2,1)S(1)}, bf16[128,512]{1,0:T(8,128)(2,1)S(1)}, u32[]{:S(2)}, u32[]{:S(2)}) collective-permute-start(bf16[128,512]{1,0:T(8,128)(2,1)S(1)} %slice.458), channel_id=1, source_target_pairs={{0,1},{1,0},{2,3},{3,2},{4,5},{5,4},{6,7},{7,6},{8,9},{9,8},{10,11... | collective-permute-start | bytes 393224 | tf_op jit(solution)/shard_map/merged_core/ppermute | solution.py:51
  190.7 4.1 %collective-permute-start.37 = (bf16[2,128,128]{2,1,0:T(8,128)(2,1)S(1)}, bf16[2,128,128]{2,1,0:T(8,128)(2,1)S(1)}, u32[]{:S(2)}, u32[]{:S(2)}) collective-permute-start(bf16[2,128,128]{2,1,0:T(8,128)(2,1)S(1)} %pad_maximum_fusion.16), channel_id=1, source_target_pairs={{0,16},{4,20},{8,24},{12,28},{16,0},{20,4},{24,8},{28,12},{1,17},{... | collective-permute-start | bytes 196616 | tf_op jit(solution)/shard_map/merged_z/ppermute | solution.py:45
  195.0 7.2 %collective-permute-done.38 = bf16[2,128,128]{2,1,0:T(8,128)(2,1)S(1)} collective-permute-done((bf16[2,128,128]{2,1,0:T(8,128)(2,1)S(1)}, bf16[2,128,128]{2,1,0:T(8,128)(2,1)S(1)}, u32[]{:S(2)}, u32[]{:S(2)}) %collective-permute-start.38) | collective-permute-done | bytes 65568 | tf_op jit(solution)/shard_map/merged_z/ppermute | solution.py:45
  203.9 11.7 %shard_map.213 = (bf16[512,1024]{1,0:T(8,128)(2,1)}, bf16[512,1024]{1,0:T(8,128)(2,1)}, bf16[1024,384]{1,0:T(8,128)(2,1)}, f32[2,2]{1,0:T(2,128)}, bf16[4,272,384]{2,1,0:T(8,128)(2,1)S(1)}) custom-call(s32[1]{0:T(128)} %bitcast.97.refs_0_, bf16[512,1024]{1,0:T(8,128)(2,1)} %bitcast.313, bf16[512,1024]{1,0:T(8,128)(2,1)} %collective-permute-done.15.far_ref.refs_2_, ...), custom_call_target="tpu_custom_call" | custom-call | flops 4194304000 | bytes 1024 | tf_op jit(solution)/shard_map/pallas_call | solution.py:467
  241.8 4.3 %collective-permute-done.44 = bf16[2,128,1024]{2,1,0:T(8,128)(2,1)} collective-permute-done((bf16[2,128,1024]{2,1,0:T(8,128)(2,1)}, bf16[2,128,1024]{2,1,0:T(8,128)(2,1)}, u32[]{:S(2)}, u32[]{:S(2)}) %collective-permute-start.44) | collective-permute-done | bytes 524320 | tf_op jit(solution)/shard_map/input_z/ppermute | solution.py:45
  257.9 5.6 %collective-permute-done.49 = bf16[1,128,1024]{2,1,0:T(8,128)(2,1)S(1)} collective-permute-done((bf16[1,128,1024]{2,1,0:T(8,128)(2,1)S(1)}, bf16[1,128,1024]{2,1,0:T(8,128)(2,1)S(1)}, u32[]{:S(2)}, u32[]{:S(2)}) %collective-permute-start.49) | collective-permute-done | bytes 262176 | tf_op jit(solution)/shard_map/input_z/ppermute | solution.py:45
  (393 shorter events, 139.5 us)
Async XLA Ops:
  7.2 132.8 %all-gather.2.cloned.1.call-start = ((), (), s32[]{:S(2)}) async-start(), calls=%async_computation.1 | async-start | bytes 3932160 | tf_op jit(solution)/shard_map/all_gather | solution.py:880
  9.5 30.4 %collective-permute-start = (bf16[128,1024]{1,0:T(8,128)(2,1)S(1)}, bf16[128,1024]{1,0:T(8,128)(2,1)S(1)}, u32[]{:S(2)}, u32[]{:S(2)}) collective-permute-start(bf16[128,1024]{1,0:T(8,128)(2,1)S(1)} %fusion.3), channel_id=1, source_target_pairs={{0,0},{1,4},{2,2},{3,6},{4,1},{5,5},{6,3},{7,7},{8,8},{9,12},{10,1... | collective-permute-start | bytes 786440 | tf_op jit(solution)/shard_map/tokens_turn/ppermute | solution.py:71
  20.8 32.7 %collective-permute-start.14 = (bf16[1,128,1024]{2,1,0:T(8,128)(2,1)S(1)}, bf16[1,128,1024]{2,1,0:T(8,128)(2,1)}, u32[]{:S(2)}, u32[]{:S(2)}) collective-permute-start(bf16[1,128,1024]{2,1,0:T(8,128)(2,1)S(1)} %copy-done.31), channel_id=1, source_target_pairs={{0,4},{4,0},{8,12},{12,8},{16,20},{20,16},{24,28},{28,24},{1,5},{5... | collective-permute-start | bytes 786440 | tf_op jit(solution)/shard_map/cotangent_x/ppermute | solution.py:48
  31.2 25.3 %collective-permute-start.9 = (bf16[272,384]{1,0:T(8,128)(2,1)}, bf16[272,384]{1,0:T(8,128)(2,1)S(1)}, u32[]{:S(2)}, u32[]{:S(2)}) collective-permute-start(bf16[272,384]{1,0:T(8,128)(2,1)} %get-tuple-element.232), channel_id=1, source_target_pairs={{0,6},{1,7},{2,4},{3,5},{4,2},{5,3},{6,0},{7,1},{8,14},{9,15},{10,... | collective-permute-start | bytes 626696 | tf_op jit(solution)/shard_map/qkv_xy/ppermute | solution.py:60
  33.9 23.5 %collective-permute-start.8 = (bf16[272,384]{1,0:T(8,128)(2,1)}, bf16[272,384]{1,0:T(8,128)(2,1)S(1)}, u32[]{:S(2)}, u32[]{:S(2)}) collective-permute-start(bf16[272,384]{1,0:T(8,128)(2,1)} %get-tuple-element.232), channel_id=1, source_target_pairs={{0,2},{1,3},{2,0},{3,1},{4,6},{5,7},{6,4},{7,5},{8,10},{9,11},{10,... | collective-permute-start | bytes 626696 | tf_op jit(solution)/shard_map/qkv_xy/ppermute | solution.py:57
  39.9 13.4 %collective-permute-start.1 = (bf16[1,128,1024]{2,1,0:T(8,128)(2,1)S(1)}, bf16[1,128,1024]{2,1,0:T(8,128)(2,1)S(1)}, u32[]{:S(2)}, u32[]{:S(2)}) collective-permute-start(bf16[1,128,1024]{2,1,0:T(8,128)(2,1)S(1)} %bitcast.351), channel_id=1, source_target_pairs={{0,16},{4,20},{8,24},{12,28},{16,0},{20,4},{24,8},{28,12},{1,17},{... | collective-permute-start | bytes 786440 | tf_op jit(solution)/shard_map/tokens_z/ppermute | solution.py:45
  46.3 15.5 %collective-permute-start.13 = (bf16[2,128,1024]{2,1,0:T(8,128)(2,1)S(1)}, bf16[2,128,1024]{2,1,0:T(8,128)(2,1)S(1)}, u32[]{:S(2)}, u32[]{:S(2)}) collective-permute-start(bf16[2,128,1024]{2,1,0:T(8,128)(2,1)S(1)} %pad_maximum_fusion.7), channel_id=1, source_target_pairs={{0,2},{1,3},{2,0},{3,1},{4,6},{5,7},{6,4},{7,5},{8,10},{9,11},{10,... | collective-permute-start | bytes 1572872 | tf_op jit(solution)/shard_map/out_xy/ppermute | solution.py:57
  72.0 159.5 %reduce-scatter.2.cloned.1.call-start = ((), (), s32[]{:S(2)}) async-start(), calls=%async_computation.2 | async-start | bytes 3932160 | tf_op jit(solution)/shard_map/reduce_scatter | solution.py:963
  72.0 28.8 %collective-permute-start.19 = (bf16[1,2,128,1024]{3,2,1,0:T(8,128)(2,1)}, bf16[1,2,128,1024]{3,2,1,0:T(8,128)(2,1)S(1)}, u32[]{:S(2)}, u32[]{:S(2)}) collective-permute-start(bf16[1,2,128,1024]{3,2,1,0:T(8,128)(2,1)} %bitcast.336), channel_id=1, source_target_pairs={{0,2},{1,3},{2,0},{3,1},{4,6},{5,7},{6,4},{7,5},{8,10},{9,11},{10,... | collective-permute-start | bytes 1572872 | tf_op jit(solution)/shard_map/cotangent_y/ppermute | solution.py:57
  73.6 29.8 %collective-permute-start.22 = (bf16[4,128,1024]{2,1,0:T(8,128)(2,1)}, bf16[4,128,1024]{2,1,0:T(8,128)(2,1)}, u32[]{:S(2)}, u32[]{:S(2)}) collective-permute-start(bf16[4,128,1024]{2,1,0:T(8,128)(2,1)} %pad_maximum_fusion.1), channel_id=1, source_target_pairs={{0,1},{1,0},{2,3},{3,2},{4,5},{5,4},{6,7},{7,6},{8,9},{9,8},{10,11... | collective-permute-start | bytes 3145736 | tf_op jit(solution)/shard_map/out_core/ppermute | solution.py:51
  87.0 13.8 %collective-permute-start.16 = (bf16[2,128,128]{2,1,0:T(8,128)(2,1)S(1)}, bf16[2,128,128]{2,1,0:T(8,128)(2,1)S(1)}, u32[]{:S(2)}, u32[]{:S(2)}) collective-permute-start(bf16[2,128,128]{2,1,0:T(8,128)(2,1)S(1)} %get-tuple-element.226), channel_id=1, source_target_pairs={{0,16},{4,20},{8,24},{12,28},{16,0},{20,4},{24,8},{28,12},{1,17},{... | collective-permute-start | bytes 196616 | tf_op jit(solution)/shard_map/attended_z/ppermute | solution.py:45
  147.7 21.6 %collective-permute-start.29 = (bf16[512,1024]{1,0:T(8,128)(2,1)}, bf16[512,1024]{1,0:T(8,128)(2,1)}, u32[]{:S(2)}, u32[]{:S(2)}) collective-permute-start(bf16[512,1024]{1,0:T(8,128)(2,1)} %get-tuple-element.109), channel_id=1, source_target_pairs={{0,1},{1,0},{2,3},{3,2},{4,5},{5,4},{6,7},{7,6},{8,9},{9,8},{10,11... | collective-permute-start | bytes 3145736 | tf_op jit(solution)/shard_map/down_core/ppermute | solution.py:51
  154.6 14.0 %collective-permute-start.33 = (bf16[128,1024]{1,0:T(8,128)(2,1)}, bf16[128,1024]{1,0:T(8,128)(2,1)}, u32[]{:S(2)}, u32[]{:S(2)}) collective-permute-start(bf16[128,1024]{1,0:T(8,128)(2,1)} %get-tuple-element.203), channel_id=1, source_target_pairs={{0,2},{1,3},{2,0},{3,1},{4,6},{5,7},{6,4},{7,5},{8,10},{9,11},{10,... | collective-permute-start | bytes 786440 | tf_op jit(solution)/shard_map/up_xy/ppermute | solution.py:57
  170.6 16.7 %collective-permute-start.31 = (bf16[1,2,128,1024]{3,2,1,0:T(8,128)(2,1)S(1)}, bf16[1,2,128,1024]{3,2,1,0:T(8,128)(2,1)S(1)}, u32[]{:S(2)}, u32[]{:S(2)}) collective-permute-start(bf16[1,2,128,1024]{3,2,1,0:T(8,128)(2,1)S(1)} %bitcast.350), channel_id=1, source_target_pairs={{0,2},{1,3},{2,0},{3,1},{4,6},{5,7},{6,4},{7,5},{8,10},{9,11},{10,... | collective-permute-start | bytes 1572872 | tf_op jit(solution)/shard_map/down_y/ppermute | solution.py:57
  188.5 14.6 %collective-permute-start.41 = (bf16[128,1024]{1,0:T(8,128)(2,1)S(1)}, bf16[128,1024]{1,0:T(8,128)(2,1)S(1)}, u32[]{:S(2)}, u32[]{:S(2)}) collective-permute-start(bf16[128,1024]{1,0:T(8,128)(2,1)S(1)} %fusion.5), channel_id=1, source_target_pairs={{0,4},{4,0},{8,12},{12,8},{16,20},{20,16},{24,28},{28,24},{1,5},{5... | collective-permute-start | bytes 786440 | tf_op jit(solution)/shard_map/down_x/ppermute | solution.py:48
  202.2 13.8 %collective-permute-start.42 = (bf16[1,2,128,1024]{3,2,1,0:T(8,128)(2,1)S(1)}, bf16[1,2,128,1024]{3,2,1,0:T(8,128)(2,1)S(1)}, u32[]{:S(2)}, u32[]{:S(2)}) collective-permute-start(bf16[1,2,128,1024]{3,2,1,0:T(8,128)(2,1)S(1)} %fusion), channel_id=1, source_target_pairs={{0,2},{1,3},{2,0},{3,1},{4,6},{5,7},{6,4},{7,5},{8,10},{9,11},{10,... | collective-permute-start | bytes 1572872 | tf_op jit(solution)/shard_map/w_out_y/ppermute | solution.py:57
  216.0 13.3 %collective-permute-start.43 = (bf16[512,1024]{1,0:T(8,128)(2,1)}, bf16[512,1024]{1,0:T(8,128)(2,1)}, u32[]{:S(2)}, u32[]{:S(2)}) collective-permute-start(bf16[512,1024]{1,0:T(8,128)(2,1)} %get-tuple-element.138), channel_id=1, source_target_pairs={{0,1},{1,0},{2,3},{3,2},{4,5},{5,4},{6,7},{7,6},{8,9},{9,8},{10,11... | collective-permute-start | bytes 3145736 | tf_op jit(solution)/shard_map/input_core/ppermute | solution.py:51
  219.1 14.3 %collective-permute-start.46 = (bf16[272,384]{1,0:T(8,128)(2,1)}, bf16[272,384]{1,0:T(8,128)(2,1)}, u32[]{:S(2)}, u32[]{:S(2)}) collective-permute-start(bf16[272,384]{1,0:T(8,128)(2,1)} %get-tuple-element.212), channel_id=1, source_target_pairs={{0,4},{4,0},{8,12},{12,8},{16,20},{20,16},{24,28},{28,24},{1,5},{5... | collective-permute-start | bytes 626696 | tf_op jit(solution)/shard_map/grad_qkv_xy/ppermute | solution.py:48
  220.0 16.2 %collective-permute-start.47 = (bf16[272,384]{1,0:T(8,128)(2,1)}, bf16[272,384]{1,0:T(8,128)(2,1)}, u32[]{:S(2)}, u32[]{:S(2)}) collective-permute-start(bf16[272,384]{1,0:T(8,128)(2,1)} %get-tuple-element.211), channel_id=1, source_target_pairs={{0,2},{1,3},{2,0},{3,1},{4,6},{5,7},{6,4},{7,5},{8,10},{9,11},{10,... | collective-permute-start | bytes 626696 | tf_op jit(solution)/shard_map/grad_qkv_xy/ppermute | solution.py:57
  220.9 15.3 %collective-permute-start.48 = (bf16[272,384]{1,0:T(8,128)(2,1)}, bf16[272,384]{1,0:T(8,128)(2,1)}, u32[]{:S(2)}, u32[]{:S(2)}) collective-permute-start(bf16[272,384]{1,0:T(8,128)(2,1)} %get-tuple-element.210), channel_id=1, source_target_pairs={{0,6},{1,7},{2,4},{3,5},{4,2},{5,3},{6,0},{7,1},{8,14},{9,15},{10,... | collective-permute-start | bytes 626696 | tf_op jit(solution)/shard_map/grad_qkv_xy/ppermute | solution.py:60
  231.5 14.6 %collective-permute-start.44 = (bf16[2,128,1024]{2,1,0:T(8,128)(2,1)}, bf16[2,128,1024]{2,1,0:T(8,128)(2,1)}, u32[]{:S(2)}, u32[]{:S(2)}) collective-permute-start(bf16[2,128,1024]{2,1,0:T(8,128)(2,1)} %bitcast.103), channel_id=1, source_target_pairs={{0,8},{4,12},{8,0},{12,4},{16,24},{20,28},{24,16},{28,20},{1,9},{5... | collective-permute-start | bytes 1572872 | tf_op jit(solution)/shard_map/input_z/ppermute | solution.py:45
  239.3 27.7 %collective-permute-start.57 = (bf16[1,32,1024]{2,1,0:T(8,128)(2,1)S(1)}, bf16[1,32,1024]{2,1,0:T(8,128)(2,1)S(1)}, u32[]{:S(2)}, u32[]{:S(2)}) collective-permute-start(bf16[1,32,1024]{2,1,0:T(8,128)(2,1)S(1)} %fusion.18), channel_id=1, source_target_pairs={{0,16},{4,20},{8,24},{12,28},{16,0},{20,4},{24,8},{28,12},{1,17},{... | collective-permute-start | bytes 196616 | tf_op jit(solution)/shard_map/w_out_z/ppermute | solution.py:45
  247.3 16.2 %collective-permute-start.49 = (bf16[1,128,1024]{2,1,0:T(8,128)(2,1)S(1)}, bf16[1,128,1024]{2,1,0:T(8,128)(2,1)S(1)}, u32[]{:S(2)}, u32[]{:S(2)}) collective-permute-start(bf16[1,128,1024]{2,1,0:T(8,128)(2,1)S(1)} %fusion.9), channel_id=1, source_target_pairs={{0,16},{4,20},{8,24},{12,28},{16,0},{20,4},{24,8},{28,12},{1,17},{... | collective-permute-start | bytes 786440 | tf_op jit(solution)/shard_map/input_z/ppermute | solution.py:45
  251.0 13.6 %collective-permute-start.51 = (bf16[80,384]{1,0:T(8,128)(2,1)S(1)}, bf16[80,384]{1,0:T(8,128)(2,1)S(1)}, u32[]{:S(2)}, u32[]{:S(2)}) collective-permute-start(bf16[80,384]{1,0:T(8,128)(2,1)S(1)} %get-tuple-element.229), channel_id=1, source_target_pairs={{0,8},{4,12},{8,0},{12,4},{16,24},{20,28},{24,16},{28,20},{1,9},{5... | collective-permute-start | bytes 184328 | tf_op jit(solution)/shard_map/grad_qkv_z/ppermute | solution.py:45
  (88 other events, 831.3 us)
Sparse Core Ops, SparseCore 0:
  72.1 67.8 all-gather.1
  168.7 62.0 reduce-scatter.1
